TPU v7x, 32 devices: a whole 2x2x4 slice. The times are simulated.
32 devices in a mesh: groups: 2 (over y), layer: 4 (over x, core), tok: 4 (over z).
Axes of the slice: x: 2, y: 2, z: 4, core: 2. Of those that a mesh axis runs over, the one named last changes fastest.
Arguments:
- keys: bfloat16 [4, 8192, 1024], P('layer', ('groups', 'tok')), parts along dimension 1, may hold values from -6 to 6
Outputs:
- gram_tiles: float32 [4, 3, 2048, 1024], P('layer', None, ('groups', 'tok')), parts along dimension 2
There are 2 independent parts, one for each index of `groups`. A program takes and returns all parts, laid end to end along the dimension named above; each array names one. Nothing has to cross between parts.
All inputs are finite; a program needn't handle non-finite values.
Results may differ from a plain program's by a relative error of at most 0.0003.
Values may be sent and summed in bfloat16 or wider, within the bound.
No kernel may reach another device: no remote copies, remote signals or barrier semaphores. Data moves between devices by JAX's collectives and lax.ppermute only.
A program may use at most 64 MiB of HBM per device.

v0:
```python
import jax
import jax.numpy as jnp
from jax import lax
from jax.sharding import PartitionSpec as P


def shifted(value, axis, steps):
    count = lax.axis_size(axis)
    pairs = [(source, (source + steps) % count) for source in range(count)]
    return lax.ppermute(value, axis, pairs)


def tile_rows(inverse, left_keys, right_keys):
    product = lax.dot_general(
        left_keys, right_keys, (((0,), (0,)), ((), ())), preferred_element_type=jnp.float32
    )
    return product * inverse


def per_device(keys):
    own_keys = keys[0]
    layers = lax.axis_size("layer")
    half_span = layers // 2
    inverse = 1.0 / (own_keys.shape[0] * lax.axis_size("tok"))
    forward_list = [own_keys]
    forward_key = own_keys
    for repeat in range(half_span):
        forward_key = shifted(forward_key, "layer", -1)
        forward_list.append(forward_key)
    tile_pairs = [(own_keys, forward_list[dist]) for dist in range(half_span + 1)]
    shares = []
    for left_keys, right_keys in tile_pairs:
        shares.append(
            lax.psum_scatter(
                tile_rows(inverse, left_keys, right_keys), "tok", scatter_dimension=0, tiled=True
            )
        )
    stacked = jnp.stack(shares)
    return stacked[None]


def solution(mesh):
    in_specs = (P("layer", ("groups", "tok"), None),)
    out_specs = P("layer", None, ("groups", "tok"), None)
    return jax.shard_map(
        per_device, mesh=mesh, in_specs=in_specs, out_specs=out_specs, check_vma=False
    )
```

profile of v0, /device:TPU:0, one launch (start us, length us, event | category | flops | bytes accessed | tf_op | source)
XLA Modules:
  0.0 262.5 jit_solution(2271327131079944801)
XLA Ops:
  6.5 0.0 reduce-scatter.4.cloned.1.call-start
  6.5 6.6 %convolution_multiply_fusion.2 = f32[1024,1024]{1,0:T(8,128)} fusion(bf16[1,1024,1024]{2,1,0:T(8,128)(2,1)} %param.1), kind=kOutput, calls=%fused_computation.3 | convolution fusion | flops 2148532224 | bytes 6291456 | tf_op jit(solution)/shard_map/dot_general | solution.py:14
  13.1 0.0 copy-start
  13.1 0.0 reduce-scatter.4.cloned.1.call-update
  13.2 0.0 reduce-scatter.6.cloned.1.call-start
  13.2 1.5 copy-done
  14.7 2.4 collective-permute-start
  17.1 23.6 %collective-permute-done = bf16[1024,1024]{1,0:T(8,128)(2,1)S(1)} collective-permute-done((bf16[1024,1024]{1,0:T(8,128)(2,1)S(1)}, bf16[1024,1024]{1,0:T(8,128)(2,1)S(1)}, u32[]{:S(2)}, u32[]{:S(2)}) %collective-permute-start) | collective-permute-done | bytes 2097184 | tf_op jit(solution)/shard_map/ppermute | solution.py:10
  40.7 0.0 copy-start.1
  40.7 1.3 copy-done.1
  42.0 4.4 %convolution_multiply_fusion.1 = f32[1024,1024]{1,0:T(8,128)} fusion(bf16[1024,1024]{1,0:T(8,128)(2,1)S(1)} %collective-permute-done, bf16[1,1024,1024]{2,1,0:T(8,128)(2,1)S(1)} %copy-done), kind=kOutput, calls=%fused_computation.2 | convolution fusion | flops 2148532224 | bytes 8388608 | tf_op jit(solution)/shard_map/dot_general | solution.py:14
  46.4 0.0 reduce-scatter.6.cloned.1.call-update
  46.4 0.0 reduce-scatter.8.cloned.1.call-start
  46.4 2.4 collective-permute-start.1
  48.8 23.9 %collective-permute-done.1 = bf16[1024,1024]{1,0:T(8,128)(2,1)S(1)} collective-permute-done((bf16[1024,1024]{1,0:T(8,128)(2,1)}, bf16[1024,1024]{1,0:T(8,128)(2,1)S(1)}, u32[]{:S(2)}, u32[]{:S(2)}) %collective-permute-start.1) | collective-permute-done | bytes 2097184 | tf_op jit(solution)/shard_map/ppermute | solution.py:10
  72.7 4.4 %convolution_multiply_fusion = f32[1024,1024]{1,0:T(8,128)} fusion(bf16[1024,1024]{1,0:T(8,128)(2,1)S(1)} %collective-permute-done.1, bf16[1,1024,1024]{2,1,0:T(8,128)(2,1)S(1)} %copy-done), kind=kOutput, calls=%fused_computation.1 | convolution fusion | flops 2148532224 | bytes 8388608 | tf_op jit(solution)/shard_map/dot_general | solution.py:14
  77.0 0.0 reduce-scatter.8.cloned.1.call-update
  77.1 15.7 %reduce-scatter.4.cloned.1.call-done = f32[256,1024]{1,0:T(8,128)} async-done(((f32[1024,1024]{1,0:T(8,128)}), f32[256,1024]{1,0:T(8,128)}) %reduce-scatter.4.cloned.1.call-update) | async-done | bytes 1048592 | tf_op jit(solution)/shard_map/reduce_scatter | solution.py:34
  92.8 79.7 %reduce-scatter.6.cloned.1.call-done = f32[256,1024]{1,0:T(8,128)} async-done(((f32[1024,1024]{1,0:T(8,128)}), f32[256,1024]{1,0:T(8,128)}) %reduce-scatter.6.cloned.1.call-update) | async-done | bytes 1048592 | tf_op jit(solution)/shard_map/reduce_scatter | solution.py:34
  172.5 79.6 %reduce-scatter.8.cloned.1.call-done = f32[256,1024]{1,0:T(8,128)} async-done(((f32[1024,1024]{1,0:T(8,128)}), f32[256,1024]{1,0:T(8,128)}) %reduce-scatter.8.cloned.1.call-update) | async-done | bytes 1048592 | tf_op jit(solution)/shard_map/reduce_scatter | solution.py:34
  252.1 3.9 %maximum_bitcast_fusion = f32[1,3,256,1024]{3,2,1,0:T(8,128)} fusion(f32[1,256,1024]{2,1,0:T(8,128)} %bitcast.16, f32[1,256,1024]{2,1,0:T(8,128)} %bitcast.15, f32[1,256,1024]{2,1,0:T(8,128)} %bitcast.14), kind=kLoop, calls=%fused_computation | loop fusion | flops 1572864 | bytes 6291456 | tf_op jit(solution)/shard_map/broadcast_in_dim | solution.py:39
Async XLA Ops:
  6.5 86.2 %reduce-scatter.4.cloned.1.call-start = ((), (), s32[]{:S(2)}) async-start(), calls=%async_computation.3 | async-start | bytes 5242880 | tf_op jit(solution)/shard_map/reduce_scatter | solution.py:34
  13.1 1.6 copy-start
  13.2 159.3 %reduce-scatter.6.cloned.1.call-start = ((), (), s32[]{:S(2)}) async-start(), calls=%async_computation.4 | async-start | bytes 5242880 | tf_op jit(solution)/shard_map/reduce_scatter | solution.py:34
  14.7 25.9 %collective-permute-start = (bf16[1024,1024]{1,0:T(8,128)(2,1)S(1)}, bf16[1024,1024]{1,0:T(8,128)(2,1)S(1)}, u32[]{:S(2)}, u32[]{:S(2)}) collective-permute-start(bf16[1024,1024]{1,0:T(8,128)(2,1)S(1)} %bitcast.17), channel_id=1, source_target_pairs={{0,12},{4,0},{8,4},{12,8},{1,13},{5,1},{9,5},{13,9},{2,14},{6,2},{... | collective-permute-start | bytes 6291464 | tf_op jit(solution)/shard_map/ppermute | solution.py:10
  40.7 1.3 copy-start.1
  46.4 205.7 %reduce-scatter.8.cloned.1.call-start = ((), (), s32[]{:S(2)}) async-start(), calls=%async_computation.5 | async-start | bytes 5242880 | tf_op jit(solution)/shard_map/reduce_scatter | solution.py:34
  46.4 26.2 %collective-permute-start.1 = (bf16[1024,1024]{1,0:T(8,128)(2,1)}, bf16[1024,1024]{1,0:T(8,128)(2,1)S(1)}, u32[]{:S(2)}, u32[]{:S(2)}) collective-permute-start(bf16[1024,1024]{1,0:T(8,128)(2,1)} %copy-done.1), channel_id=1, source_target_pairs={{0,12},{4,0},{8,4},{12,8},{1,13},{5,1},{9,5},{13,9},{2,14},{6,2},{... | collective-permute-start | bytes 6291464 | tf_op jit(solution)/shard_map/ppermute | solution.py:10
Sparse Core Ops, SparseCore 0:
  13.3 79.4 reduce-scatter.3
  95.2 77.2 reduce-scatter.5
  174.8 77.2 reduce-scatter.7
where the time goes:
time: 263 us
  waiting for transfers between devices  222 us (84%)
  matrix products  15.4 us (6%)
  between operations  13.1 us (5%)
  starting transfers between devices  4.82 us (2%)
  other arithmetic  3.93 us (1%)
  local copies, waits for them, and re-layouts  2.84 us (1%)
    reduce_scatter x3, waiting for transfers between devices, per_device(): lax.psum_scatter(tile_rows(inverse, left_keys, right_keys), 'tok', scatte...  175 us
    ppermute x2, waiting for transfers between devices, shifted(): return lax.ppermute(value, axis, pairs)  47.4 us
    dot_general x3, matrix products, tile_rows(): lax.dot_general(left_keys, right_keys, (((0,), (0,)), ((), ())), preferre...  15.4 us
  transfers between devices with their start and end apart: 5, of which 5 were waited for; matrix products, arithmetic and copies ran while one was open for 3% of the time, Pallas kernels for 0%

commit v1 on v0

v1 whole, which is shorter than its diff:
```python
import functools

import jax
import jax.numpy as jnp
from jax import lax
from jax.experimental import pallas as pl
from jax.experimental.pallas import tpu as pltpu
from jax.sharding import PartitionSpec as P

OUTER_TO_INNER = [(0, 1), (3, 2)]
ACROSS_MIDDLE = [(1, 2), (2, 1)]
INNER_TO_OUTER = [(1, 0), (2, 3)]
FAR, NEXT, NEAR = 3, 2, 1

HALF = 128
TAIL = 16
SPREAD = 13777.0
SMALLEST = 1e-30
COST = 10_000_000_000
VMEM_BYTES = 24 * 1024 * 1024


def shifted(value, axis, steps):
    count = lax.axis_size(axis)
    pairs = [(source, (source + steps) % count) for source in range(count)]
    return lax.ppermute(value, axis, pairs)


def tile_rows(inverse, left_keys, right_keys):
    product = lax.dot_general(
        left_keys, right_keys, (((0,), (0,)), ((), ())), preferred_element_type=jnp.float32
    )
    return product * inverse


def reduce_scattered(own_keys, forward_list, inverse):
    shares = [
        lax.psum_scatter(
            tile_rows(inverse, own_keys, right_keys), "tok", scatter_dimension=0, tiled=True
        )
        for right_keys in forward_list
    ]
    return jnp.stack(shares)[None]


def fold():
    place = lax.axis_index("tok")
    upper = place >= 2
    inner = jnp.logical_or(place == 1, place == 2)
    return upper, inner


def block_at(upper, index):
    return jnp.where(upper, 3 - index, index)


def product(inverse, left_ref, right_ref, upper, row, column, rows):
    left = left_ref[:, pl.ds(pl.multiple_of(block_at(upper, row) * rows, rows), rows)]
    if column is None:
        return tile_rows(inverse, left, right_ref[...])
    at = pl.ds(pl.multiple_of(block_at(upper, column) * rows, rows), rows)
    return tile_rows(inverse, left, right_ref[:, at])


def row_factor(rows):
    index = lax.broadcasted_iota(jnp.int32, (rows, HALF), 0).astype(jnp.float32) * 0.6180339887
    return 1.0 + (index - jnp.floor(index))


def column_factor(half):
    index = lax.broadcasted_iota(jnp.int32, (1, HALF), 1).astype(jnp.float32) + float(half * HALF)
    index = index * 0.7548776662
    return 1.0 + (index - jnp.floor(index))


def peak_of(value):
    return jnp.max(jnp.max(jnp.abs(value), axis=0, keepdims=True), axis=1, keepdims=True)


def write_message(message_ref, blocks):
    rows = blocks[0].shape[0]
    peak = functools.reduce(jnp.maximum, [peak_of(block) for block in blocks])
    peak = (jnp.maximum(peak, SMALLEST) * 1.02).astype(jnp.bfloat16).astype(jnp.float32)
    peak = jnp.broadcast_to(peak, (1, HALF))
    factor = row_factor(rows)
    for number, block in enumerate(blocks):
        for half in range(rows // HALF):
            scaled = block[:, half * HALF : (half + 1) * HALF] * factor
            scaled = scaled * (column_factor(half) * (SPREAD / peak))
            power = scaled * scaled
            power = power * power
            power = power * power
            coded = jnp.where(scaled < 0.0, -power, power)
            start = (number * (rows // HALF) + half) * rows
            message_ref[start : start + rows, :] = coded.astype(jnp.bfloat16)
    start = len(blocks) * (rows // HALF) * rows
    message_ref[start : start + TAIL, :] = jnp.broadcast_to(peak, (TAIL, HALF)).astype(jnp.bfloat16)


def read_block(message_ref, number, rows):
    peak = message_ref[message_ref.shape[0] - TAIL :, :].astype(jnp.float32)[0:1]
    factor = 1.0 / row_factor(rows)
    halves = []
    for half in range(rows // HALF):
        start = (number * (rows // HALF) + half) * rows
        coded = message_ref[start : start + rows, :].astype(jnp.float32)
        root = lax.rsqrt(lax.rsqrt(jnp.maximum(jnp.abs(coded), 1.2e-38)))
        root = root * lax.rsqrt(root)
        root = jnp.where(coded < 0.0, -root, root)
        halves.append(root * factor * (peak * (1.0 / SPREAD) / column_factor(half)))
    return jnp.concatenate(halves, axis=1)


def message_shape(count, rows):
    return jax.ShapeDtypeStruct((count * rows * rows // HALF + TAIL, HALF), jnp.bfloat16)


def columns_of(value, upper_value, rows, index):
    return jnp.where(
        upper_value,
        value[:, (3 - index) * rows : (4 - index) * rows],
        value[:, index * rows : (index + 1) * rows],
    )


def send_kernel(parts, inverse, left_ref, *refs):
    *right_refs, message_ref = refs
    rows = left_ref.shape[1] // 4
    upper, inner = fold()

    @pl.when(jnp.logical_not(inner))
    def _():
        write_message(
            message_ref,
            [
                product(inverse, left_ref, right_refs[which], upper, row, column, rows)
                for which, row, count in parts
                for column in range(count)
            ],
        )


def pass_on_kernel(parts, inverse, left_ref, right_ref, message_ref, copy_ref):
    copy_ref[...] = right_ref[...]
    send_kernel(parts, inverse, left_ref, right_ref, message_ref)


def copy_block(turned_ref, message_ref, number, rows):
    size = rows * rows // HALF
    turned_ref[0:size, :] = message_ref[number * size : (number + 1) * size, :]
    turned_ref[size : size + TAIL, :] = message_ref[message_ref.shape[0] - TAIL :, :]


def cross_kernel(row, count, inverse, left_ref, right_ref, in_ref, message_ref, *turned_refs):
    rows = left_ref.shape[1] // 4
    upper, inner = fold()

    @pl.when(inner)
    def _():
        write_message(
            message_ref,
            [
                product(inverse, left_ref, right_ref, upper, row, column, rows)
                + read_block(in_ref, column, rows)
                for column in range(count)
            ],
        )
        for turned_ref in turned_refs:
            copy_block(turned_ref, in_ref, 1, rows)


def back_kernel(inverse, left_ref, right_ref, across_ref, message_ref, *turned_refs):
    rows = left_ref.shape[1] // 4
    upper, inner = fold()

    @pl.when(inner)
    def _():
        write_message(
            message_ref,
            [
                product(inverse, left_ref, right_ref, upper, 0, column, rows)
                + read_block(across_ref, 3 - column, rows)
                for column in range(4)
            ],
        )
        for turned_ref in turned_refs:
            copy_block(turned_ref, across_ref, 2, rows)


def put(out_ref, upper, column, rows, value):
    at = pl.ds(pl.multiple_of(block_at(upper, column) * rows, rows), rows)
    out_ref[0, 0, :, at] = value


def finish_kernel(near_at, turned_at, inverse, left_ref, right_ref, near_ref, next_ref, back_ref, *refs):
    *turned_refs, token_ref, out_ref = refs
    token_ref[...] = jnp.zeros_like(token_ref)
    folds = len(turned_at) > 0
    rows = left_ref.shape[1] // 4
    upper, inner = fold()

    @pl.when(jnp.logical_not(inner))
    def _():
        for column in range(4):
            own = product(inverse, left_ref, right_ref, upper, 0, column, rows)
            put(out_ref, upper, column, rows, own + read_block(back_ref, column, rows))

    def turned_block(number):
        return read_block(turned_refs[number], turned_at[number], rows).T

    @pl.when(inner)
    def _():
        for column in range(4):
            own = product(inverse, left_ref, right_ref, upper, 1, column, rows)
            if folds and column >= 2:
                own = own + turned_block(3 - column)
            else:
                own = own + read_block(near_ref, near_at + column, rows)
            if folds and column == 0:
                own = own + turned_block(2)
            else:
                own = own + read_block(next_ref, 3 - column, rows)
            put(out_ref, upper, column, rows, own)


def ordered(body, count, held, *refs):
    body(*refs[:count], *refs[count + held :])


def call(body, operands, held, cost, out_shape, **options):
    specs = [pl.BlockSpec(memory_space=pltpu.VMEM)] * len(operands)
    specs += [pl.BlockSpec(memory_space=pl.ANY)] * len(held)
    return pl.pallas_call(
        functools.partial(ordered, body, len(operands), len(held)),
        out_shape=out_shape,
        in_specs=specs,
        compiler_params=pltpu.CompilerParams(vmem_limit_bytes=VMEM_BYTES),
        cost_estimate=pl.CostEstimate(flops=cost, bytes_accessed=cost // 1000, transcendentals=0),
        **options,
    )(*operands, *held)


def folded_line(own_keys, inverse):
    width = own_keys.shape[1]
    rows = width // 4
    last = [own_keys]

    def run(body, operands, shapes, held=(), **options):
        held = (*held, last[0])
        result = call(functools.partial(body, inverse), operands, held, COST, shapes, **options)
        last[0] = jax.tree.leaves(result)[0]
        return result

    def send(rights, *parts):
        count = sum(part[-1] for part in parts)
        operands = (own_keys, *rights)
        message = run(functools.partial(send_kernel, parts), operands, message_shape(count, rows))
        return lax.ppermute(message, "tok", OUTER_TO_INNER)

    def swap(messages):
        half_turn = [(source, (source + 2) % 4) for source in range(4)]
        return [lax.ppermute(message, "layer", half_turn) for message in messages]

    def cross(right, row, count, arrived, swaps=0):
        body = functools.partial(cross_kernel, row, count)
        shapes = [message_shape(count, rows)] + [message_shape(1, rows)] * swaps
        message, *turned = run(body, (own_keys, right, arrived), shapes)
        return lax.ppermute(message, "tok", ACROSS_MIDDLE), *swap(turned)

    def back(right, crossed, swaps=0):
        shapes = [message_shape(4, rows)] + [message_shape(1, rows)] * swaps
        message, *turned = run(back_kernel, (own_keys, right, crossed), shapes)
        return lax.ppermute(message, "tok", INNER_TO_OUTER), *swap(turned)

    def finish(out, distance, right, near_at, turned_at, *operands):
        options = {}
        operands = (own_keys, right, *operands)
        if out is not None:
            options = {"held": (out,), "input_output_aliases": {len(operands): 1}}
        token, out = run(
            functools.partial(finish_kernel, near_at, turned_at),
            operands,
            [
                jax.ShapeDtypeStruct((TAIL, HALF), jnp.bfloat16),
                jax.ShapeDtypeStruct((1, 3, rows, width), jnp.float32),
            ],
            grid=(1,),
            out_specs=[
                pl.BlockSpec((TAIL, HALF), lambda step: (0, 0)),
                pl.BlockSpec((1, 1, rows, width), lambda step: (0, distance, 0, 0)),
            ],
            **options,
        )
        return out

    second_keys = shifted(own_keys, "layer", -1)
    far_0 = send((own_keys,), (0, FAR, 4))
    rest_0 = send((own_keys,), (0, NEXT, 3), (0, NEAR, 2))
    (far_across_0,) = cross(own_keys, FAR, 4, far_0)
    far_1, passed = run(
        functools.partial(pass_on_kernel, ((0, FAR, 4),)),
        (own_keys, second_keys),
        [message_shape(4, rows), jax.ShapeDtypeStruct(own_keys.shape, own_keys.dtype)],
    )
    third_keys = shifted(passed, "layer", -1)
    far_1 = lax.ppermute(far_1, "tok", OUTER_TO_INNER)
    next_1 = send((second_keys,), (0, NEXT, 4))
    (next_across_0,) = cross(own_keys, NEXT, 3, rest_0)
    (back_0,) = back(own_keys, far_across_0)
    (far_across_1,) = cross(second_keys, FAR, 4, far_1)
    far_2 = send((third_keys,), (0, FAR, 4))
    next_2 = send((third_keys,), (0, NEXT, 3))
    (next_across_1,) = cross(second_keys, NEXT, 4, next_1)
    (back_1,) = back(second_keys, far_across_1)
    out = finish(
        None, 0, own_keys, 3, (1, 1, 2), rest_0, next_across_0, back_0, far_0, rest_0, far_across_0
    )
    near = send((second_keys, third_keys), (0, NEAR, 4), (1, NEAR, 2))
    far_across_2, turned_far = cross(third_keys, FAR, 4, far_2, 1)
    next_across_2, turned_next = cross(third_keys, NEXT, 3, next_2, 1)
    back_2, turned_across = back(third_keys, far_across_2, 1)
    out = finish(out, 1, second_keys, 0, (), near, next_across_1, back_1)
    turned = (turned_far, turned_next, turned_across)
    return finish(out, 2, third_keys, 4, (0, 0, 0), near, next_across_2, back_2, *turned)


def per_device(keys):
    own_keys = keys[0]
    layers = lax.axis_size("layer")
    half_span = layers // 2
    inverse = 1.0 / (own_keys.shape[0] * lax.axis_size("tok"))
    if lax.axis_size("tok") == 4 and layers == 4 and own_keys.shape[1] % (8 * HALF) == 0:
        return folded_line(own_keys, inverse)
    forward_list = [own_keys]
    for repeat in range(half_span):
        forward_list.append(shifted(forward_list[-1], "layer", -1))
    return reduce_scattered(own_keys, forward_list, inverse)


def solution(mesh):
    in_specs = (P("layer", ("groups", "tok"), None),)
    out_specs = P("layer", None, ("groups", "tok"), None)
    return jax.shard_map(
        per_device, mesh=mesh, in_specs=in_specs, out_specs=out_specs, check_vma=False
    )
```

time: 263 us -> 108 us (0.41)
  waiting for transfers between devices: 222 us -> 57.2 us
  starting transfers between devices: 4.82 us -> 33 us
  Pallas kernels: 0 us -> 15.7 us
  matrix products: 15.4 us -> 0 us
  between operations: 13.1 us -> 0.32 us
  other arithmetic: 3.93 us -> 0 us
    reduce_scatter x3 -> x0, waiting for transfers between devices: 175 us -> none  [per_device(): lax.psum_scatter(tile_rows(inverse, left_keys, right_keys), 'tok', scatte...]
    ppermute x0 -> x19, waiting for transfers between devices: none -> 42.3 us  [the longest x6 25.2 us: send(): return lax.ppermute(message, 'tok', OUTER_TO_INNER)]
    ppermute x2, waiting for transfers between devices: 47.4 us -> 14.9 us  [shifted(): return lax.ppermute(value, axis, pairs)]
    ppermute x0 -> x19, starting transfers between devices: none -> 28.8 us  [the longest x6 15.3 us: send(): return lax.ppermute(message, 'tok', OUTER_TO_INNER)]
    pallas_call x0 -> x19, Pallas kernels: none -> 15.7 us  [call(): pl.pallas_call(functools.partial(ordered, body, len(operands), len(held))...]
    dot_general x3 -> x0, matrix products: 15.4 us -> none  [tile_rows(): lax.dot_general(left_keys, right_keys, (((0,), (0,)), ((), ())), preferre...]
    broadcast_in_dim x1 -> x0, other arithmetic: 3.93 us -> none  [per_device(): return stacked[None]]
  transfers between devices with their start and end apart: 5 -> 21, of which waited for: 5 -> 8; matrix products, arithmetic and copies ran while one was open for 3% -> 0% of each run, Pallas kernels for 0% -> 13%
where the time goes in v1:
time: 108 us
  waiting for transfers between devices  57.2 us (53%)
  starting transfers between devices  33 us (31%)
  Pallas kernels  15.7 us (15%)
  local copies, waits for them, and re-layouts  1.62 us (2%)
    ppermute x6, waiting for transfers between devices, send(): return lax.ppermute(message, 'tok', OUTER_TO_INNER)  25.2 us
    pallas_call x19, Pallas kernels, call(): pl.pallas_call(functools.partial(ordered, body, len(operands), len(held))...  15.7 us
    ppermute x6, starting transfers between devices, send(): return lax.ppermute(message, 'tok', OUTER_TO_INNER)  15.3 us
    ppermute x2, waiting for transfers between devices, shifted(): return lax.ppermute(value, axis, pairs)  14.9 us
    ppermute x1, waiting for transfers between devices, folded_line(): far_1 = lax.ppermute(far_1, 'tok', OUTER_TO_INNER)  8.97 us
    ppermute x3, waiting for transfers between devices, back(): return (lax.ppermute(message, 'tok', INNER_TO_OUTER), *swap(turned))  4.44 us
    ppermute x6, starting transfers between devices, cross(): return (lax.ppermute(message, 'tok', ACROSS_MIDDLE), *swap(turned))  4.33 us
    ppermute x2, starting transfers between devices, shifted(): return lax.ppermute(value, axis, pairs)  4.25 us
  transfers between devices with their start and end apart: 21, of which 8 were waited for; matrix products, arithmetic and copies ran while one was open for 0% of the time, Pallas kernels for 13%

profile of v1, /device:TPU:0, one launch (start us, length us, event | category | flops | bytes accessed | tf_op | source)
XLA Modules:
  0.0 107.9 jit_solution(16373944416131335837)
XLA Ops:
  0.0 2.4 %collective-permute-start = (bf16[1024,1024]{1,0:T(8,128)(2,1)}, bf16[1024,1024]{1,0:T(8,128)(2,1)S(1)}, u32[]{:S(2)}, u32[]{:S(2)}) collective-permute-start(bf16[1024,1024]{1,0:T(8,128)(2,1)} %bitcast.1), channel_id=1, source_target_pairs={{0,12},{4,0},{8,4},{12,8},{1,13},{5,1},{9,5},{13,9},{2,14},{6,2},{... | collective-permute-start | bytes 6291464 | tf_op jit(solution)/shard_map/ppermute | solution.py:26
  2.4 1.6 %copy-done = bf16[1,1024,1024]{2,1,0:T(8,128)(2,1)S(1)} copy-done((bf16[1,1024,1024]{2,1,0:T(8,128)(2,1)S(1)}, bf16[1,1024,1024]{2,1,0:T(8,128)(2,1)}, u32[]{:S(2)}) %copy-start) | copy-done | bytes 2097176
  4.0 1.2 %shard_map.17.refs_2_ = bf16[2064,128]{1,0:T(8,128)(2,1)S(1)} custom-call(bf16[1024,1024]{1,0:T(8,128)(2,1)S(1)} %bitcast.2, bf16[1024,1024]{1,0:T(8,128)(2,1)S(1)} %bitcast.3, bf16[1024,1024]{1,0:T(8,128)(2,1)S(1)} %bitcast.4), custom_call_target="tpu_custom_call" | custom-call | flops 10000000000 | bytes 10000000 | tf_op jit(solution)/shard_map/pallas_call | solution.py:233
  5.2 2.3 %collective-permute-start.1 = (bf16[2064,128]{1,0:T(8,128)(2,1)S(1)}, bf16[2064,128]{1,0:T(8,128)(2,1)S(1)}, u32[]{:S(2)}, u32[]{:S(2)}) collective-permute-start(bf16[2064,128]{1,0:T(8,128)(2,1)S(1)} %shard_map.17.refs_2_), channel_id=1, source_target_pairs={{0,1},{3,2},{4,5},{7,6},{8,9},{11,10},{12,13},{15,14},{16,17},{19,... | collective-permute-start | bytes 1585160 | tf_op jit(solution)/shard_map/ppermute | solution.py:258
  7.5 1.5 %shard_map.18.refs_3_ = bf16[2576,128]{1,0:T(8,128)(2,1)S(1)} custom-call(bf16[1024,1024]{1,0:T(8,128)(2,1)S(1)} %bitcast.5, bf16[1024,1024]{1,0:T(8,128)(2,1)S(1)} %bitcast.6, bf16[2064,128]{1,0:T(8,128)(2,1)S(1)} %shard_map.17.refs_2_), custom_call_target="tpu_custom_call" | custom-call | flops 10000000000 | bytes 10000000 | tf_op jit(solution)/shard_map/pallas_call | solution.py:233
  9.0 1.3 %collective-permute-start.3 = (bf16[2576,128]{1,0:T(8,128)(2,1)S(1)}, bf16[2576,128]{1,0:T(8,128)(2,1)S(1)}, u32[]{:S(2)}, u32[]{:S(2)}) collective-permute-start(bf16[2576,128]{1,0:T(8,128)(2,1)S(1)} %shard_map.18.refs_3_), channel_id=1, source_target_pairs={{0,1},{3,2},{4,5},{7,6},{8,9},{11,10},{12,13},{15,14},{16,17},{19,... | collective-permute-start | bytes 1978376 | tf_op jit(solution)/shard_map/ppermute | solution.py:258
  10.3 9.6 %collective-permute-done.1.refs_2_.refs_5_ = bf16[2064,128]{1,0:T(8,128)(2,1)S(1)} collective-permute-done((bf16[2064,128]{1,0:T(8,128)(2,1)S(1)}, bf16[2064,128]{1,0:T(8,128)(2,1)S(1)}, u32[]{:S(2)}, u32[]{:S(2)}) %collective-permute-start.1) | collective-permute-done | bytes 528416 | tf_op jit(solution)/shard_map/ppermute | solution.py:258
  20.6 5.6 %collective-permute-done.refs_1_ = bf16[1024,1024]{1,0:T(8,128)(2,1)S(1)} collective-permute-done((bf16[1024,1024]{1,0:T(8,128)(2,1)}, bf16[1024,1024]{1,0:T(8,128)(2,1)S(1)}, u32[]{:S(2)}, u32[]{:S(2)}) %collective-permute-start) | collective-permute-done | bytes 2097184 | tf_op jit(solution)/shard_map/ppermute | solution.py:26
  26.2 1.4 %shard_map.20 = (bf16[2064,128]{1,0:T(8,128)(2,1)S(1)}, bf16[1024,1024]{1,0:T(8,128)(2,1)S(1)}) custom-call(bf16[1024,1024]{1,0:T(8,128)(2,1)S(1)} %bitcast.9, bf16[1024,1024]{1,0:T(8,128)(2,1)S(1)} %collective-permute-done.refs_1_, bf16[2064,128]{1,0:T(8,128)(2,1)S(1)} %shard_map.19.refs_2_), custom_call_target="tpu_custom_call" | custom-call | flops 10000000000 | bytes 10000000 | tf_op jit(solution)/shard_map/pallas_call | solution.py:233
  27.6 2.3 %collective-permute-start.7 = (bf16[2064,128]{1,0:T(8,128)(2,1)S(1)}, bf16[2064,128]{1,0:T(8,128)(2,1)S(1)}, u32[]{:S(2)}, u32[]{:S(2)}) collective-permute-start(bf16[2064,128]{1,0:T(8,128)(2,1)S(1)} %get-tuple-element.19.refs_2_), channel_id=1, source_target_pairs={{0,1},{3,2},{4,5},{7,6},{8,9},{11,10},{12,13},{15,14},{16,17},{19,... | collective-permute-start | bytes 1585160 | tf_op jit(solution)/shard_map/ppermute | solution.py:306
  29.9 1.9 %collective-permute-start.2 = (bf16[1024,1024]{1,0:T(8,128)(2,1)S(1)}, bf16[1024,1024]{1,0:T(8,128)(2,1)S(1)}, u32[]{:S(2)}, u32[]{:S(2)}) collective-permute-start(bf16[1024,1024]{1,0:T(8,128)(2,1)S(1)} %get-tuple-element.18), channel_id=1, source_target_pairs={{0,12},{4,0},{8,4},{12,8},{1,13},{5,1},{9,5},{13,9},{2,14},{6,2},{... | collective-permute-start | bytes 6291464 | tf_op jit(solution)/shard_map/ppermute | solution.py:26
  31.8 1.2 %shard_map.21.refs_3_ = bf16[2064,128]{1,0:T(8,128)(2,1)S(1)} custom-call(bf16[1024,1024]{1,0:T(8,128)(2,1)S(1)} %bitcast.10, bf16[1024,1024]{1,0:T(8,128)(2,1)S(1)} %collective-permute-done.refs_1_, bf16[2064,128]{1,0:T(8,128)(2,1)S(1)} %get-tuple-element.19.refs_2_), custom_call_target="tpu_custom_call" | custom-call | flops 10000000000 | bytes 10000000 | tf_op jit(solution)/shard_map/pallas_call | solution.py:233
  33.0 1.3 %collective-permute-start.9 = (bf16[2064,128]{1,0:T(8,128)(2,1)S(1)}, bf16[2064,128]{1,0:T(8,128)(2,1)S(1)}, u32[]{:S(2)}, u32[]{:S(2)}) collective-permute-start(bf16[2064,128]{1,0:T(8,128)(2,1)S(1)} %shard_map.21.refs_3_), channel_id=1, source_target_pairs={{0,1},{3,2},{4,5},{7,6},{8,9},{11,10},{12,13},{15,14},{16,17},{19,... | collective-permute-start | bytes 1585160 | tf_op jit(solution)/shard_map/ppermute | solution.py:258
  35.1 1.3 %collective-permute-start.6 = (bf16[2064,128]{1,0:T(8,128)(2,1)S(1)}, bf16[2064,128]{1,0:T(8,128)(2,1)S(1)}, u32[]{:S(2)}, u32[]{:S(2)}) collective-permute-start(bf16[2064,128]{1,0:T(8,128)(2,1)S(1)} %shard_map.23.refs_3_), channel_id=1, source_target_pairs={{1,0},{2,3},{5,4},{6,7},{9,8},{10,11},{13,12},{14,15},{17,16},{18,... | collective-permute-start | bytes 1585160 | tf_op jit(solution)/shard_map/ppermute | solution.py:273
  36.4 9.0 %collective-permute-done.7.refs_2_ = bf16[2064,128]{1,0:T(8,128)(2,1)S(1)} collective-permute-done((bf16[2064,128]{1,0:T(8,128)(2,1)S(1)}, bf16[2064,128]{1,0:T(8,128)(2,1)S(1)}, u32[]{:S(2)}, u32[]{:S(2)}) %collective-permute-start.7) | collective-permute-done | bytes 528416 | tf_op jit(solution)/shard_map/ppermute | solution.py:306
  46.1 9.3 %collective-permute-done.2.refs_1_.refs_2_ = bf16[1024,1024]{1,0:T(8,128)(2,1)S(1)} collective-permute-done((bf16[1024,1024]{1,0:T(8,128)(2,1)S(1)}, bf16[1024,1024]{1,0:T(8,128)(2,1)S(1)}, u32[]{:S(2)}, u32[]{:S(2)}) %collective-permute-start.2) | collective-permute-done | bytes 2097184 | tf_op jit(solution)/shard_map/ppermute | solution.py:26
  55.3 1.2 %shard_map.25.refs_2_ = bf16[2064,128]{1,0:T(8,128)(2,1)S(1)} custom-call(bf16[1024,1024]{1,0:T(8,128)(2,1)S(1)} %bitcast.16, bf16[1024,1024]{1,0:T(8,128)(2,1)S(1)} %collective-permute-done.2.refs_1_.refs_2_, bf16[2064,128]{1,0:T(8,128)(2,1)S(1)} %shard_map.24.refs_2_), custom_call_target="tpu_custom_call" | custom-call | flops 10000000000 | bytes 10000000 | tf_op jit(solution)/shard_map/pallas_call | solution.py:233
  56.6 1.3 %collective-permute-start.12 = (bf16[2064,128]{1,0:T(8,128)(2,1)S(1)}, bf16[2064,128]{1,0:T(8,128)(2,1)S(1)}, u32[]{:S(2)}, u32[]{:S(2)}) collective-permute-start(bf16[2064,128]{1,0:T(8,128)(2,1)S(1)} %shard_map.25.refs_2_), channel_id=1, source_target_pairs={{0,1},{3,2},{4,5},{7,6},{8,9},{11,10},{12,13},{15,14},{16,17},{19,... | collective-permute-start | bytes 1585160 | tf_op jit(solution)/shard_map/ppermute | solution.py:258
  57.9 1.0 shard_map.26.refs_3_
  58.9 1.3 %collective-permute-start.11 = (bf16[1552,128]{1,0:T(8,128)(2,1)S(1)}, bf16[1552,128]{1,0:T(8,128)(2,1)S(1)}, u32[]{:S(2)}, u32[]{:S(2)}) collective-permute-start(bf16[1552,128]{1,0:T(8,128)(2,1)S(1)} %shard_map.26.refs_3_), channel_id=1, source_target_pairs={{0,1},{3,2},{4,5},{7,6},{8,9},{11,10},{12,13},{15,14},{16,17},{19,... | collective-permute-start | bytes 1191944 | tf_op jit(solution)/shard_map/ppermute | solution.py:258
  61.0 1.3 %collective-permute-start.20 = (bf16[2064,128]{1,0:T(8,128)(2,1)S(1)}, bf16[2064,128]{1,0:T(8,128)(2,1)S(1)}, u32[]{:S(2)}, u32[]{:S(2)}) collective-permute-start(bf16[2064,128]{1,0:T(8,128)(2,1)S(1)} %shard_map.28.refs_8_), channel_id=1, source_target_pairs={{1,0},{2,3},{5,4},{6,7},{9,8},{10,11},{13,12},{14,15},{17,16},{18,... | collective-permute-start | bytes 1585160 | tf_op jit(solution)/shard_map/ppermute | solution.py:273
  62.3 2.2 %shard_map.29 = (bf16[16,128]{1,0:T(8,128)(2,1)S(1)}, f32[1,3,256,1024]{3,2,1,0:T(8,128)}) custom-call(bf16[1024,1024]{1,0:T(8,128)(2,1)S(1)} %bitcast.20, bf16[1024,1024]{1,0:T(8,128)(2,1)S(1)} %bitcast.21, bf16[2576,128]{1,0:T(8,128)(2,1)S(1)} %collective-permute-done.3.refs_2_.refs_6_, bf16[1552,128]{1,0:T(8,128)(2,1)S(1)} %collective-permute-done.4.refs_3_, ...), custom_call_target="tpu_custom_call" | custom-call | flops 10000000000 | bytes 10000000 | tf_op jit(solution)/shard_map/pallas_call | solution.py:233
  64.5 1.7 %shard_map.30.refs_3_ = bf16[3088,128]{1,0:T(8,128)(2,1)S(1)} custom-call(bf16[1024,1024]{1,0:T(8,128)(2,1)S(1)} %bitcast.22, bf16[1024,1024]{1,0:T(8,128)(2,1)S(1)} %collective-permute-done.refs_1_, bf16[1024,1024]{1,0:T(8,128)(2,1)S(1)} %collective-permute-done.2.refs_1_.refs_2_, bf16[16,128]{1,0:T(8,128)(2,1)S(1)} %get-tuple-element.20.refs_3_), custom_call_target="tpu_custom_call" | custom-call | flops 10000000000 | bytes 10000000 | tf_op jit(solution)/shard_map/pallas_call | solution.py:233
  66.2 7.7 %collective-permute-start.10 = (bf16[3088,128]{1,0:T(8,128)(2,1)S(1)}, bf16[3088,128]{1,0:T(8,128)(2,1)S(1)}, u32[]{:S(2)}, u32[]{:S(2)}) collective-permute-start(bf16[3088,128]{1,0:T(8,128)(2,1)S(1)} %shard_map.30.refs_3_), channel_id=1, source_target_pairs={{0,1},{3,2},{4,5},{7,6},{8,9},{11,10},{12,13},{15,14},{16,17},{19,... | collective-permute-start | bytes 2371592 | tf_op jit(solution)/shard_map/ppermute | solution.py:258
  74.6 4.0 %collective-permute-done.11.refs_2_ = bf16[1552,128]{1,0:T(8,128)(2,1)S(1)} collective-permute-done((bf16[1552,128]{1,0:T(8,128)(2,1)S(1)}, bf16[1552,128]{1,0:T(8,128)(2,1)S(1)}, u32[]{:S(2)}, u32[]{:S(2)}) %collective-permute-start.11) | collective-permute-done | bytes 397344 | tf_op jit(solution)/shard_map/ppermute | solution.py:258
  79.6 3.0 %collective-permute-start.16 = (bf16[528,128]{1,0:T(8,128)(2,1)S(1)}, bf16[528,128]{1,0:T(8,128)(2,1)S(1)}, u32[]{:S(2)}, u32[]{:S(2)}) collective-permute-start(bf16[528,128]{1,0:T(8,128)(2,1)S(1)} %get-tuple-element.24), channel_id=1, source_target_pairs={{0,8},{4,12},{8,0},{12,4},{1,9},{5,13},{9,1},{13,5},{2,10},{6,14},... | collective-permute-start | bytes 405512 | tf_op jit(solution)/shard_map/ppermute | solution.py:262
  82.6 1.3 %collective-permute-start.15 = (bf16[2064,128]{1,0:T(8,128)(2,1)S(1)}, bf16[2064,128]{1,0:T(8,128)(2,1)S(1)}, u32[]{:S(2)}, u32[]{:S(2)}) collective-permute-start(bf16[2064,128]{1,0:T(8,128)(2,1)S(1)} %get-tuple-element.23.refs_6_), channel_id=1, source_target_pairs={{1,0},{2,3},{5,4},{6,7},{9,8},{10,11},{13,12},{14,15},{17,16},{18,... | collective-permute-start | bytes 1585160 | tf_op jit(solution)/shard_map/ppermute | solution.py:273
  83.9 11.7 %collective-permute-done.10.refs_2_ = bf16[3088,128]{1,0:T(8,128)(2,1)S(1)} collective-permute-done((bf16[3088,128]{1,0:T(8,128)(2,1)S(1)}, bf16[3088,128]{1,0:T(8,128)(2,1)S(1)}, u32[]{:S(2)}, u32[]{:S(2)}) %collective-permute-start.10) | collective-permute-done | bytes 790560 | tf_op jit(solution)/shard_map/ppermute | solution.py:258
  95.6 2.1 %shard_map.34 = (bf16[16,128]{1,0:T(8,128)(2,1)S(1)}, f32[1,3,256,1024]{3,2,1,0:T(8,128)}) custom-call(bf16[1024,1024]{1,0:T(8,128)(2,1)S(1)} %bitcast.26, bf16[1024,1024]{1,0:T(8,128)(2,1)S(1)} %collective-permute-done.refs_1_, bf16[3088,128]{1,0:T(8,128)(2,1)S(1)} %collective-permute-done.10.refs_2_, ...), custom_call_target="tpu_custom_call", output_to_operand_aliasing={{1}: (5, {})} | custom-call | flops 10000000000 | bytes 10000000 | tf_op jit(solution)/shard_map/pallas_call | solution.py:233
  97.7 3.7 %collective-permute-done.18.refs_7_ = bf16[528,128]{1,0:T(8,128)(2,1)S(1)} collective-permute-done((bf16[528,128]{1,0:T(8,128)(2,1)S(1)}, bf16[528,128]{1,0:T(8,128)(2,1)S(1)}, u32[]{:S(2)}, u32[]{:S(2)}) %collective-permute-start.18) | collective-permute-done | bytes 135200 | tf_op jit(solution)/shard_map/ppermute | solution.py:262
  101.3 4.4 %collective-permute-done.15.refs_4_ = bf16[2064,128]{1,0:T(8,128)(2,1)S(1)} collective-permute-done((bf16[2064,128]{1,0:T(8,128)(2,1)S(1)}, bf16[2064,128]{1,0:T(8,128)(2,1)S(1)}, u32[]{:S(2)}, u32[]{:S(2)}) %collective-permute-start.15) | collective-permute-done | bytes 528416 | tf_op jit(solution)/shard_map/ppermute | solution.py:273
  105.8 2.1 %shard_map.35 = (bf16[16,128]{1,0:T(8,128)(2,1)}, f32[1,3,256,1024]{3,2,1,0:T(8,128)}) custom-call(bf16[1024,1024]{1,0:T(8,128)(2,1)S(1)} %bitcast.27, bf16[1024,1024]{1,0:T(8,128)(2,1)S(1)} %collective-permute-done.2.refs_1_.refs_2_, bf16[3088,128]{1,0:T(8,128)(2,1)S(1)} %collective-permute-done.10.refs_2_, ...), custom_call_target="tpu_custom_call", output_to_operand_aliasing={{1}: (8, {})} | custom-call | flops 10000000000 | bytes 10000000 | tf_op jit(solution)/shard_map/pallas_call | solution.py:233
  (31 shorter events, 4.5 us)
Async XLA Ops:
  0.0 26.2 %collective-permute-start = (bf16[1024,1024]{1,0:T(8,128)(2,1)}, bf16[1024,1024]{1,0:T(8,128)(2,1)S(1)}, u32[]{:S(2)}, u32[]{:S(2)}) collective-permute-start(bf16[1024,1024]{1,0:T(8,128)(2,1)} %bitcast.1), channel_id=1, source_target_pairs={{0,12},{4,0},{8,4},{12,8},{1,13},{5,1},{9,5},{13,9},{2,14},{6,2},{... | collective-permute-start | bytes 6291464 | tf_op jit(solution)/shard_map/ppermute | solution.py:26
  2.4 1.6 %copy-start = (bf16[1,1024,1024]{2,1,0:T(8,128)(2,1)S(1)}, bf16[1,1024,1024]{2,1,0:T(8,128)(2,1)}, u32[]{:S(2)}) copy-start(bf16[1,1024,1024]{2,1,0:T(8,128)(2,1)} %param.1) | copy-start | bytes 6291460
  5.2 14.7 %collective-permute-start.1 = (bf16[2064,128]{1,0:T(8,128)(2,1)S(1)}, bf16[2064,128]{1,0:T(8,128)(2,1)S(1)}, u32[]{:S(2)}, u32[]{:S(2)}) collective-permute-start(bf16[2064,128]{1,0:T(8,128)(2,1)S(1)} %shard_map.17.refs_2_), channel_id=1, source_target_pairs={{0,1},{3,2},{4,5},{7,6},{8,9},{11,10},{12,13},{15,14},{16,17},{19,... | collective-permute-start | bytes 1585160 | tf_op jit(solution)/shard_map/ppermute | solution.py:258
  9.0 25.3 %collective-permute-start.3 = (bf16[2576,128]{1,0:T(8,128)(2,1)S(1)}, bf16[2576,128]{1,0:T(8,128)(2,1)S(1)}, u32[]{:S(2)}, u32[]{:S(2)}) collective-permute-start(bf16[2576,128]{1,0:T(8,128)(2,1)S(1)} %shard_map.18.refs_3_), channel_id=1, source_target_pairs={{0,1},{3,2},{4,5},{7,6},{8,9},{11,10},{12,13},{15,14},{16,17},{19,... | collective-permute-start | bytes 1978376 | tf_op jit(solution)/shard_map/ppermute | solution.py:258
  19.9 15.2 %collective-permute-start.5 = (bf16[2064,128]{1,0:T(8,128)(2,1)S(1)}, bf16[2064,128]{1,0:T(8,128)(2,1)S(1)}, u32[]{:S(2)}, u32[]{:S(2)}) collective-permute-start(bf16[2064,128]{1,0:T(8,128)(2,1)S(1)} %shard_map.19.refs_2_), channel_id=1, source_target_pairs={{1,2},{2,1},{5,6},{6,5},{9,10},{10,9},{13,14},{14,13},{17,18},{18,... | collective-permute-start | bytes 1585160 | tf_op jit(solution)/shard_map/ppermute | solution.py:268
  27.6 17.8 %collective-permute-start.7 = (bf16[2064,128]{1,0:T(8,128)(2,1)S(1)}, bf16[2064,128]{1,0:T(8,128)(2,1)S(1)}, u32[]{:S(2)}, u32[]{:S(2)}) collective-permute-start(bf16[2064,128]{1,0:T(8,128)(2,1)S(1)} %get-tuple-element.19.refs_2_), channel_id=1, source_target_pairs={{0,1},{3,2},{4,5},{7,6},{8,9},{11,10},{12,13},{15,14},{16,17},{19,... | collective-permute-start | bytes 1585160 | tf_op jit(solution)/shard_map/ppermute | solution.py:306
  29.9 25.4 %collective-permute-start.2 = (bf16[1024,1024]{1,0:T(8,128)(2,1)S(1)}, bf16[1024,1024]{1,0:T(8,128)(2,1)S(1)}, u32[]{:S(2)}, u32[]{:S(2)}) collective-permute-start(bf16[1024,1024]{1,0:T(8,128)(2,1)S(1)} %get-tuple-element.18), channel_id=1, source_target_pairs={{0,12},{4,0},{8,4},{12,8},{1,13},{5,1},{9,5},{13,9},{2,14},{6,2},{... | collective-permute-start | bytes 6291464 | tf_op jit(solution)/shard_map/ppermute | solution.py:26
  33.0 25.9 %collective-permute-start.9 = (bf16[2064,128]{1,0:T(8,128)(2,1)S(1)}, bf16[2064,128]{1,0:T(8,128)(2,1)S(1)}, u32[]{:S(2)}, u32[]{:S(2)}) collective-permute-start(bf16[2064,128]{1,0:T(8,128)(2,1)S(1)} %shard_map.21.refs_3_), channel_id=1, source_target_pairs={{0,1},{3,2},{4,5},{7,6},{8,9},{11,10},{12,13},{15,14},{16,17},{19,... | collective-permute-start | bytes 1585160 | tf_op jit(solution)/shard_map/ppermute | solution.py:258
  34.4 26.7 %collective-permute-start.4 = (bf16[1552,128]{1,0:T(8,128)(2,1)S(1)}, bf16[1552,128]{1,0:T(8,128)(2,1)S(1)}, u32[]{:S(2)}, u32[]{:S(2)}) collective-permute-start(bf16[1552,128]{1,0:T(8,128)(2,1)S(1)} %shard_map.22.refs_3_), channel_id=1, source_target_pairs={{1,2},{2,1},{5,6},{6,5},{9,10},{10,9},{13,14},{14,13},{17,18},{18,... | collective-permute-start | bytes 1191944 | tf_op jit(solution)/shard_map/ppermute | solution.py:268
  35.1 27.2 %collective-permute-start.6 = (bf16[2064,128]{1,0:T(8,128)(2,1)S(1)}, bf16[2064,128]{1,0:T(8,128)(2,1)S(1)}, u32[]{:S(2)}, u32[]{:S(2)}) collective-permute-start(bf16[2064,128]{1,0:T(8,128)(2,1)S(1)} %shard_map.23.refs_3_), channel_id=1, source_target_pairs={{1,0},{2,3},{5,4},{6,7},{9,8},{10,11},{13,12},{14,15},{17,16},{18,... | collective-permute-start | bytes 1585160 | tf_op jit(solution)/shard_map/ppermute | solution.py:273
  45.4 14.9 %collective-permute-start.8 = (bf16[2064,128]{1,0:T(8,128)(2,1)S(1)}, bf16[2064,128]{1,0:T(8,128)(2,1)S(1)}, u32[]{:S(2)}, u32[]{:S(2)}) collective-permute-start(bf16[2064,128]{1,0:T(8,128)(2,1)S(1)} %shard_map.24.refs_2_), channel_id=1, source_target_pairs={{1,2},{2,1},{5,6},{6,5},{9,10},{10,9},{13,14},{14,13},{17,18},{18,... | collective-permute-start | bytes 1585160 | tf_op jit(solution)/shard_map/ppermute | solution.py:268
  56.6 17.4 %collective-permute-start.12 = (bf16[2064,128]{1,0:T(8,128)(2,1)S(1)}, bf16[2064,128]{1,0:T(8,128)(2,1)S(1)}, u32[]{:S(2)}, u32[]{:S(2)}) collective-permute-start(bf16[2064,128]{1,0:T(8,128)(2,1)S(1)} %shard_map.25.refs_2_), channel_id=1, source_target_pairs={{0,1},{3,2},{4,5},{7,6},{8,9},{11,10},{12,13},{15,14},{16,17},{19,... | collective-permute-start | bytes 1585160 | tf_op jit(solution)/shard_map/ppermute | solution.py:258
  58.9 19.7 %collective-permute-start.11 = (bf16[1552,128]{1,0:T(8,128)(2,1)S(1)}, bf16[1552,128]{1,0:T(8,128)(2,1)S(1)}, u32[]{:S(2)}, u32[]{:S(2)}) collective-permute-start(bf16[1552,128]{1,0:T(8,128)(2,1)S(1)} %shard_map.26.refs_3_), channel_id=1, source_target_pairs={{0,1},{3,2},{4,5},{7,6},{8,9},{11,10},{12,13},{15,14},{16,17},{19,... | collective-permute-start | bytes 1191944 | tf_op jit(solution)/shard_map/ppermute | solution.py:258
  60.3 22.3 %collective-permute-start.19 = (bf16[2064,128]{1,0:T(8,128)(2,1)S(1)}, bf16[2064,128]{1,0:T(8,128)(2,1)S(1)}, u32[]{:S(2)}, u32[]{:S(2)}) collective-permute-start(bf16[2064,128]{1,0:T(8,128)(2,1)S(1)} %shard_map.27.refs_3_), channel_id=1, source_target_pairs={{1,2},{2,1},{5,6},{6,5},{9,10},{10,9},{13,14},{14,13},{17,18},{18,... | collective-permute-start | bytes 1585160 | tf_op jit(solution)/shard_map/ppermute | solution.py:268
  61.0 18.6 %collective-permute-start.20 = (bf16[2064,128]{1,0:T(8,128)(2,1)S(1)}, bf16[2064,128]{1,0:T(8,128)(2,1)S(1)}, u32[]{:S(2)}, u32[]{:S(2)}) collective-permute-start(bf16[2064,128]{1,0:T(8,128)(2,1)S(1)} %shard_map.28.refs_8_), channel_id=1, source_target_pairs={{1,0},{2,3},{5,4},{6,7},{9,8},{10,11},{13,12},{14,15},{17,16},{18,... | collective-permute-start | bytes 1585160 | tf_op jit(solution)/shard_map/ppermute | solution.py:273
  66.2 29.4 %collective-permute-start.10 = (bf16[3088,128]{1,0:T(8,128)(2,1)S(1)}, bf16[3088,128]{1,0:T(8,128)(2,1)S(1)}, u32[]{:S(2)}, u32[]{:S(2)}) collective-permute-start(bf16[3088,128]{1,0:T(8,128)(2,1)S(1)} %shard_map.30.refs_3_), channel_id=1, source_target_pairs={{0,1},{3,2},{4,5},{7,6},{8,9},{11,10},{12,13},{15,14},{16,17},{19,... | collective-permute-start | bytes 2371592 | tf_op jit(solution)/shard_map/ppermute | solution.py:258
  73.9 5.6 %collective-permute-start.14 = (bf16[2064,128]{1,0:T(8,128)(2,1)S(1)}, bf16[2064,128]{1,0:T(8,128)(2,1)S(1)}, u32[]{:S(2)}, u32[]{:S(2)}) collective-permute-start(bf16[2064,128]{1,0:T(8,128)(2,1)S(1)} %get-tuple-element.21.refs_3_), channel_id=1, source_target_pairs={{1,2},{2,1},{5,6},{6,5},{9,10},{10,9},{13,14},{14,13},{17,18},{18,... | collective-permute-start | bytes 1585160 | tf_op jit(solution)/shard_map/ppermute | solution.py:268
  78.6 19.1 %collective-permute-start.13 = (bf16[1552,128]{1,0:T(8,128)(2,1)S(1)}, bf16[1552,128]{1,0:T(8,128)(2,1)S(1)}, u32[]{:S(2)}, u32[]{:S(2)}) collective-permute-start(bf16[1552,128]{1,0:T(8,128)(2,1)S(1)} %get-tuple-element.22.refs_3_), channel_id=1, source_target_pairs={{1,2},{2,1},{5,6},{6,5},{9,10},{10,9},{13,14},{14,13},{17,18},{18,... | collective-permute-start | bytes 1191944 | tf_op jit(solution)/shard_map/ppermute | solution.py:268
  79.5 18.2 %collective-permute-start.17 = (bf16[528,128]{1,0:T(8,128)(2,1)S(1)}, bf16[528,128]{1,0:T(8,128)(2,1)S(1)}, u32[]{:S(2)}, u32[]{:S(2)}) collective-permute-start(bf16[528,128]{1,0:T(8,128)(2,1)S(1)} %get-tuple-element.25), channel_id=1, source_target_pairs={{0,8},{4,12},{8,0},{12,4},{1,9},{5,13},{9,1},{13,5},{2,10},{6,14},... | collective-permute-start | bytes 405512 | tf_op jit(solution)/shard_map/ppermute | solution.py:262
  79.6 18.0 %collective-permute-start.16 = (bf16[528,128]{1,0:T(8,128)(2,1)S(1)}, bf16[528,128]{1,0:T(8,128)(2,1)S(1)}, u32[]{:S(2)}, u32[]{:S(2)}) collective-permute-start(bf16[528,128]{1,0:T(8,128)(2,1)S(1)} %get-tuple-element.24), channel_id=1, source_target_pairs={{0,8},{4,12},{8,0},{12,4},{1,9},{5,13},{9,1},{13,5},{2,10},{6,14},... | collective-permute-start | bytes 405512 | tf_op jit(solution)/shard_map/ppermute | solution.py:262
  82.6 23.2 %collective-permute-start.15 = (bf16[2064,128]{1,0:T(8,128)(2,1)S(1)}, bf16[2064,128]{1,0:T(8,128)(2,1)S(1)}, u32[]{:S(2)}, u32[]{:S(2)}) collective-permute-start(bf16[2064,128]{1,0:T(8,128)(2,1)S(1)} %get-tuple-element.23.refs_6_), channel_id=1, source_target_pairs={{1,0},{2,3},{5,4},{6,7},{9,8},{10,11},{13,12},{14,15},{17,16},{18,... | collective-permute-start | bytes 1585160 | tf_op jit(solution)/shard_map/ppermute | solution.py:273
  95.5 5.8 %collective-permute-start.18 = (bf16[528,128]{1,0:T(8,128)(2,1)S(1)}, bf16[528,128]{1,0:T(8,128)(2,1)S(1)}, u32[]{:S(2)}, u32[]{:S(2)}) collective-permute-start(bf16[528,128]{1,0:T(8,128)(2,1)S(1)} %get-tuple-element.26), channel_id=1, source_target_pairs={{0,8},{4,12},{8,0},{12,4},{1,9},{5,13},{9,1},{13,5},{2,10},{6,14},... | collective-permute-start | bytes 405512 | tf_op jit(solution)/shard_map/ppermute | solution.py:262

commit v2 on v1

v2 whole, which is shorter than its diff:
```python
import functools

import jax
import jax.numpy as jnp
from jax import lax
from jax.experimental import pallas as pl
from jax.experimental.pallas import tpu as pltpu
from jax.sharding import PartitionSpec as P

OUTER_TO_INNER = [(0, 1), (3, 2)]
ACROSS_MIDDLE = [(1, 2), (2, 1)]
INNER_TO_OUTER = [(1, 0), (2, 3)]
FAR, NEXT, NEAR = 3, 2, 1

HALF = 128
TAIL = 16
SPREAD = 13777.0
SMALLEST = 1e-30
COSTS = tuple(1_000_000_000 * cost for cost in (3, 3, 3, 30, 4, 4, 4, 4, 4, 4, 4, 4, 4, 4, 4, 4, 4, 4, 4, 4, 4))
VMEM_BYTES = 24 * 1024 * 1024


def shifted(value, axis, steps):
    count = lax.axis_size(axis)
    pairs = [(source, (source + steps) % count) for source in range(count)]
    return lax.ppermute(value, axis, pairs)


def tile_rows(inverse, left_keys, right_keys):
    product = lax.dot_general(
        left_keys, right_keys, (((0,), (0,)), ((), ())), preferred_element_type=jnp.float32
    )
    return product * inverse


def reduce_scattered(own_keys, forward_list, inverse):
    shares = [
        lax.psum_scatter(
            tile_rows(inverse, own_keys, right_keys), "tok", scatter_dimension=0, tiled=True
        )
        for right_keys in forward_list
    ]
    return jnp.stack(shares)[None]


def fold():
    place = lax.axis_index("tok")
    upper = place >= 2
    inner = jnp.logical_or(place == 1, place == 2)
    return upper, inner


def block_at(upper, index):
    return jnp.where(upper, 3 - index, index)


def product(inverse, left_ref, right_ref, upper, row, column, rows):
    left = left_ref[:, pl.ds(pl.multiple_of(block_at(upper, row) * rows, rows), rows)]
    if column is None:
        return tile_rows(inverse, left, right_ref[...])
    at = pl.ds(pl.multiple_of(block_at(upper, column) * rows, rows), rows)
    return tile_rows(inverse, left, right_ref[:, at])


def row_factor(rows):
    index = lax.broadcasted_iota(jnp.int32, (rows, HALF), 0).astype(jnp.float32) * 0.6180339887
    return 1.0 + (index - jnp.floor(index))


def column_factor(half):
    index = lax.broadcasted_iota(jnp.int32, (1, HALF), 1).astype(jnp.float32) + float(half * HALF)
    index = index * 0.7548776662
    return 1.0 + (index - jnp.floor(index))


def peak_of(value):
    return jnp.max(jnp.max(jnp.abs(value), axis=0, keepdims=True), axis=1, keepdims=True)


def code(scaled):
    power = scaled * scaled
    power = power * power
    power = power * power
    return jnp.where(scaled < 0.0, -power, power)


def decoded(coded):
    root = lax.rsqrt(lax.rsqrt(jnp.maximum(jnp.abs(coded), 1.2e-38)))
    root = root * lax.rsqrt(root)
    return jnp.where(coded < 0.0, -root, root)


def write_message(message_ref, blocks, diagonal=None):
    rows = blocks[0].shape[0]
    peak = functools.reduce(jnp.maximum, [peak_of(block) for block in blocks])
    peak = (jnp.maximum(peak, SMALLEST) * 1.02).astype(jnp.bfloat16).astype(jnp.float32)
    peak = jnp.broadcast_to(peak, (1, HALF))
    factor = row_factor(rows)
    for number, block in enumerate(blocks):
        for half in range(rows // HALF):
            scaled = block[:, half * HALF : (half + 1) * HALF] * factor
            scaled = scaled * (column_factor(half) * (SPREAD / peak))
            start = (number * (rows // HALF) + half) * rows
            message_ref[start : start + rows, :] = code(scaled).astype(jnp.bfloat16)
    start = len(blocks) * (rows // HALF) * rows
    if diagonal is not None:
        write_diagonal(message_ref, start, diagonal, peak)
        start += rows // HALF * TAIL
    message_ref[start : start + TAIL, :] = jnp.broadcast_to(peak, (TAIL, HALF)).astype(jnp.bfloat16)


def place_in_block(rows):
    row = lax.broadcasted_iota(jnp.int32, (rows, rows), 0)
    return row, lax.broadcasted_iota(jnp.int32, (rows, rows), 1)


def write_diagonal(message_ref, start, block, peak):
    rows = block.shape[0]
    row, column = place_in_block(rows)
    line = jnp.sum(jnp.where(row == column, block, 0.0), axis=0, keepdims=True)
    for half in range(rows // HALF):
        scaled = line[:, half * HALF : (half + 1) * HALF] * (column_factor(half) * (SPREAD / peak))
        coded = jnp.broadcast_to(code(scaled), (TAIL, HALF))
        message_ref[start + half * TAIL : start + (half + 1) * TAIL, :] = coded.astype(jnp.bfloat16)


def read_packed(message_ref, number, rows):
    packed = read_block(message_ref, number, rows)
    peak = message_ref[message_ref.shape[0] - TAIL :, :].astype(jnp.float32)[0:1]
    start = message_ref.shape[0] - TAIL - rows // HALF * TAIL
    line = []
    for half in range(rows // HALF):
        coded = message_ref[start + half * TAIL : start + (half + 1) * TAIL, :].astype(jnp.float32)
        line.append(decoded(coded[0:1]) * (peak * (1.0 / SPREAD) / column_factor(half)))
    line = jnp.broadcast_to(jnp.concatenate(line, axis=1), (rows, rows))
    row, column = place_in_block(rows)
    return jnp.where(row < column, packed, jnp.where(row == column, line, packed.T))


def read_block(message_ref, number, rows):
    peak = message_ref[message_ref.shape[0] - TAIL :, :].astype(jnp.float32)[0:1]
    factor = 1.0 / row_factor(rows)
    halves = []
    for half in range(rows // HALF):
        start = (number * (rows // HALF) + half) * rows
        coded = message_ref[start : start + rows, :].astype(jnp.float32)
        factors = peak * (1.0 / SPREAD) / column_factor(half)
        halves.append(decoded(coded) * factor * factors)
    return jnp.concatenate(halves, axis=1)


def message_shape(count, rows, diagonals=0):
    tails = TAIL + diagonals * rows // HALF * TAIL
    return jax.ShapeDtypeStruct((count * rows * rows // HALF + tails, HALF), jnp.bfloat16)


def columns_of(value, upper_value, rows, index):
    return jnp.where(
        upper_value,
        value[:, (3 - index) * rows : (4 - index) * rows],
        value[:, index * rows : (index + 1) * rows],
    )


def send_kernel(parts, inverse, left_ref, *refs):
    *right_refs, message_ref = refs
    rows = left_ref.shape[1] // 4
    upper, inner = fold()

    @pl.when(jnp.logical_not(inner))
    def _():
        write_message(
            message_ref,
            [
                product(inverse, left_ref, right_refs[which], upper, row, column, rows)
                for which, row, count in parts
                for column in range(count)
            ],
        )


def rest_kernel(inverse, left_ref, right_ref, message_ref):
    rows = left_ref.shape[1] // 4
    upper, inner = fold()

    @pl.when(jnp.logical_not(inner))
    def _():
        def own(row, column):
            return product(inverse, left_ref, right_ref, upper, row, column, rows)

        row, column = place_in_block(rows)
        near = own(NEAR, NEAR)
        packed = jnp.where(row >= column, own(NEXT, NEXT), near)
        write_message(message_ref, [own(NEXT, 0), own(NEXT, 1), packed, own(NEAR, 0)], near)


def copy_block(turned_ref, message_ref, number, rows):
    size = rows * rows // HALF
    turned_ref[0:size, :] = message_ref[number * size : (number + 1) * size, :]
    turned_ref[size : size + TAIL, :] = message_ref[message_ref.shape[0] - TAIL :, :]


def cross_kernel(row, columns, inverse, left_ref, right_ref, in_ref, message_ref):
    rows = left_ref.shape[1] // 4
    upper, inner = fold()

    @pl.when(inner)
    def _():
        write_message(
            message_ref,
            [
                product(inverse, left_ref, right_ref, upper, row, column, rows)
                + read_block(in_ref, column, rows)
                for column in columns
            ],
        )


def back_kernel(columns, inverse, left_ref, right_ref, across_ref, *refs):
    message_ref = refs[0] if len(refs) == 1 else refs[2]
    rows = left_ref.shape[1] // 4
    size = rows * rows // HALF + TAIL
    upper, inner = fold()

    @pl.when(inner)
    def _():
        write_message(
            message_ref,
            [
                product(inverse, left_ref, right_ref, upper, 0, 3 - column, rows)
                + read_block(across_ref, number, rows)
                for number, column in enumerate(columns)
            ],
        )
        if len(refs) > 1:
            far_ref, next_ref, _, turned_ref = refs
            copy_block(turned_ref.at[pl.ds(0, size)], far_ref, 1, rows)
            copy_block(turned_ref.at[pl.ds(size, size)], next_ref, 1, rows)
            copy_block(turned_ref.at[pl.ds(2 * size, size)], across_ref, columns.index(2), rows)


def put(out_ref, upper, column, rows, value):
    at = pl.ds(pl.multiple_of(block_at(upper, column) * rows, rows), rows)
    out_ref[0, 0, :, at] = value


def finish_kernel(near_at, turned_at, packs, backs, inverse, left_ref, right_ref, next_ref, near_ref, *refs):
    *refs, token_ref, out_ref = refs
    back_refs, turned_refs = refs[: len(backs)], refs[len(backs) :]
    token_ref[...] = jnp.zeros_like(token_ref)
    folds = len(turned_at) > 0
    rows = left_ref.shape[1] // 4
    upper, inner = fold()

    @pl.when(jnp.logical_not(inner))
    def _():
        for back_ref, columns in zip(back_refs, backs):
            for number, column in enumerate(columns):
                own = product(inverse, left_ref, right_ref, upper, 0, 3 - column, rows)
                put(out_ref, upper, 3 - column, rows, own + read_block(back_ref, number, rows))

    def turned_block(number):
        if len(turned_refs) == 1:
            size = rows * rows // HALF + TAIL
            return read_block(turned_refs[0].at[pl.ds(number * size, size)], 0, rows).T
        return read_block(turned_refs[number], turned_at[number], rows).T

    @pl.when(inner)
    def _():
        for column in range(4):
            own = product(inverse, left_ref, right_ref, upper, 1, column, rows)
            if folds and column >= 2:
                own = own + turned_block(3 - column)
            elif packs and column == 1:
                own = own + read_packed(near_ref, 2, rows)
            else:
                own = own + read_block(near_ref, near_at + column, rows)
            if folds and column == 0:
                own = own + turned_block(2)
            elif packs and column == 1:
                across = read_block(next_ref, 2, rows)
                row, place = place_in_block(rows)
                own = own + jnp.where(row >= place, across, across.T)
            else:
                own = own + read_block(next_ref, 3 - column, rows)
            put(out_ref, upper, column, rows, own)


def ordered(body, count, held, *refs):
    body(*refs[:count], *refs[count + held :])


def call(body, operands, held, cost, out_shape, **options):
    specs = [pl.BlockSpec(memory_space=pltpu.VMEM)] * len(operands)
    specs += [pl.BlockSpec(memory_space=pl.ANY)] * len(held)
    return pl.pallas_call(
        functools.partial(ordered, body, len(operands), len(held)),
        out_shape=out_shape,
        in_specs=specs,
        compiler_params=pltpu.CompilerParams(vmem_limit_bytes=VMEM_BYTES),
        cost_estimate=pl.CostEstimate(flops=cost, bytes_accessed=cost // 1000, transcendentals=0),
        **options,
    )(*operands, *held)


def folded_line(own_keys, inverse):
    width = own_keys.shape[1]
    rows = width // 4
    last, calls = [own_keys], []

    def run(body, operands, shapes, held=(), **options):
        held = (*held, last[0])
        cost = int(COSTS[len(calls)])
        calls.append(cost)
        result = call(functools.partial(body, inverse), operands, held, cost, shapes, **options)
        last[0] = jax.tree.leaves(result)[0]
        return result

    def send(rights, *parts):
        count = sum(part[-1] for part in parts)
        operands = (own_keys, *rights)
        message = run(functools.partial(send_kernel, parts), operands, message_shape(count, rows))
        return lax.ppermute(message, "tok", OUTER_TO_INNER)

    def cross(right, row, columns, arrived, held=()):
        body = functools.partial(cross_kernel, row, columns)
        message = run(body, (own_keys, right, arrived), message_shape(len(columns), rows), held)
        return lax.ppermute(message, "tok", ACROSS_MIDDLE)

    def back(right, columns, crossed, *arrived, held=()):
        body = functools.partial(back_kernel, columns)
        shapes = [message_shape(len(columns), rows)]
        if arrived:
            block = message_shape(1, rows)
            shapes.append(jax.ShapeDtypeStruct((3 * block.shape[0], HALF), block.dtype))
        message, *turned = run(body, (own_keys, right, crossed, *arrived), shapes, held)
        half_turn = [(source, (source + 2) % 4) for source in range(4)]
        turned = [lax.ppermute(part, "layer", half_turn) for part in turned]
        return lax.ppermute(message, "tok", INNER_TO_OUTER), *turned

    tile = jax.ShapeDtypeStruct((1, 3, rows, width), jnp.float32)
    token = jax.ShapeDtypeStruct((TAIL, HALF), jnp.bfloat16)

    def tile_specs(distance):
        return [
            pl.BlockSpec((TAIL, HALF), lambda step: (0, 0)),
            pl.BlockSpec((1, 1, rows, width), lambda step: (0, distance, 0, 0)),
        ]

    def finish(out, distance, right, next_across, backs, near, turned=(), near_at=0, turned_at=(), packs=False):
        operands = (own_keys, right, next_across, near, *backs.values(), *turned)
        options = {}
        if out is not None:
            options = {"held": (out,), "input_output_aliases": {len(operands): 1}}
        body = functools.partial(finish_kernel, near_at, turned_at, packs, tuple(backs))
        _, out = run(body, operands, [token, tile], grid=(1,), out_specs=tile_specs(distance), **options)
        return out

    every, upper_half, lower_half = (0, 1, 2, 3), (2, 3), (0, 1)
    second_keys = shifted(own_keys, "layer", -1)
    third_keys = shifted(second_keys, "layer", -1)
    far_0 = send((own_keys,), (0, FAR, 4))
    rest_0 = run(rest_kernel, (own_keys, own_keys), message_shape(4, rows, 1))
    rest_0 = lax.ppermute(rest_0, "tok", OUTER_TO_INNER)
    far_across_0 = cross(own_keys, FAR, every, far_0)
    far_1 = send((second_keys,), (0, FAR, 4))
    next_across_0 = cross(own_keys, NEXT, (0, 1, 2), rest_0)
    (back_0,) = back(own_keys, every, far_across_0)
    next_1 = send((second_keys,), (0, NEXT, 4))
    far_across_1 = cross(second_keys, FAR, every, far_1)
    far_2 = send((third_keys,), (0, FAR, 4))
    turned = (far_0, rest_0, far_across_0)
    out = finish(None, 0, own_keys, next_across_0, {every: back_0}, rest_0, turned, 3, (1, 1, 2), True)
    next_across_1 = cross(second_keys, NEXT, every, next_1)
    next_2 = send((third_keys,), (0, NEXT, 3))
    (back_1,) = back(second_keys, every, far_across_1)
    near = send((second_keys, third_keys), (0, NEAR, 4), (1, NEAR, 2))
    far_across_2 = cross(third_keys, FAR, upper_half, far_2)
    far_across_3 = cross(third_keys, FAR, lower_half, far_2, (next_across_1,))
    back_2, turned = back(third_keys, upper_half, far_across_2, far_2, next_2, held=(back_1,))
    next_across_2 = cross(third_keys, NEXT, (0, 1, 2), next_2)
    (back_3,) = back(third_keys, lower_half, far_across_3)
    backs = {upper_half: back_2, lower_half: back_3}
    out = finish(out, 1, second_keys, next_across_1, {every: back_1}, near)
    return finish(out, 2, third_keys, next_across_2, backs, near, (turned,), 4, (0, 0, 0))


def per_device(keys):
    own_keys = keys[0]
    layers = lax.axis_size("layer")
    half_span = layers // 2
    inverse = 1.0 / (own_keys.shape[0] * lax.axis_size("tok"))
    if lax.axis_size("tok") == 4 and layers == 4 and own_keys.shape[1] % (8 * HALF) == 0:
        return folded_line(own_keys, inverse)
    forward_list = [own_keys]
    for repeat in range(half_span):
        forward_list.append(shifted(forward_list[-1], "layer", -1))
    return reduce_scattered(own_keys, forward_list, inverse)


def solution(mesh):
    in_specs = (P("layer", ("groups", "tok"), None),)
    out_specs = P("layer", None, ("groups", "tok"), None)
    return jax.shard_map(
        per_device, mesh=mesh, in_specs=in_specs, out_specs=out_specs, check_vma=False
    )
```

time: 108 us -> 100 us (0.926)
  waiting for transfers between devices: 57.2 us -> 43.6 us
  starting transfers between devices: 33 us -> 38.5 us
    ppermute x13, waiting for transfers between devices: 17.1 us -> 6.84 us  [the longest x4 6.82 us: back(): return (lax.ppermute(message, 'tok', INNER_TO_OUTER), *turned)]
    ppermute x6, starting transfers between devices: 15.3 us -> 22.5 us  [send(): return lax.ppermute(message, 'tok', OUTER_TO_INNER)]
    ppermute x6, waiting for transfers between devices: 25.2 us -> 23.3 us  [send(): return lax.ppermute(message, 'tok', OUTER_TO_INNER)]
    ppermute x13, starting transfers between devices: 13.5 us -> 11.8 us  [the longest x4 5.15 us: back(): return (lax.ppermute(message, 'tok', INNER_TO_OUTER), *turned)]
    ppermute x2, waiting for transfers between devices: 14.9 us -> 13.4 us  [shifted(): return lax.ppermute(value, axis, pairs)]
    pallas_call x19 -> x21, Pallas kernels: 15.7 us -> 15.6 us  [call(): pl.pallas_call(functools.partial(ordered, body, len(operands), len(held))...]
where the time goes in v2:
time: 100 us; the launch traced here: 99.6 us
  waiting for transfers between devices  43.6 us (44%)
  starting transfers between devices  38.5 us (38%)
  Pallas kernels  15.6 us (16%)
  local copies, waits for them, and re-layouts  1.62 us (2%)
    ppermute x6, waiting for transfers between devices, send(): return lax.ppermute(message, 'tok', OUTER_TO_INNER)  23.3 us
    ppermute x6, starting transfers between devices, send(): return lax.ppermute(message, 'tok', OUTER_TO_INNER)  22.5 us
    pallas_call x21, Pallas kernels, call(): pl.pallas_call(functools.partial(ordered, body, len(operands), len(held))...  15.6 us
    ppermute x2, waiting for transfers between devices, shifted(): return lax.ppermute(value, axis, pairs)  13.4 us
    ppermute x4, waiting for transfers between devices, back(): return (lax.ppermute(message, 'tok', INNER_TO_OUTER), *turned)  6.82 us
    ppermute x4, starting transfers between devices, back(): return (lax.ppermute(message, 'tok', INNER_TO_OUTER), *turned)  5.15 us
    ppermute x7, starting transfers between devices, cross(): return lax.ppermute(message, 'tok', ACROSS_MIDDLE)  4.78 us
    ppermute x2, starting transfers between devices, shifted(): return lax.ppermute(value, axis, pairs)  4.18 us
  transfers between devices with their start and end apart: 21, of which 8 were waited for; matrix products, arithmetic and copies ran while one was open for 0% of the time, Pallas kernels for 13%

profile of v2, /device:TPU:0, one launch (start us, length us, event | category | flops | bytes accessed | tf_op | source)
XLA Modules:
  0.0 99.6 jit_solution(576965367385802539)
XLA Ops:
  0.0 2.4 %collective-permute-start = (bf16[1024,1024]{1,0:T(8,128)(2,1)}, bf16[1024,1024]{1,0:T(8,128)(2,1)S(1)}, u32[]{:S(2)}, u32[]{:S(2)}) collective-permute-start(bf16[1024,1024]{1,0:T(8,128)(2,1)} %bitcast.1), channel_id=1, source_target_pairs={{0,12},{4,0},{8,4},{12,8},{1,13},{5,1},{9,5},{13,9},{2,14},{6,2},{... | collective-permute-start | bytes 6291464 | tf_op jit(solution)/shard_map/ppermute | solution.py:26
  2.4 1.6 %copy-done = bf16[1,1024,1024]{2,1,0:T(8,128)(2,1)S(1)} copy-done((bf16[1,1024,1024]{2,1,0:T(8,128)(2,1)S(1)}, bf16[1,1024,1024]{2,1,0:T(8,128)(2,1)}, u32[]{:S(2)}) %copy-start) | copy-done | bytes 2097176
  4.0 1.2 %shard_map.17.refs_2_ = bf16[2064,128]{1,0:T(8,128)(2,1)S(1)} custom-call(bf16[1024,1024]{1,0:T(8,128)(2,1)S(1)} %bitcast.2, bf16[1024,1024]{1,0:T(8,128)(2,1)S(1)} %bitcast.3, bf16[1024,1024]{1,0:T(8,128)(2,1)S(1)} %bitcast.4), custom_call_target="tpu_custom_call" | custom-call | flops 3000000000 | bytes 3000000 | tf_op jit(solution)/shard_map/pallas_call | solution.py:296
  5.2 2.3 %collective-permute-start.2 = (bf16[2064,128]{1,0:T(8,128)(2,1)S(1)}, bf16[2064,128]{1,0:T(8,128)(2,1)S(1)}, u32[]{:S(2)}, u32[]{:S(2)}) collective-permute-start(bf16[2064,128]{1,0:T(8,128)(2,1)S(1)} %shard_map.17.refs_2_), channel_id=1, source_target_pairs={{0,1},{3,2},{4,5},{7,6},{8,9},{11,10},{12,13},{15,14},{16,17},{19,... | collective-permute-start | bytes 1585160 | tf_op jit(solution)/shard_map/ppermute | solution.py:323
  7.5 1.4 %shard_map.18.refs_3_ = bf16[2096,128]{1,0:T(8,128)(2,1)S(1)} custom-call(bf16[1024,1024]{1,0:T(8,128)(2,1)S(1)} %bitcast.5, bf16[1024,1024]{1,0:T(8,128)(2,1)S(1)} %bitcast.6, bf16[2064,128]{1,0:T(8,128)(2,1)S(1)} %shard_map.17.refs_2_), custom_call_target="tpu_custom_call" | custom-call | flops 3000000000 | bytes 3000000 | tf_op jit(solution)/shard_map/pallas_call | solution.py:296
  8.9 1.3 %collective-permute-start.4 = (bf16[2096,128]{1,0:T(8,128)(2,1)S(1)}, bf16[2096,128]{1,0:T(8,128)(2,1)S(1)}, u32[]{:S(2)}, u32[]{:S(2)}) collective-permute-start(bf16[2096,128]{1,0:T(8,128)(2,1)S(1)} %shard_map.18.refs_3_), channel_id=1, source_target_pairs={{0,1},{3,2},{4,5},{7,6},{8,9},{11,10},{12,13},{15,14},{16,17},{19,... | collective-permute-start | bytes 1609736 | tf_op jit(solution)/shard_map/ppermute | solution.py:364
  10.3 9.7 %collective-permute-done.2.refs_2_.refs_5_ = bf16[2064,128]{1,0:T(8,128)(2,1)S(1)} collective-permute-done((bf16[2064,128]{1,0:T(8,128)(2,1)S(1)}, bf16[2064,128]{1,0:T(8,128)(2,1)S(1)}, u32[]{:S(2)}, u32[]{:S(2)}) %collective-permute-start.2) | collective-permute-done | bytes 528416 | tf_op jit(solution)/shard_map/ppermute | solution.py:323
  20.6 5.6 %collective-permute-done.refs_1_ = bf16[1024,1024]{1,0:T(8,128)(2,1)S(1)} collective-permute-done((bf16[1024,1024]{1,0:T(8,128)(2,1)}, bf16[1024,1024]{1,0:T(8,128)(2,1)S(1)}, u32[]{:S(2)}, u32[]{:S(2)}) %collective-permute-start) | collective-permute-done | bytes 2097184 | tf_op jit(solution)/shard_map/ppermute | solution.py:26
  26.2 1.8 %collective-permute-start.1 = (bf16[1024,1024]{1,0:T(8,128)(2,1)S(1)}, bf16[1024,1024]{1,0:T(8,128)(2,1)S(1)}, u32[]{:S(2)}, u32[]{:S(2)}) collective-permute-start(bf16[1024,1024]{1,0:T(8,128)(2,1)S(1)} %collective-permute-done.refs_1_), channel_id=1, source_target_pairs={{0,12},{4,0},{8,4},{12,8},{1,13},{5,1},{9,5},{13,9},{2,14},{6,2},{... | collective-permute-start | bytes 6291464 | tf_op jit(solution)/shard_map/ppermute | solution.py:26
  28.0 1.2 %shard_map.20.refs_3_ = bf16[2064,128]{1,0:T(8,128)(2,1)S(1)} custom-call(bf16[1024,1024]{1,0:T(8,128)(2,1)S(1)} %bitcast.9, bf16[1024,1024]{1,0:T(8,128)(2,1)S(1)} %collective-permute-done.refs_1_, bf16[2064,128]{1,0:T(8,128)(2,1)S(1)} %shard_map.19.refs_2_), custom_call_target="tpu_custom_call" | custom-call | flops 30000001024 | bytes 30000000 | tf_op jit(solution)/shard_map/pallas_call | solution.py:296
  29.3 2.6 %collective-permute-start.8 = (bf16[2064,128]{1,0:T(8,128)(2,1)S(1)}, bf16[2064,128]{1,0:T(8,128)(2,1)S(1)}, u32[]{:S(2)}, u32[]{:S(2)}) collective-permute-start(bf16[2064,128]{1,0:T(8,128)(2,1)S(1)} %shard_map.20.refs_3_), channel_id=1, source_target_pairs={{0,1},{3,2},{4,5},{7,6},{8,9},{11,10},{12,13},{15,14},{16,17},{19,... | collective-permute-start | bytes 1585160 | tf_op jit(solution)/shard_map/ppermute | solution.py:323
  32.6 1.3 %collective-permute-start.7 = (bf16[2064,128]{1,0:T(8,128)(2,1)S(1)}, bf16[2064,128]{1,0:T(8,128)(2,1)S(1)}, u32[]{:S(2)}, u32[]{:S(2)}) collective-permute-start(bf16[2064,128]{1,0:T(8,128)(2,1)S(1)} %shard_map.22.refs_2_), channel_id=1, source_target_pairs={{1,0},{2,3},{5,4},{6,7},{9,8},{10,11},{13,12},{14,15},{17,16},{18,... | collective-permute-start | bytes 1585160 | tf_op jit(solution)/shard_map/ppermute | solution.py:339
  33.9 1.2 %shard_map.23.refs_3_ = bf16[2064,128]{1,0:T(8,128)(2,1)S(1)} custom-call(bf16[1024,1024]{1,0:T(8,128)(2,1)S(1)} %bitcast.14, bf16[1024,1024]{1,0:T(8,128)(2,1)S(1)} %collective-permute-done.refs_1_, bf16[2064,128]{1,0:T(8,128)(2,1)S(1)} %shard_map.22.refs_2_), custom_call_target="tpu_custom_call" | custom-call | flops 4000000000 | bytes 4000000 | tf_op jit(solution)/shard_map/pallas_call | solution.py:296
  35.2 7.3 %collective-permute-start.5 = (bf16[2064,128]{1,0:T(8,128)(2,1)S(1)}, bf16[2064,128]{1,0:T(8,128)(2,1)S(1)}, u32[]{:S(2)}, u32[]{:S(2)}) collective-permute-start(bf16[2064,128]{1,0:T(8,128)(2,1)S(1)} %shard_map.23.refs_3_), channel_id=1, source_target_pairs={{0,1},{3,2},{4,5},{7,6},{8,9},{11,10},{12,13},{15,14},{16,17},{19,... | collective-permute-start | bytes 1585160 | tf_op jit(solution)/shard_map/ppermute | solution.py:323
  42.4 0.7 collective-permute-done.8.refs_2_
  43.8 7.8 %collective-permute-done.1.refs_1_.refs_2_ = bf16[1024,1024]{1,0:T(8,128)(2,1)S(1)} collective-permute-done((bf16[1024,1024]{1,0:T(8,128)(2,1)S(1)}, bf16[1024,1024]{1,0:T(8,128)(2,1)S(1)}, u32[]{:S(2)}, u32[]{:S(2)}) %collective-permute-start.1) | collective-permute-done | bytes 2097184 | tf_op jit(solution)/shard_map/ppermute | solution.py:26
  51.6 1.2 %shard_map.25.refs_8_ = bf16[2064,128]{1,0:T(8,128)(2,1)S(1)} custom-call(bf16[1024,1024]{1,0:T(8,128)(2,1)S(1)} %bitcast.16, bf16[1024,1024]{1,0:T(8,128)(2,1)S(1)} %collective-permute-done.1.refs_1_.refs_2_, bf16[2064,128]{1,0:T(8,128)(2,1)S(1)} %shard_map.24.refs_2_), custom_call_target="tpu_custom_call" | custom-call | flops 4000000000 | bytes 4000000 | tf_op jit(solution)/shard_map/pallas_call | solution.py:296
  52.8 2.6 %collective-permute-start.10 = (bf16[2064,128]{1,0:T(8,128)(2,1)S(1)}, bf16[2064,128]{1,0:T(8,128)(2,1)S(1)}, u32[]{:S(2)}, u32[]{:S(2)}) collective-permute-start(bf16[2064,128]{1,0:T(8,128)(2,1)S(1)} %shard_map.25.refs_8_), channel_id=1, source_target_pairs={{0,1},{3,2},{4,5},{7,6},{8,9},{11,10},{12,13},{15,14},{16,17},{19,... | collective-permute-start | bytes 1585160 | tf_op jit(solution)/shard_map/ppermute | solution.py:323
  55.4 2.1 %shard_map.26 = (bf16[16,128]{1,0:T(8,128)(2,1)S(1)}, f32[1,3,256,1024]{3,2,1,0:T(8,128)}) custom-call(bf16[1024,1024]{1,0:T(8,128)(2,1)S(1)} %bitcast.17, bf16[1024,1024]{1,0:T(8,128)(2,1)S(1)} %bitcast.18, bf16[1552,128]{1,0:T(8,128)(2,1)S(1)} %collective-permute-done.6.refs_2_, bf16[2096,128]{1,0:T(8,128)(2,1)S(1)} %collective-permute-done.4.refs_2_.refs_3_.refs_6_, ...), custom_call_target="tpu_custom_call" | custom-call | flops 4000000000 | bytes 4000000 | tf_op jit(solution)/shard_map/pallas_call | solution.py:296
  58.3 1.0 %shard_map.28.refs_3_ = bf16[1552,128]{1,0:T(8,128)(2,1)S(1)} custom-call(bf16[1024,1024]{1,0:T(8,128)(2,1)S(1)} %bitcast.20, bf16[1024,1024]{1,0:T(8,128)(2,1)S(1)} %collective-permute-done.1.refs_1_.refs_2_, bf16[2064,128]{1,0:T(8,128)(2,1)S(1)} %shard_map.27.refs_2_), custom_call_target="tpu_custom_call" | custom-call | flops 4000000000 | bytes 4000000 | tf_op jit(solution)/shard_map/pallas_call | solution.py:296
  59.3 4.9 %collective-permute-start.9 = (bf16[1552,128]{1,0:T(8,128)(2,1)S(1)}, bf16[1552,128]{1,0:T(8,128)(2,1)S(1)}, u32[]{:S(2)}, u32[]{:S(2)}) collective-permute-start(bf16[1552,128]{1,0:T(8,128)(2,1)S(1)} %shard_map.28.refs_3_), channel_id=1, source_target_pairs={{0,1},{3,2},{4,5},{7,6},{8,9},{11,10},{12,13},{15,14},{16,17},{19,... | collective-permute-start | bytes 1191944 | tf_op jit(solution)/shard_map/ppermute | solution.py:323
  64.3 1.3 %collective-permute-start.13 = (bf16[2064,128]{1,0:T(8,128)(2,1)S(1)}, bf16[2064,128]{1,0:T(8,128)(2,1)S(1)}, u32[]{:S(2)}, u32[]{:S(2)}) collective-permute-start(bf16[2064,128]{1,0:T(8,128)(2,1)S(1)} %shard_map.29.refs_3_), channel_id=1, source_target_pairs={{1,0},{2,3},{5,4},{6,7},{9,8},{10,11},{13,12},{14,15},{17,16},{18,... | collective-permute-start | bytes 1585160 | tf_op jit(solution)/shard_map/ppermute | solution.py:339
  65.6 1.7 %shard_map.30.refs_3_ = bf16[3088,128]{1,0:T(8,128)(2,1)S(1)} custom-call(bf16[1024,1024]{1,0:T(8,128)(2,1)S(1)} %bitcast.22, bf16[1024,1024]{1,0:T(8,128)(2,1)S(1)} %collective-permute-done.refs_1_, bf16[1024,1024]{1,0:T(8,128)(2,1)S(1)} %collective-permute-done.1.refs_1_.refs_2_, bf16[2064,128]{1,0:T(8,128)(2,1)S(1)} %shard_map.29.refs_3_), custom_call_target="tpu_custom_call" | custom-call | flops 4000000000 | bytes 4000000 | tf_op jit(solution)/shard_map/pallas_call | solution.py:296
  67.3 2.9 %collective-permute-start.16 = (bf16[3088,128]{1,0:T(8,128)(2,1)S(1)}, bf16[3088,128]{1,0:T(8,128)(2,1)S(1)}, u32[]{:S(2)}, u32[]{:S(2)}) collective-permute-start(bf16[3088,128]{1,0:T(8,128)(2,1)S(1)} %shard_map.30.refs_3_), channel_id=1, source_target_pairs={{0,1},{3,2},{4,5},{7,6},{8,9},{11,10},{12,13},{15,14},{16,17},{19,... | collective-permute-start | bytes 2371592 | tf_op jit(solution)/shard_map/ppermute | solution.py:323
  71.7 4.4 %collective-permute-done.9.refs_4_.refs_2_ = bf16[1552,128]{1,0:T(8,128)(2,1)S(1)} collective-permute-done((bf16[1552,128]{1,0:T(8,128)(2,1)S(1)}, bf16[1552,128]{1,0:T(8,128)(2,1)S(1)}, u32[]{:S(2)}, u32[]{:S(2)}) %collective-permute-start.9) | collective-permute-done | bytes 397344 | tf_op jit(solution)/shard_map/ppermute | solution.py:323
  76.1 4.5 %collective-permute-done.13.refs_5_.refs_4_ = bf16[2064,128]{1,0:T(8,128)(2,1)S(1)} collective-permute-done((bf16[2064,128]{1,0:T(8,128)(2,1)S(1)}, bf16[2064,128]{1,0:T(8,128)(2,1)S(1)}, u32[]{:S(2)}, u32[]{:S(2)}) %collective-permute-start.13) | collective-permute-done | bytes 528416 | tf_op jit(solution)/shard_map/ppermute | solution.py:339
  80.7 1.3 %collective-permute-start.17 = (bf16[1040,128]{1,0:T(8,128)(2,1)S(1)}, bf16[1040,128]{1,0:T(8,128)(2,1)S(1)}, u32[]{:S(2)}, u32[]{:S(2)}) collective-permute-start(bf16[1040,128]{1,0:T(8,128)(2,1)S(1)} %get-tuple-element.13.refs_3_), channel_id=1, source_target_pairs={{1,0},{2,3},{5,4},{6,7},{9,8},{10,11},{13,12},{14,15},{17,16},{18,... | collective-permute-start | bytes 798728 | tf_op jit(solution)/shard_map/ppermute | solution.py:339
  83.3 1.3 %collective-permute-start.19 = (bf16[1040,128]{1,0:T(8,128)(2,1)S(1)}, bf16[1040,128]{1,0:T(8,128)(2,1)S(1)}, u32[]{:S(2)}, u32[]{:S(2)}) collective-permute-start(bf16[1040,128]{1,0:T(8,128)(2,1)S(1)} %shard_map.35.refs_6_), channel_id=1, source_target_pairs={{1,0},{2,3},{5,4},{6,7},{9,8},{10,11},{13,12},{14,15},{17,16},{18,... | collective-permute-start | bytes 798728 | tf_op jit(solution)/shard_map/ppermute | solution.py:339
  84.5 8.5 %collective-permute-done.16.refs_3_ = bf16[3088,128]{1,0:T(8,128)(2,1)S(1)} collective-permute-done((bf16[3088,128]{1,0:T(8,128)(2,1)S(1)}, bf16[3088,128]{1,0:T(8,128)(2,1)S(1)}, u32[]{:S(2)}, u32[]{:S(2)}) %collective-permute-start.16) | collective-permute-done | bytes 790560 | tf_op jit(solution)/shard_map/ppermute | solution.py:323
  93.1 2.1 %shard_map.36 = (bf16[16,128]{1,0:T(8,128)(2,1)S(1)}, f32[1,3,256,1024]{3,2,1,0:T(8,128)}) custom-call(bf16[1024,1024]{1,0:T(8,128)(2,1)S(1)} %bitcast.28, bf16[1024,1024]{1,0:T(8,128)(2,1)S(1)} %collective-permute-done.refs_1_, bf16[2064,128]{1,0:T(8,128)(2,1)S(1)} %collective-permute-done.14.refs_3_.refs_2_, ...), custom_call_target="tpu_custom_call", output_to_operand_aliasing={{1}: (5, {})} | custom-call | flops 4000000000 | bytes 4000000 | tf_op jit(solution)/shard_map/pallas_call | solution.py:296
  95.2 2.3 %collective-permute-done.19.refs_5_ = bf16[1040,128]{1,0:T(8,128)(2,1)S(1)} collective-permute-done((bf16[1040,128]{1,0:T(8,128)(2,1)S(1)}, bf16[1040,128]{1,0:T(8,128)(2,1)S(1)}, u32[]{:S(2)}, u32[]{:S(2)}) %collective-permute-start.19) | collective-permute-done | bytes 266272 | tf_op jit(solution)/shard_map/ppermute | solution.py:339
  97.5 2.2 %shard_map.37 = (bf16[16,128]{1,0:T(8,128)(2,1)}, f32[1,3,256,1024]{3,2,1,0:T(8,128)}) custom-call(bf16[1024,1024]{1,0:T(8,128)(2,1)S(1)} %bitcast.29, bf16[1024,1024]{1,0:T(8,128)(2,1)S(1)} %collective-permute-done.1.refs_1_.refs_2_, bf16[1552,128]{1,0:T(8,128)(2,1)S(1)} %collective-permute-done.15.refs_2_, ...), custom_call_target="tpu_custom_call", output_to_operand_aliasing={{1}: (7, {})} | custom-call | flops 4000000000 | bytes 4000000 | tf_op jit(solution)/shard_map/pallas_call | solution.py:296
  (33 shorter events, 5.5 us)
Async XLA Ops:
  0.0 26.2 %collective-permute-start = (bf16[1024,1024]{1,0:T(8,128)(2,1)}, bf16[1024,1024]{1,0:T(8,128)(2,1)S(1)}, u32[]{:S(2)}, u32[]{:S(2)}) collective-permute-start(bf16[1024,1024]{1,0:T(8,128)(2,1)} %bitcast.1), channel_id=1, source_target_pairs={{0,12},{4,0},{8,4},{12,8},{1,13},{5,1},{9,5},{13,9},{2,14},{6,2},{... | collective-permute-start | bytes 6291464 | tf_op jit(solution)/shard_map/ppermute | solution.py:26
  2.4 1.6 %copy-start = (bf16[1,1024,1024]{2,1,0:T(8,128)(2,1)S(1)}, bf16[1,1024,1024]{2,1,0:T(8,128)(2,1)}, u32[]{:S(2)}) copy-start(bf16[1,1024,1024]{2,1,0:T(8,128)(2,1)} %param.1) | copy-start | bytes 6291460
  5.2 14.7 %collective-permute-start.2 = (bf16[2064,128]{1,0:T(8,128)(2,1)S(1)}, bf16[2064,128]{1,0:T(8,128)(2,1)S(1)}, u32[]{:S(2)}, u32[]{:S(2)}) collective-permute-start(bf16[2064,128]{1,0:T(8,128)(2,1)S(1)} %shard_map.17.refs_2_), channel_id=1, source_target_pairs={{0,1},{3,2},{4,5},{7,6},{8,9},{11,10},{12,13},{15,14},{16,17},{19,... | collective-permute-start | bytes 1585160 | tf_op jit(solution)/shard_map/ppermute | solution.py:323
  8.9 22.9 %collective-permute-start.4 = (bf16[2096,128]{1,0:T(8,128)(2,1)S(1)}, bf16[2096,128]{1,0:T(8,128)(2,1)S(1)}, u32[]{:S(2)}, u32[]{:S(2)}) collective-permute-start(bf16[2096,128]{1,0:T(8,128)(2,1)S(1)} %shard_map.18.refs_3_), channel_id=1, source_target_pairs={{0,1},{3,2},{4,5},{7,6},{8,9},{11,10},{12,13},{15,14},{16,17},{19,... | collective-permute-start | bytes 1609736 | tf_op jit(solution)/shard_map/ppermute | solution.py:364
  19.9 12.7 %collective-permute-start.3 = (bf16[2064,128]{1,0:T(8,128)(2,1)S(1)}, bf16[2064,128]{1,0:T(8,128)(2,1)S(1)}, u32[]{:S(2)}, u32[]{:S(2)}) collective-permute-start(bf16[2064,128]{1,0:T(8,128)(2,1)S(1)} %shard_map.19.refs_2_), channel_id=1, source_target_pairs={{1,2},{2,1},{5,6},{6,5},{9,10},{10,9},{13,14},{14,13},{17,18},{18,... | collective-permute-start | bytes 1585160 | tf_op jit(solution)/shard_map/ppermute | solution.py:328
  26.2 25.4 %collective-permute-start.1 = (bf16[1024,1024]{1,0:T(8,128)(2,1)S(1)}, bf16[1024,1024]{1,0:T(8,128)(2,1)S(1)}, u32[]{:S(2)}, u32[]{:S(2)}) collective-permute-start(bf16[1024,1024]{1,0:T(8,128)(2,1)S(1)} %collective-permute-done.refs_1_), channel_id=1, source_target_pairs={{0,12},{4,0},{8,4},{12,8},{1,13},{5,1},{9,5},{13,9},{2,14},{6,2},{... | collective-permute-start | bytes 6291464 | tf_op jit(solution)/shard_map/ppermute | solution.py:26
  29.3 13.8 %collective-permute-start.8 = (bf16[2064,128]{1,0:T(8,128)(2,1)S(1)}, bf16[2064,128]{1,0:T(8,128)(2,1)S(1)}, u32[]{:S(2)}, u32[]{:S(2)}) collective-permute-start(bf16[2064,128]{1,0:T(8,128)(2,1)S(1)} %shard_map.20.refs_3_), channel_id=1, source_target_pairs={{0,1},{3,2},{4,5},{7,6},{8,9},{11,10},{12,13},{15,14},{16,17},{19,... | collective-permute-start | bytes 1585160 | tf_op jit(solution)/shard_map/ppermute | solution.py:323
  31.9 23.5 %collective-permute-start.6 = (bf16[1552,128]{1,0:T(8,128)(2,1)S(1)}, bf16[1552,128]{1,0:T(8,128)(2,1)S(1)}, u32[]{:S(2)}, u32[]{:S(2)}) collective-permute-start(bf16[1552,128]{1,0:T(8,128)(2,1)S(1)} %shard_map.21.refs_3_), channel_id=1, source_target_pairs={{1,2},{2,1},{5,6},{6,5},{9,10},{10,9},{13,14},{14,13},{17,18},{18,... | collective-permute-start | bytes 1191944 | tf_op jit(solution)/shard_map/ppermute | solution.py:328
  32.6 22.8 %collective-permute-start.7 = (bf16[2064,128]{1,0:T(8,128)(2,1)S(1)}, bf16[2064,128]{1,0:T(8,128)(2,1)S(1)}, u32[]{:S(2)}, u32[]{:S(2)}) collective-permute-start(bf16[2064,128]{1,0:T(8,128)(2,1)S(1)} %shard_map.22.refs_2_), channel_id=1, source_target_pairs={{1,0},{2,3},{5,4},{6,7},{9,8},{10,11},{13,12},{14,15},{17,16},{18,... | collective-permute-start | bytes 1585160 | tf_op jit(solution)/shard_map/ppermute | solution.py:339
  35.2 22.4 %collective-permute-start.5 = (bf16[2064,128]{1,0:T(8,128)(2,1)S(1)}, bf16[2064,128]{1,0:T(8,128)(2,1)S(1)}, u32[]{:S(2)}, u32[]{:S(2)}) collective-permute-start(bf16[2064,128]{1,0:T(8,128)(2,1)S(1)} %shard_map.23.refs_3_), channel_id=1, source_target_pairs={{0,1},{3,2},{4,5},{7,6},{8,9},{11,10},{12,13},{15,14},{16,17},{19,... | collective-permute-start | bytes 1585160 | tf_op jit(solution)/shard_map/ppermute | solution.py:323
  43.1 21.1 %collective-permute-start.11 = (bf16[2064,128]{1,0:T(8,128)(2,1)S(1)}, bf16[2064,128]{1,0:T(8,128)(2,1)S(1)}, u32[]{:S(2)}, u32[]{:S(2)}) collective-permute-start(bf16[2064,128]{1,0:T(8,128)(2,1)S(1)} %shard_map.24.refs_2_), channel_id=1, source_target_pairs={{1,2},{2,1},{5,6},{6,5},{9,10},{10,9},{13,14},{14,13},{17,18},{18,... | collective-permute-start | bytes 1585160 | tf_op jit(solution)/shard_map/ppermute | solution.py:328
  52.8 17.4 %collective-permute-start.10 = (bf16[2064,128]{1,0:T(8,128)(2,1)S(1)}, bf16[2064,128]{1,0:T(8,128)(2,1)S(1)}, u32[]{:S(2)}, u32[]{:S(2)}) collective-permute-start(bf16[2064,128]{1,0:T(8,128)(2,1)S(1)} %shard_map.25.refs_8_), channel_id=1, source_target_pairs={{0,1},{3,2},{4,5},{7,6},{8,9},{11,10},{12,13},{15,14},{16,17},{19,... | collective-permute-start | bytes 1585160 | tf_op jit(solution)/shard_map/ppermute | solution.py:323
  57.6 13.4 %collective-permute-start.14 = (bf16[2064,128]{1,0:T(8,128)(2,1)S(1)}, bf16[2064,128]{1,0:T(8,128)(2,1)S(1)}, u32[]{:S(2)}, u32[]{:S(2)}) collective-permute-start(bf16[2064,128]{1,0:T(8,128)(2,1)S(1)} %shard_map.27.refs_2_), channel_id=1, source_target_pairs={{1,2},{2,1},{5,6},{6,5},{9,10},{10,9},{13,14},{14,13},{17,18},{18,... | collective-permute-start | bytes 1585160 | tf_op jit(solution)/shard_map/ppermute | solution.py:328
  59.3 16.8 %collective-permute-start.9 = (bf16[1552,128]{1,0:T(8,128)(2,1)S(1)}, bf16[1552,128]{1,0:T(8,128)(2,1)S(1)}, u32[]{:S(2)}, u32[]{:S(2)}) collective-permute-start(bf16[1552,128]{1,0:T(8,128)(2,1)S(1)} %shard_map.28.refs_3_), channel_id=1, source_target_pairs={{0,1},{3,2},{4,5},{7,6},{8,9},{11,10},{12,13},{15,14},{16,17},{19,... | collective-permute-start | bytes 1191944 | tf_op jit(solution)/shard_map/ppermute | solution.py:323
  64.3 16.4 %collective-permute-start.13 = (bf16[2064,128]{1,0:T(8,128)(2,1)S(1)}, bf16[2064,128]{1,0:T(8,128)(2,1)S(1)}, u32[]{:S(2)}, u32[]{:S(2)}) collective-permute-start(bf16[2064,128]{1,0:T(8,128)(2,1)S(1)} %shard_map.29.refs_3_), channel_id=1, source_target_pairs={{1,0},{2,3},{5,4},{6,7},{9,8},{10,11},{13,12},{14,15},{17,16},{18,... | collective-permute-start | bytes 1585160 | tf_op jit(solution)/shard_map/ppermute | solution.py:339
  67.3 25.8 %collective-permute-start.16 = (bf16[3088,128]{1,0:T(8,128)(2,1)S(1)}, bf16[3088,128]{1,0:T(8,128)(2,1)S(1)}, u32[]{:S(2)}, u32[]{:S(2)}) collective-permute-start(bf16[3088,128]{1,0:T(8,128)(2,1)S(1)} %shard_map.30.refs_3_), channel_id=1, source_target_pairs={{0,1},{3,2},{4,5},{7,6},{8,9},{11,10},{12,13},{15,14},{16,17},{19,... | collective-permute-start | bytes 2371592 | tf_op jit(solution)/shard_map/ppermute | solution.py:323
  70.3 10.4 %collective-permute-start.12 = (bf16[1040,128]{1,0:T(8,128)(2,1)S(1)}, bf16[1040,128]{1,0:T(8,128)(2,1)S(1)}, u32[]{:S(2)}, u32[]{:S(2)}) collective-permute-start(bf16[1040,128]{1,0:T(8,128)(2,1)S(1)} %shard_map.31.refs_4_), channel_id=1, source_target_pairs={{1,2},{2,1},{5,6},{6,5},{9,10},{10,9},{13,14},{14,13},{17,18},{18,... | collective-permute-start | bytes 798728 | tf_op jit(solution)/shard_map/ppermute | solution.py:328
  71.0 12.3 %collective-permute-start.18 = (bf16[1040,128]{1,0:T(8,128)(2,1)S(1)}, bf16[1040,128]{1,0:T(8,128)(2,1)S(1)}, u32[]{:S(2)}, u32[]{:S(2)}) collective-permute-start(bf16[1040,128]{1,0:T(8,128)(2,1)S(1)} %shard_map.32.refs_6_), channel_id=1, source_target_pairs={{1,2},{2,1},{5,6},{6,5},{9,10},{10,9},{13,14},{14,13},{17,18},{18,... | collective-permute-start | bytes 798728 | tf_op jit(solution)/shard_map/ppermute | solution.py:328
  80.7 16.8 %collective-permute-start.17 = (bf16[1040,128]{1,0:T(8,128)(2,1)S(1)}, bf16[1040,128]{1,0:T(8,128)(2,1)S(1)}, u32[]{:S(2)}, u32[]{:S(2)}) collective-permute-start(bf16[1040,128]{1,0:T(8,128)(2,1)S(1)} %get-tuple-element.13.refs_3_), channel_id=1, source_target_pairs={{1,0},{2,3},{5,4},{6,7},{9,8},{10,11},{13,12},{14,15},{17,16},{18,... | collective-permute-start | bytes 798728 | tf_op jit(solution)/shard_map/ppermute | solution.py:339
  82.0 15.5 %collective-permute-start.15 = (bf16[1552,128]{1,0:T(8,128)(2,1)S(1)}, bf16[1552,128]{1,0:T(8,128)(2,1)S(1)}, u32[]{:S(2)}, u32[]{:S(2)}) collective-permute-start(bf16[1552,128]{1,0:T(8,128)(2,1)S(1)} %shard_map.34.refs_3_), channel_id=1, source_target_pairs={{1,2},{2,1},{5,6},{6,5},{9,10},{10,9},{13,14},{14,13},{17,18},{18,... | collective-permute-start | bytes 1191944 | tf_op jit(solution)/shard_map/ppermute | solution.py:328
  82.7 14.8 %collective-permute-start.20 = (bf16[1584,128]{1,0:T(8,128)(2,1)S(1)}, bf16[1584,128]{1,0:T(8,128)(2,1)S(1)}, u32[]{:S(2)}, u32[]{:S(2)}) collective-permute-start(bf16[1584,128]{1,0:T(8,128)(2,1)S(1)} %get-tuple-element.14), channel_id=1, source_target_pairs={{0,8},{4,12},{8,0},{12,4},{1,9},{5,13},{9,1},{13,5},{2,10},{6,14},... | collective-permute-start | bytes 1216520 | tf_op jit(solution)/shard_map/ppermute | solution.py:338
  83.3 14.2 %collective-permute-start.19 = (bf16[1040,128]{1,0:T(8,128)(2,1)S(1)}, bf16[1040,128]{1,0:T(8,128)(2,1)S(1)}, u32[]{:S(2)}, u32[]{:S(2)}) collective-permute-start(bf16[1040,128]{1,0:T(8,128)(2,1)S(1)} %shard_map.35.refs_6_), channel_id=1, source_target_pairs={{1,0},{2,3},{5,4},{6,7},{9,8},{10,11},{13,12},{14,15},{17,16},{18,... | collective-permute-start | bytes 798728 | tf_op jit(solution)/shard_map/ppermute | solution.py:339

commit v3 on v2

--- a/solution.py
+++ b/solution.py
@@ -16,7 +16,7 @@
 TAIL = 16
 SPREAD = 13777.0
 SMALLEST = 1e-30
-COSTS = tuple(1_000_000_000 * cost for cost in (3, 3, 3, 30, 4, 4, 4, 4, 4, 4, 4, 4, 4, 4, 4, 4, 4, 4, 4, 4, 4))
+COSTS = tuple(1_000_000_000 * cost for cost in (6, 6, 6, 6, 6, 6, 6, 6, 6, 6, 6, 6, 6, 6, 6, 6, 6, 6, 6))
 VMEM_BYTES = 24 * 1024 * 1024
 
 
@@ -54,12 +54,17 @@
     return jnp.where(upper, 3 - index, index)
 
 
+def block_of(ref, upper, index, rows):
+    count = ref.shape[1] // rows
+    if count == 1:
+        return ref[...]
+    at = jnp.where(upper, count - 1 - index, index)
+    return ref[:, pl.ds(pl.multiple_of(at * rows, rows), rows)]
+
+
 def product(inverse, left_ref, right_ref, upper, row, column, rows):
-    left = left_ref[:, pl.ds(pl.multiple_of(block_at(upper, row) * rows, rows), rows)]
-    if column is None:
-        return tile_rows(inverse, left, right_ref[...])
-    at = pl.ds(pl.multiple_of(block_at(upper, column) * rows, rows), rows)
-    return tile_rows(inverse, left, right_ref[:, at])
+    left = block_of(left_ref, upper, row, rows)
+    return tile_rows(inverse, left, block_of(right_ref, upper, column, rows))
 
 
 def row_factor(rows):
@@ -162,9 +167,8 @@
     )
 
 
-def send_kernel(parts, inverse, left_ref, *refs):
-    *right_refs, message_ref = refs
-    rows = left_ref.shape[1] // 4
+def send_kernel(row, count, inverse, left_ref, right_ref, message_ref):
+    rows = right_ref.shape[1] // 4
     upper, inner = fold()
 
     @pl.when(jnp.logical_not(inner))
@@ -172,8 +176,32 @@
         write_message(
             message_ref,
             [
-                product(inverse, left_ref, right_refs[which], upper, row, column, rows)
-                for which, row, count in parts
+                product(inverse, left_ref, right_ref, upper, row, column, rows)
+                for column in range(count)
+            ],
+        )
+
+
+def pass_on_kernel(row, count, inverse, left_ref, right_ref, message_ref, far_ref, rest_ref):
+    rows = right_ref.shape[1] // 4
+    upper, inner = fold()
+    far_ref[...] = block_of(right_ref, upper, FAR, rows)
+    rest_at = pl.multiple_of(jnp.where(upper, rows, 0), rows)
+    rest_ref[...] = right_ref[:, pl.ds(rest_at, 3 * rows)]
+    send_kernel(row, count, inverse, left_ref, right_ref, message_ref)
+
+
+def near_kernel(inverse, left_ref, plain_ref, folded_ref, message_ref):
+    rows = left_ref.shape[1] // 4
+    upper, inner = fold()
+
+    @pl.when(jnp.logical_not(inner))
+    def _():
+        write_message(
+            message_ref,
+            [
+                product(inverse, left_ref, right_ref, upper, NEAR, column, rows)
+                for right_ref, count in ((plain_ref, 4), (folded_ref, 2))
                 for column in range(count)
             ],
         )
@@ -194,14 +222,8 @@
         write_message(message_ref, [own(NEXT, 0), own(NEXT, 1), packed, own(NEAR, 0)], near)
 
 
-def copy_block(turned_ref, message_ref, number, rows):
-    size = rows * rows // HALF
-    turned_ref[0:size, :] = message_ref[number * size : (number + 1) * size, :]
-    turned_ref[size : size + TAIL, :] = message_ref[message_ref.shape[0] - TAIL :, :]
-
-
-def cross_kernel(row, columns, inverse, left_ref, right_ref, in_ref, message_ref):
-    rows = left_ref.shape[1] // 4
+def cross_kernel(row, count, inverse, left_ref, right_ref, in_ref, message_ref):
+    rows = right_ref.shape[1] // 4
     upper, inner = fold()
 
     @pl.when(inner)
@@ -211,15 +233,13 @@
             [
                 product(inverse, left_ref, right_ref, upper, row, column, rows)
                 + read_block(in_ref, column, rows)
-                for column in columns
+                for column in range(count)
             ],
         )
 
 
-def back_kernel(columns, inverse, left_ref, right_ref, across_ref, *refs):
-    message_ref = refs[0] if len(refs) == 1 else refs[2]
-    rows = left_ref.shape[1] // 4
-    size = rows * rows // HALF + TAIL
+def back_kernel(inverse, left_ref, right_ref, across_ref, message_ref):
+    rows = right_ref.shape[1] // 4
     upper, inner = fold()
 
     @pl.when(inner)
@@ -227,16 +247,11 @@
         write_message(
             message_ref,
             [
-                product(inverse, left_ref, right_ref, upper, 0, 3 - column, rows)
-                + read_block(across_ref, number, rows)
-                for number, column in enumerate(columns)
+                product(inverse, left_ref, right_ref, upper, 0, column, rows)
+                + read_block(across_ref, 3 - column, rows)
+                for column in range(4)
             ],
         )
-        if len(refs) > 1:
-            far_ref, next_ref, _, turned_ref = refs
-            copy_block(turned_ref.at[pl.ds(0, size)], far_ref, 1, rows)
-            copy_block(turned_ref.at[pl.ds(size, size)], next_ref, 1, rows)
-            copy_block(turned_ref.at[pl.ds(2 * size, size)], across_ref, columns.index(2), rows)
 
 
 def put(out_ref, upper, column, rows, value):
@@ -244,31 +259,29 @@
     out_ref[0, 0, :, at] = value
 
 
-def finish_kernel(near_at, turned_at, packs, backs, inverse, left_ref, right_ref, next_ref, near_ref, *refs):
-    *refs, token_ref, out_ref = refs
-    back_refs, turned_refs = refs[: len(backs)], refs[len(backs) :]
+def finish_kernel(near_at, folds, packs, rights, inverse, left_ref, *refs):
+    right_refs, (next_ref, near_ref, back_ref) = refs[:rights], refs[rights : rights + 3]
+    *turned_refs, token_ref, out_ref = refs[rights + 3 :]
     token_ref[...] = jnp.zeros_like(token_ref)
-    folds = len(turned_at) > 0
     rows = left_ref.shape[1] // 4
     upper, inner = fold()
 
+    def own_sums(row, column):
+        right_ref = right_refs[-1] if column == FAR else right_refs[0]
+        return product(inverse, left_ref, right_ref, upper, row, column, rows)
+
+    def turned_block(number):
+        return read_block(turned_refs[number], (1, 1, 2)[number], rows).T
+
     @pl.when(jnp.logical_not(inner))
     def _():
-        for back_ref, columns in zip(back_refs, backs):
-            for number, column in enumerate(columns):
-                own = product(inverse, left_ref, right_ref, upper, 0, 3 - column, rows)
-                put(out_ref, upper, 3 - column, rows, own + read_block(back_ref, number, rows))
-
-    def turned_block(number):
-        if len(turned_refs) == 1:
-            size = rows * rows // HALF + TAIL
-            return read_block(turned_refs[0].at[pl.ds(number * size, size)], 0, rows).T
-        return read_block(turned_refs[number], turned_at[number], rows).T
+        for column in range(4):
+            put(out_ref, upper, column, rows, own_sums(0, column) + read_block(back_ref, column, rows))
 
     @pl.when(inner)
     def _():
         for column in range(4):
-            own = product(inverse, left_ref, right_ref, upper, 1, column, rows)
+            own = own_sums(1, column)
             if folds and column >= 2:
                 own = own + turned_block(3 - column)
             elif packs and column == 1:
@@ -316,27 +329,27 @@
         last[0] = jax.tree.leaves(result)[0]
         return result
 
-    def send(rights, *parts):
-        count = sum(part[-1] for part in parts)
-        operands = (own_keys, *rights)
-        message = run(functools.partial(send_kernel, parts), operands, message_shape(count, rows))
-        return lax.ppermute(message, "tok", OUTER_TO_INNER)
-
-    def cross(right, row, columns, arrived, held=()):
-        body = functools.partial(cross_kernel, row, columns)
-        message = run(body, (own_keys, right, arrived), message_shape(len(columns), rows), held)
-        return lax.ppermute(message, "tok", ACROSS_MIDDLE)
-
-    def back(right, columns, crossed, *arrived, held=()):
-        body = functools.partial(back_kernel, columns)
-        shapes = [message_shape(len(columns), rows)]
-        if arrived:
-            block = message_shape(1, rows)
-            shapes.append(jax.ShapeDtypeStruct((3 * block.shape[0], HALF), block.dtype))
-        message, *turned = run(body, (own_keys, right, crossed, *arrived), shapes, held)
-        half_turn = [(source, (source + 2) % 4) for source in range(4)]
-        turned = [lax.ppermute(part, "layer", half_turn) for part in turned]
-        return lax.ppermute(message, "tok", INNER_TO_OUTER), *turned
+    def hop(message, pairs, layers=0):
+        count = lax.axis_size("layer")
+        pairs = [
+            (layer * 4 + source, (layer + layers) % count * 4 + target)
+            for layer in range(count)
+            for source, target in pairs
+        ]
+        return lax.ppermute(message, ("layer", "tok"), pairs)
+
+    def send(left, right, row, count):
+        body = functools.partial(send_kernel, row, count)
+        return hop(run(body, (left, right), message_shape(count, rows)), OUTER_TO_INNER)
+
+    def cross(left, right, row, count, arrived, layers=0):
+        body = functools.partial(cross_kernel, row, count)
+        message = run(body, (left, right, arrived), message_shape(count, rows))
+        return hop(message, ACROSS_MIDDLE, layers)
+
+    def back(left, right, crossed, layers=0, held=()):
+        message = run(back_kernel, (left, right, crossed), message_shape(4, rows), held)
+        return hop(message, INNER_TO_OUTER, layers)
 
     tile = jax.ShapeDtypeStruct((1, 3, rows, width), jnp.float32)
     token = jax.ShapeDtypeStruct((TAIL, HALF), jnp.bfloat16)
@@ -347,42 +360,47 @@
             pl.BlockSpec((1, 1, rows, width), lambda step: (0, distance, 0, 0)),
         ]
 
-    def finish(out, distance, right, next_across, backs, near, turned=(), near_at=0, turned_at=(), packs=False):
-        operands = (own_keys, right, next_across, near, *backs.values(), *turned)
-        options = {}
+    def finish(out, distance, rights, next_across, near, returned, turned=(), near_at=0, packs=False, held=()):
+        operands = (own_keys, *rights, next_across, near, returned, *turned)
+        options = {"held": held}
         if out is not None:
-            options = {"held": (out,), "input_output_aliases": {len(operands): 1}}
-        body = functools.partial(finish_kernel, near_at, turned_at, packs, tuple(backs))
+            options = {"held": (out, *held), "input_output_aliases": {len(operands): 1}}
+        body = functools.partial(finish_kernel, near_at, len(turned) > 0, packs, len(rights))
         _, out = run(body, operands, [token, tile], grid=(1,), out_specs=tile_specs(distance), **options)
         return out
 
-    every, upper_half, lower_half = (0, 1, 2, 3), (2, 3), (0, 1)
     second_keys = shifted(own_keys, "layer", -1)
-    third_keys = shifted(second_keys, "layer", -1)
-    far_0 = send((own_keys,), (0, FAR, 4))
+    far_0 = send(own_keys, own_keys, FAR, 4)
     rest_0 = run(rest_kernel, (own_keys, own_keys), message_shape(4, rows, 1))
-    rest_0 = lax.ppermute(rest_0, "tok", OUTER_TO_INNER)
-    far_across_0 = cross(own_keys, FAR, every, far_0)
-    far_1 = send((second_keys,), (0, FAR, 4))
-    next_across_0 = cross(own_keys, NEXT, (0, 1, 2), rest_0)
-    (back_0,) = back(own_keys, every, far_across_0)
-    next_1 = send((second_keys,), (0, NEXT, 4))
-    far_across_1 = cross(second_keys, FAR, every, far_1)
-    far_2 = send((third_keys,), (0, FAR, 4))
+    rest_0 = hop(rest_0, OUTER_TO_INNER)
+    far_across_0 = cross(own_keys, own_keys, FAR, 4, far_0)
+    far_1, far_part, rest_part = run(
+        functools.partial(pass_on_kernel, FAR, 4),
+        (own_keys, second_keys),
+        [message_shape(4, rows)]
+        + [jax.ShapeDtypeStruct((own_keys.shape[0], count * rows), own_keys.dtype) for count in (1, 3)],
+    )
+    far_1 = hop(far_1, OUTER_TO_INNER)
+    far_part = shifted(far_part, "layer", -1)
+    rest_part = shifted(rest_part, "layer", -1)
+    next_across_0 = cross(own_keys, own_keys, NEXT, 3, rest_0)
+    far_2 = send(far_part, own_keys, FAR, 4)
+    back_0 = back(own_keys, own_keys, far_across_0)
+    far_across_1 = cross(own_keys, second_keys, FAR, 4, far_1)
+    next_1 = send(own_keys, second_keys, NEXT, 4)
     turned = (far_0, rest_0, far_across_0)
-    out = finish(None, 0, own_keys, next_across_0, {every: back_0}, rest_0, turned, 3, (1, 1, 2), True)
-    next_across_1 = cross(second_keys, NEXT, every, next_1)
-    next_2 = send((third_keys,), (0, NEXT, 3))
-    (back_1,) = back(second_keys, every, far_across_1)
-    near = send((second_keys, third_keys), (0, NEAR, 4), (1, NEAR, 2))
-    far_across_2 = cross(third_keys, FAR, upper_half, far_2)
-    far_across_3 = cross(third_keys, FAR, lower_half, far_2, (next_across_1,))
-    back_2, turned = back(third_keys, upper_half, far_across_2, far_2, next_2, held=(back_1,))
-    next_across_2 = cross(third_keys, NEXT, (0, 1, 2), next_2)
-    (back_3,) = back(third_keys, lower_half, far_across_3)
-    backs = {upper_half: back_2, lower_half: back_3}
-    out = finish(out, 1, second_keys, next_across_1, {every: back_1}, near)
-    return finish(out, 2, third_keys, next_across_2, backs, near, (turned,), 4, (0, 0, 0))
+    out = finish(None, 0, (own_keys,), next_across_0, rest_0, back_0, turned, 3, True)
+    far_across_2 = cross(far_part, own_keys, FAR, 4, far_2)
+    next_2 = send(rest_part, own_keys, NEXT, 3)
+    back_1 = back(own_keys, second_keys, far_across_1)
+    next_across_1 = cross(own_keys, second_keys, NEXT, 4, next_1)
+    near = run(near_kernel, (own_keys, second_keys, rest_part), message_shape(6, rows))
+    near = hop(near, OUTER_TO_INNER)
+    back_2 = back(rest_part, own_keys, far_across_2, 2)
+    next_across_2 = cross(rest_part, own_keys, NEXT, 3, next_2, 2)
+    turned = (far_2, next_2, far_across_2)
+    out = finish(out, 1, (second_keys,), next_across_1, near, back_1)
+    return finish(out, 2, (rest_part, far_part), next_across_2, near, back_2, turned, 4)
 
 
 def per_device(keys):

time: 100 us -> 96.2 us (0.962)
  waiting for transfers between devices: 43.6 us -> 36.6 us
  starting transfers between devices: 38.5 us -> 40.9 us
    ppermute x2 -> x3, waiting for transfers between devices: 13.4 us -> 8.96 us  [shifted(): return lax.ppermute(value, axis, pairs)]
    ppermute x19 -> x16, waiting for transfers between devices: 30.2 us -> 27.6 us  [hop(): return lax.ppermute(message, ('layer', 'tok'), pairs)]
    ppermute x19 -> x16, starting transfers between devices: 34.3 us -> 36.6 us  [hop(): return lax.ppermute(message, ('layer', 'tok'), pairs)]
    pallas_call x21 -> x19, Pallas kernels: 15.6 us -> 16 us  [call(): pl.pallas_call(functools.partial(ordered, body, len(operands), len(held))...]
    ppermute x2 -> x3, starting transfers between devices: 4.18 us -> 4.28 us  [shifted(): return lax.ppermute(value, axis, pairs)]
  transfers between devices with their start and end apart: 21 -> 19, of which waited for: 8 -> 7; matrix products, arithmetic and copies ran while one was open for 0% -> 0% of each run, Pallas kernels for 13% -> 15%
where the time goes in v3:
time: 96.2 us; the launch traced here: 95.4 us
  starting transfers between devices  40.9 us (43%)
  waiting for transfers between devices  36.6 us (38%)
  Pallas kernels  16 us (17%)
  local copies, waits for them, and re-layouts  1.62 us (2%)
    ppermute x16, starting transfers between devices, hop(): return lax.ppermute(message, ('layer', 'tok'), pairs)  36.6 us
    ppermute x16, waiting for transfers between devices, hop(): return lax.ppermute(message, ('layer', 'tok'), pairs)  27.6 us
    pallas_call x19, Pallas kernels, call(): pl.pallas_call(functools.partial(ordered, body, len(operands), len(held))...  16 us
    ppermute x3, waiting for transfers between devices, shifted(): return lax.ppermute(value, axis, pairs)  8.96 us
    ppermute x3, starting transfers between devices, shifted(): return lax.ppermute(value, axis, pairs)  4.28 us
  transfers between devices with their start and end apart: 19, of which 7 were waited for; matrix products, arithmetic and copies ran while one was open for 0% of the time, Pallas kernels for 15%

profile of v3, /device:TPU:0, one launch (start us, length us, event | category | flops | bytes accessed | tf_op | source)
XLA Modules:
  0.0 95.4 jit_solution(2899912098205420066)
XLA Ops:
  0.0 2.4 %collective-permute-start = (bf16[1024,1024]{1,0:T(8,128)(2,1)}, bf16[1024,1024]{1,0:T(8,128)(2,1)S(1)}, u32[]{:S(2)}, u32[]{:S(2)}) collective-permute-start(bf16[1024,1024]{1,0:T(8,128)(2,1)} %bitcast.1), channel_id=1, source_target_pairs={{0,12},{4,0},{8,4},{12,8},{1,13},{5,1},{9,5},{13,9},{2,14},{6,2},{... | collective-permute-start | bytes 6291464 | tf_op jit(solution)/shard_map/ppermute | solution.py:26
  2.4 1.6 %copy-done = bf16[1,1024,1024]{2,1,0:T(8,128)(2,1)S(1)} copy-done((bf16[1,1024,1024]{2,1,0:T(8,128)(2,1)S(1)}, bf16[1,1024,1024]{2,1,0:T(8,128)(2,1)}, u32[]{:S(2)}) %copy-start) | copy-done | bytes 2097176
  4.0 1.2 %shard_map.17.refs_2_ = bf16[2064,128]{1,0:T(8,128)(2,1)S(1)} custom-call(bf16[1024,1024]{1,0:T(8,128)(2,1)S(1)} %bitcast.2, bf16[1024,1024]{1,0:T(8,128)(2,1)S(1)} %bitcast.3, bf16[1024,1024]{1,0:T(8,128)(2,1)S(1)} %bitcast.4), custom_call_target="tpu_custom_call" | custom-call | flops 6000000000 | bytes 6000000 | tf_op jit(solution)/shard_map/pallas_call | solution.py:309
  5.2 2.3 %collective-permute-start.1 = (bf16[2064,128]{1,0:T(8,128)(2,1)S(1)}, bf16[2064,128]{1,0:T(8,128)(2,1)S(1)}, u32[]{:S(2)}, u32[]{:S(2)}) collective-permute-start(bf16[2064,128]{1,0:T(8,128)(2,1)S(1)} %shard_map.17.refs_2_), channel_id=1, source_target_pairs={{0,1},{3,2},{4,5},{7,6},{8,9},{11,10},{12,13},{15,14},{16,17},{19,... | collective-permute-start | bytes 1585160 | tf_op jit(solution)/shard_map/ppermute | solution.py:339
  7.5 1.4 %shard_map.18.refs_3_ = bf16[2096,128]{1,0:T(8,128)(2,1)S(1)} custom-call(bf16[1024,1024]{1,0:T(8,128)(2,1)S(1)} %bitcast.5, bf16[1024,1024]{1,0:T(8,128)(2,1)S(1)} %bitcast.6, bf16[2064,128]{1,0:T(8,128)(2,1)S(1)} %shard_map.17.refs_2_), custom_call_target="tpu_custom_call" | custom-call | flops 6000000000 | bytes 6000000 | tf_op jit(solution)/shard_map/pallas_call | solution.py:309
  8.9 1.3 %collective-permute-start.4 = (bf16[2096,128]{1,0:T(8,128)(2,1)S(1)}, bf16[2096,128]{1,0:T(8,128)(2,1)S(1)}, u32[]{:S(2)}, u32[]{:S(2)}) collective-permute-start(bf16[2096,128]{1,0:T(8,128)(2,1)S(1)} %shard_map.18.refs_3_), channel_id=1, source_target_pairs={{0,1},{3,2},{4,5},{7,6},{8,9},{11,10},{12,13},{15,14},{16,17},{19,... | collective-permute-start | bytes 1609736 | tf_op jit(solution)/shard_map/ppermute | solution.py:339
  10.3 9.7 %collective-permute-done.1.refs_2_.refs_5_ = bf16[2064,128]{1,0:T(8,128)(2,1)S(1)} collective-permute-done((bf16[2064,128]{1,0:T(8,128)(2,1)S(1)}, bf16[2064,128]{1,0:T(8,128)(2,1)S(1)}, u32[]{:S(2)}, u32[]{:S(2)}) %collective-permute-start.1) | collective-permute-done | bytes 528416 | tf_op jit(solution)/shard_map/ppermute | solution.py:339
  20.6 5.6 %collective-permute-done.refs_1_ = bf16[1024,1024]{1,0:T(8,128)(2,1)S(1)} collective-permute-done((bf16[1024,1024]{1,0:T(8,128)(2,1)}, bf16[1024,1024]{1,0:T(8,128)(2,1)S(1)}, u32[]{:S(2)}, u32[]{:S(2)}) %collective-permute-start) | collective-permute-done | bytes 2097184 | tf_op jit(solution)/shard_map/ppermute | solution.py:26
  26.2 1.4 %shard_map.20 = (bf16[2064,128]{1,0:T(8,128)(2,1)S(1)}, bf16[1024,256]{1,0:T(8,128)(2,1)S(1)}, bf16[1024,768]{1,0:T(8,128)(2,1)S(1)}) custom-call(bf16[1024,1024]{1,0:T(8,128)(2,1)S(1)} %bitcast.9, bf16[1024,1024]{1,0:T(8,128)(2,1)S(1)} %collective-permute-done.refs_1_, bf16[2064,128]{1,0:T(8,128)(2,1)S(1)} %shard_map.19.refs_2_), custom_call_target="tpu_custom_call" | custom-call | flops 6000000000 | bytes 6000000 | tf_op jit(solution)/shard_map/pallas_call | solution.py:309
  27.6 1.8 %collective-permute-start.3 = (bf16[1024,256]{1,0:T(8,128)(2,1)S(1)}, bf16[1024,256]{1,0:T(8,128)(2,1)S(1)}, u32[]{:S(2)}, u32[]{:S(2)}) collective-permute-start(bf16[1024,256]{1,0:T(8,128)(2,1)S(1)} %get-tuple-element.14), channel_id=1, source_target_pairs={{0,12},{4,0},{8,4},{12,8},{1,13},{5,1},{9,5},{13,9},{2,14},{6,2},{... | collective-permute-start | bytes 1572872 | tf_op jit(solution)/shard_map/ppermute | solution.py:26
  29.5 2.6 %collective-permute-start.9 = (bf16[2064,128]{1,0:T(8,128)(2,1)S(1)}, bf16[2064,128]{1,0:T(8,128)(2,1)S(1)}, u32[]{:S(2)}, u32[]{:S(2)}) collective-permute-start(bf16[2064,128]{1,0:T(8,128)(2,1)S(1)} %get-tuple-element.15.refs_3_), channel_id=1, source_target_pairs={{0,1},{3,2},{4,5},{7,6},{8,9},{11,10},{12,13},{15,14},{16,17},{19,... | collective-permute-start | bytes 1585160 | tf_op jit(solution)/shard_map/ppermute | solution.py:339
  32.1 0.7 collective-permute-start.6
  32.9 3.3 %collective-permute-done.3.refs_0_.refs_2_ = bf16[1024,256]{1,0:T(8,128)(2,1)S(1)} collective-permute-done((bf16[1024,256]{1,0:T(8,128)(2,1)S(1)}, bf16[1024,256]{1,0:T(8,128)(2,1)S(1)}, u32[]{:S(2)}, u32[]{:S(2)}) %collective-permute-start.3) | collective-permute-done | bytes 524320 | tf_op jit(solution)/shard_map/ppermute | solution.py:26
  36.2 1.2 %shard_map.22.refs_3_ = bf16[2064,128]{1,0:T(8,128)(2,1)S(1)} custom-call(bf16[1024,256]{1,0:T(8,128)(2,1)S(1)} %collective-permute-done.3.refs_0_.refs_2_, bf16[1024,1024]{1,0:T(8,128)(2,1)S(1)} %bitcast.12, bf16[1552,128]{1,0:T(8,128)(2,1)S(1)} %shard_map.21.refs_2_), custom_call_target="tpu_custom_call" | custom-call | flops 6000000000 | bytes 6000000 | tf_op jit(solution)/shard_map/pallas_call | solution.py:309
  37.4 2.9 %collective-permute-start.5 = (bf16[2064,128]{1,0:T(8,128)(2,1)S(1)}, bf16[2064,128]{1,0:T(8,128)(2,1)S(1)}, u32[]{:S(2)}, u32[]{:S(2)}) collective-permute-start(bf16[2064,128]{1,0:T(8,128)(2,1)S(1)} %shard_map.22.refs_3_), channel_id=1, source_target_pairs={{0,1},{3,2},{4,5},{7,6},{8,9},{11,10},{12,13},{15,14},{16,17},{19,... | collective-permute-start | bytes 1585160 | tf_op jit(solution)/shard_map/ppermute | solution.py:339
  40.3 1.3 %collective-permute-start.8 = (bf16[2064,128]{1,0:T(8,128)(2,1)S(1)}, bf16[2064,128]{1,0:T(8,128)(2,1)S(1)}, u32[]{:S(2)}, u32[]{:S(2)}) collective-permute-start(bf16[2064,128]{1,0:T(8,128)(2,1)S(1)} %shard_map.23.refs_3_), channel_id=1, source_target_pairs={{1,0},{2,3},{5,4},{6,7},{9,8},{10,11},{13,12},{14,15},{17,16},{18,... | collective-permute-start | bytes 1585160 | tf_op jit(solution)/shard_map/ppermute | solution.py:339
  41.6 2.9 %collective-permute-done.9.refs_2_ = bf16[2064,128]{1,0:T(8,128)(2,1)S(1)} collective-permute-done((bf16[2064,128]{1,0:T(8,128)(2,1)S(1)}, bf16[2064,128]{1,0:T(8,128)(2,1)S(1)}, u32[]{:S(2)}, u32[]{:S(2)}) %collective-permute-start.9) | collective-permute-done | bytes 528416 | tf_op jit(solution)/shard_map/ppermute | solution.py:339
  45.2 1.4 %shard_map.25.refs_8_ = bf16[2064,128]{1,0:T(8,128)(2,1)S(1)} custom-call(bf16[1024,1024]{1,0:T(8,128)(2,1)S(1)} %bitcast.16, bf16[1024,1024]{1,0:T(8,128)(2,1)S(1)} %collective-permute-done.refs_1_, bf16[2064,128]{1,0:T(8,128)(2,1)S(1)} %shard_map.24.refs_2_), custom_call_target="tpu_custom_call" | custom-call | flops 6000000000 | bytes 6000000 | tf_op jit(solution)/shard_map/pallas_call | solution.py:309
  46.6 7.0 %collective-permute-start.12 = (bf16[2064,128]{1,0:T(8,128)(2,1)S(1)}, bf16[2064,128]{1,0:T(8,128)(2,1)S(1)}, u32[]{:S(2)}, u32[]{:S(2)}) collective-permute-start(bf16[2064,128]{1,0:T(8,128)(2,1)S(1)} %shard_map.25.refs_8_), channel_id=1, source_target_pairs={{0,1},{3,2},{4,5},{7,6},{8,9},{11,10},{12,13},{15,14},{16,17},{19,... | collective-permute-start | bytes 1585160 | tf_op jit(solution)/shard_map/ppermute | solution.py:339
  53.6 2.0 %collective-permute-done.8.refs_4_ = bf16[2064,128]{1,0:T(8,128)(2,1)S(1)} collective-permute-done((bf16[2064,128]{1,0:T(8,128)(2,1)S(1)}, bf16[2064,128]{1,0:T(8,128)(2,1)S(1)}, u32[]{:S(2)}, u32[]{:S(2)}) %collective-permute-start.8) | collective-permute-done | bytes 528416 | tf_op jit(solution)/shard_map/ppermute | solution.py:339
  55.6 2.1 %shard_map.26 = (bf16[16,128]{1,0:T(8,128)(2,1)S(1)}, f32[1,3,256,1024]{3,2,1,0:T(8,128)}) custom-call(bf16[1024,1024]{1,0:T(8,128)(2,1)S(1)} %bitcast.17, bf16[1024,1024]{1,0:T(8,128)(2,1)S(1)} %bitcast.18, bf16[1552,128]{1,0:T(8,128)(2,1)S(1)} %collective-permute-done.6.refs_2_, bf16[2096,128]{1,0:T(8,128)(2,1)S(1)} %collective-permute-done.4.refs_2_.refs_3_.refs_6_, ...), custom_call_target="tpu_custom_call" | custom-call | flops 6000000000 | bytes 6000000 | tf_op jit(solution)/shard_map/pallas_call | solution.py:309
  58.5 1.0 %shard_map.28.refs_3_ = bf16[1552,128]{1,0:T(8,128)(2,1)S(1)} custom-call(bf16[1024,768]{1,0:T(8,128)(2,1)S(1)} %collective-permute-done.2.refs_0_.refs_2_.refs_1_, bf16[1024,1024]{1,0:T(8,128)(2,1)S(1)} %bitcast.20, bf16[2064,128]{1,0:T(8,128)(2,1)S(1)} %shard_map.27.refs_2_), custom_call_target="tpu_custom_call" | custom-call | flops 6000000000 | bytes 6000000 | tf_op jit(solution)/shard_map/pallas_call | solution.py:309
  59.5 6.0 %collective-permute-start.10 = (bf16[1552,128]{1,0:T(8,128)(2,1)S(1)}, bf16[1552,128]{1,0:T(8,128)(2,1)S(1)}, u32[]{:S(2)}, u32[]{:S(2)}) collective-permute-start(bf16[1552,128]{1,0:T(8,128)(2,1)S(1)} %shard_map.28.refs_3_), channel_id=1, source_target_pairs={{0,1},{3,2},{4,5},{7,6},{8,9},{11,10},{12,13},{15,14},{16,17},{19,... | collective-permute-start | bytes 1191944 | tf_op jit(solution)/shard_map/ppermute | solution.py:339
  65.6 1.3 %collective-permute-start.18 = (bf16[2064,128]{1,0:T(8,128)(2,1)S(1)}, bf16[2064,128]{1,0:T(8,128)(2,1)S(1)}, u32[]{:S(2)}, u32[]{:S(2)}) collective-permute-start(bf16[2064,128]{1,0:T(8,128)(2,1)S(1)} %shard_map.29.refs_3_), channel_id=1, source_target_pairs={{1,0},{2,3},{5,4},{6,7},{9,8},{10,11},{13,12},{14,15},{17,16},{18,... | collective-permute-start | bytes 1585160 | tf_op jit(solution)/shard_map/ppermute | solution.py:339
  66.9 0.7 collective-permute-start.17
  67.6 1.7 %shard_map.31.refs_3_ = bf16[3088,128]{1,0:T(8,128)(2,1)S(1)} custom-call(bf16[1024,1024]{1,0:T(8,128)(2,1)S(1)} %bitcast.23, bf16[1024,1024]{1,0:T(8,128)(2,1)S(1)} %collective-permute-done.refs_1_, bf16[1024,768]{1,0:T(8,128)(2,1)S(1)} %collective-permute-done.2.refs_0_.refs_2_.refs_1_, bf16[2064,128]{1,0:T(8,128)(2,1)S(1)} %shard_map.30.refs_3_), custom_call_target="tpu_custom_call" | custom-call | flops 6000000000 | bytes 6000000 | tf_op jit(solution)/shard_map/pallas_call | solution.py:309
  69.3 6.5 %collective-permute-start.15 = (bf16[3088,128]{1,0:T(8,128)(2,1)S(1)}, bf16[3088,128]{1,0:T(8,128)(2,1)S(1)}, u32[]{:S(2)}, u32[]{:S(2)}) collective-permute-start(bf16[3088,128]{1,0:T(8,128)(2,1)S(1)} %shard_map.31.refs_3_), channel_id=1, source_target_pairs={{0,1},{3,2},{4,5},{7,6},{8,9},{11,10},{12,13},{15,14},{16,17},{19,... | collective-permute-start | bytes 2371592 | tf_op jit(solution)/shard_map/ppermute | solution.py:339
  76.1 1.3 %collective-permute-start.16 = (bf16[2064,128]{1,0:T(8,128)(2,1)S(1)}, bf16[2064,128]{1,0:T(8,128)(2,1)S(1)}, u32[]{:S(2)}, u32[]{:S(2)}) collective-permute-start(bf16[2064,128]{1,0:T(8,128)(2,1)S(1)} %shard_map.32.refs_3_), channel_id=1, source_target_pairs={{1,8},{2,11},{5,12},{6,15},{9,0},{10,3},{13,4},{14,7},{17,24},{18,... | collective-permute-start | bytes 1585160 | tf_op jit(solution)/shard_map/ppermute | solution.py:339
  78.1 4.3 %collective-permute-done.18.refs_4_ = bf16[2064,128]{1,0:T(8,128)(2,1)S(1)} collective-permute-done((bf16[2064,128]{1,0:T(8,128)(2,1)S(1)}, bf16[2064,128]{1,0:T(8,128)(2,1)S(1)}, u32[]{:S(2)}, u32[]{:S(2)}) %collective-permute-start.18) | collective-permute-done | bytes 528416 | tf_op jit(solution)/shard_map/ppermute | solution.py:339
  82.4 8.7 %collective-permute-done.15.refs_3_.refs_4_ = bf16[3088,128]{1,0:T(8,128)(2,1)S(1)} collective-permute-done((bf16[3088,128]{1,0:T(8,128)(2,1)S(1)}, bf16[3088,128]{1,0:T(8,128)(2,1)S(1)}, u32[]{:S(2)}, u32[]{:S(2)}) %collective-permute-start.15) | collective-permute-done | bytes 790560 | tf_op jit(solution)/shard_map/ppermute | solution.py:339
  91.1 2.1 %shard_map.34 = (bf16[16,128]{1,0:T(8,128)(2,1)S(1)}, f32[1,3,256,1024]{3,2,1,0:T(8,128)}) custom-call(bf16[1024,1024]{1,0:T(8,128)(2,1)S(1)} %bitcast.26, bf16[1024,1024]{1,0:T(8,128)(2,1)S(1)} %collective-permute-done.refs_1_, bf16[2064,128]{1,0:T(8,128)(2,1)S(1)} %collective-permute-done.17.refs_2_, ...), custom_call_target="tpu_custom_call", output_to_operand_aliasing={{1}: (5, {})} | custom-call | flops 6000000000 | bytes 6000000 | tf_op jit(solution)/shard_map/pallas_call | solution.py:309
  93.3 2.1 %shard_map.35 = (bf16[16,128]{1,0:T(8,128)(2,1)}, f32[1,3,256,1024]{3,2,1,0:T(8,128)}) custom-call(bf16[1024,1024]{1,0:T(8,128)(2,1)S(1)} %bitcast.27, bf16[1024,768]{1,0:T(8,128)(2,1)S(1)} %collective-permute-done.2.refs_0_.refs_2_.refs_1_, bf16[1024,256]{1,0:T(8,128)(2,1)S(1)} %collective-permute-done.3.refs_0_.refs_2_, ...), custom_call_target="tpu_custom_call", output_to_operand_aliasing={{1}: (9, {})} | custom-call | flops 6000000000 | bytes 6000000 | tf_op jit(solution)/shard_map/pallas_call | solution.py:309
  (27 shorter events, 3.1 us)
Async XLA Ops:
  0.0 26.2 %collective-permute-start = (bf16[1024,1024]{1,0:T(8,128)(2,1)}, bf16[1024,1024]{1,0:T(8,128)(2,1)S(1)}, u32[]{:S(2)}, u32[]{:S(2)}) collective-permute-start(bf16[1024,1024]{1,0:T(8,128)(2,1)} %bitcast.1), channel_id=1, source_target_pairs={{0,12},{4,0},{8,4},{12,8},{1,13},{5,1},{9,5},{13,9},{2,14},{6,2},{... | collective-permute-start | bytes 6291464 | tf_op jit(solution)/shard_map/ppermute | solution.py:26
  2.4 1.6 %copy-start = (bf16[1,1024,1024]{2,1,0:T(8,128)(2,1)S(1)}, bf16[1,1024,1024]{2,1,0:T(8,128)(2,1)}, u32[]{:S(2)}) copy-start(bf16[1,1024,1024]{2,1,0:T(8,128)(2,1)} %param.1) | copy-start | bytes 6291460
  5.2 14.7 %collective-permute-start.1 = (bf16[2064,128]{1,0:T(8,128)(2,1)S(1)}, bf16[2064,128]{1,0:T(8,128)(2,1)S(1)}, u32[]{:S(2)}, u32[]{:S(2)}) collective-permute-start(bf16[2064,128]{1,0:T(8,128)(2,1)S(1)} %shard_map.17.refs_2_), channel_id=1, source_target_pairs={{0,1},{3,2},{4,5},{7,6},{8,9},{11,10},{12,13},{15,14},{16,17},{19,... | collective-permute-start | bytes 1585160 | tf_op jit(solution)/shard_map/ppermute | solution.py:339
  8.9 23.1 %collective-permute-start.4 = (bf16[2096,128]{1,0:T(8,128)(2,1)S(1)}, bf16[2096,128]{1,0:T(8,128)(2,1)S(1)}, u32[]{:S(2)}, u32[]{:S(2)}) collective-permute-start(bf16[2096,128]{1,0:T(8,128)(2,1)S(1)} %shard_map.18.refs_3_), channel_id=1, source_target_pairs={{0,1},{3,2},{4,5},{7,6},{8,9},{11,10},{12,13},{15,14},{16,17},{19,... | collective-permute-start | bytes 1609736 | tf_op jit(solution)/shard_map/ppermute | solution.py:339
  19.9 20.4 %collective-permute-start.7 = (bf16[2064,128]{1,0:T(8,128)(2,1)S(1)}, bf16[2064,128]{1,0:T(8,128)(2,1)S(1)}, u32[]{:S(2)}, u32[]{:S(2)}) collective-permute-start(bf16[2064,128]{1,0:T(8,128)(2,1)S(1)} %shard_map.19.refs_2_), channel_id=1, source_target_pairs={{1,2},{2,1},{5,6},{6,5},{9,10},{10,9},{13,14},{14,13},{17,18},{18,... | collective-permute-start | bytes 1585160 | tf_op jit(solution)/shard_map/ppermute | solution.py:339
  27.6 8.5 %collective-permute-start.3 = (bf16[1024,256]{1,0:T(8,128)(2,1)S(1)}, bf16[1024,256]{1,0:T(8,128)(2,1)S(1)}, u32[]{:S(2)}, u32[]{:S(2)}) collective-permute-start(bf16[1024,256]{1,0:T(8,128)(2,1)S(1)} %get-tuple-element.14), channel_id=1, source_target_pairs={{0,12},{4,0},{8,4},{12,8},{1,13},{5,1},{9,5},{13,9},{2,14},{6,2},{... | collective-permute-start | bytes 1572872 | tf_op jit(solution)/shard_map/ppermute | solution.py:26
  29.5 15.0 %collective-permute-start.9 = (bf16[2064,128]{1,0:T(8,128)(2,1)S(1)}, bf16[2064,128]{1,0:T(8,128)(2,1)S(1)}, u32[]{:S(2)}, u32[]{:S(2)}) collective-permute-start(bf16[2064,128]{1,0:T(8,128)(2,1)S(1)} %get-tuple-element.15.refs_3_), channel_id=1, source_target_pairs={{0,1},{3,2},{4,5},{7,6},{8,9},{11,10},{12,13},{15,14},{16,17},{19,... | collective-permute-start | bytes 1585160 | tf_op jit(solution)/shard_map/ppermute | solution.py:339
  32.1 14.5 %collective-permute-start.6 = (bf16[1552,128]{1,0:T(8,128)(2,1)S(1)}, bf16[1552,128]{1,0:T(8,128)(2,1)S(1)}, u32[]{:S(2)}, u32[]{:S(2)}) collective-permute-start(bf16[1552,128]{1,0:T(8,128)(2,1)S(1)} %shard_map.21.refs_2_), channel_id=1, source_target_pairs={{1,2},{2,1},{5,6},{6,5},{9,10},{10,9},{13,14},{14,13},{17,18},{18,... | collective-permute-start | bytes 1191944 | tf_op jit(solution)/shard_map/ppermute | solution.py:339
  32.8 25.7 %collective-permute-start.2 = (bf16[1024,768]{1,0:T(8,128)(2,1)S(1)}, bf16[1024,768]{1,0:T(8,128)(2,1)S(1)}, u32[]{:S(2)}, u32[]{:S(2)}) collective-permute-start(bf16[1024,768]{1,0:T(8,128)(2,1)S(1)} %get-tuple-element.13), channel_id=1, source_target_pairs={{0,12},{4,0},{8,4},{12,8},{1,13},{5,1},{9,5},{13,9},{2,14},{6,2},{... | collective-permute-start | bytes 4718600 | tf_op jit(solution)/shard_map/ppermute | solution.py:26
  37.4 20.4 %collective-permute-start.5 = (bf16[2064,128]{1,0:T(8,128)(2,1)S(1)}, bf16[2064,128]{1,0:T(8,128)(2,1)S(1)}, u32[]{:S(2)}, u32[]{:S(2)}) collective-permute-start(bf16[2064,128]{1,0:T(8,128)(2,1)S(1)} %shard_map.22.refs_3_), channel_id=1, source_target_pairs={{0,1},{3,2},{4,5},{7,6},{8,9},{11,10},{12,13},{15,14},{16,17},{19,... | collective-permute-start | bytes 1585160 | tf_op jit(solution)/shard_map/ppermute | solution.py:339
  40.3 15.3 %collective-permute-start.8 = (bf16[2064,128]{1,0:T(8,128)(2,1)S(1)}, bf16[2064,128]{1,0:T(8,128)(2,1)S(1)}, u32[]{:S(2)}, u32[]{:S(2)}) collective-permute-start(bf16[2064,128]{1,0:T(8,128)(2,1)S(1)} %shard_map.23.refs_3_), channel_id=1, source_target_pairs={{1,0},{2,3},{5,4},{6,7},{9,8},{10,11},{13,12},{14,15},{17,16},{18,... | collective-permute-start | bytes 1585160 | tf_op jit(solution)/shard_map/ppermute | solution.py:339
  44.5 21.1 %collective-permute-start.13 = (bf16[2064,128]{1,0:T(8,128)(2,1)S(1)}, bf16[2064,128]{1,0:T(8,128)(2,1)S(1)}, u32[]{:S(2)}, u32[]{:S(2)}) collective-permute-start(bf16[2064,128]{1,0:T(8,128)(2,1)S(1)} %shard_map.24.refs_2_), channel_id=1, source_target_pairs={{1,2},{2,1},{5,6},{6,5},{9,10},{10,9},{13,14},{14,13},{17,18},{18,... | collective-permute-start | bytes 1585160 | tf_op jit(solution)/shard_map/ppermute | solution.py:339
  46.6 20.3 %collective-permute-start.12 = (bf16[2064,128]{1,0:T(8,128)(2,1)S(1)}, bf16[2064,128]{1,0:T(8,128)(2,1)S(1)}, u32[]{:S(2)}, u32[]{:S(2)}) collective-permute-start(bf16[2064,128]{1,0:T(8,128)(2,1)S(1)} %shard_map.25.refs_8_), channel_id=1, source_target_pairs={{0,1},{3,2},{4,5},{7,6},{8,9},{11,10},{12,13},{15,14},{16,17},{19,... | collective-permute-start | bytes 1585160 | tf_op jit(solution)/shard_map/ppermute | solution.py:339
  57.8 18.0 %collective-permute-start.11 = (bf16[2064,128]{1,0:T(8,128)(2,1)S(1)}, bf16[2064,128]{1,0:T(8,128)(2,1)S(1)}, u32[]{:S(2)}, u32[]{:S(2)}) collective-permute-start(bf16[2064,128]{1,0:T(8,128)(2,1)S(1)} %shard_map.27.refs_2_), channel_id=1, source_target_pairs={{1,2},{2,1},{5,6},{6,5},{9,10},{10,9},{13,14},{14,13},{17,18},{18,... | collective-permute-start | bytes 1585160 | tf_op jit(solution)/shard_map/ppermute | solution.py:339
  59.5 17.9 %collective-permute-start.10 = (bf16[1552,128]{1,0:T(8,128)(2,1)S(1)}, bf16[1552,128]{1,0:T(8,128)(2,1)S(1)}, u32[]{:S(2)}, u32[]{:S(2)}) collective-permute-start(bf16[1552,128]{1,0:T(8,128)(2,1)S(1)} %shard_map.28.refs_3_), channel_id=1, source_target_pairs={{0,1},{3,2},{4,5},{7,6},{8,9},{11,10},{12,13},{15,14},{16,17},{19,... | collective-permute-start | bytes 1191944 | tf_op jit(solution)/shard_map/ppermute | solution.py:339
  65.6 16.8 %collective-permute-start.18 = (bf16[2064,128]{1,0:T(8,128)(2,1)S(1)}, bf16[2064,128]{1,0:T(8,128)(2,1)S(1)}, u32[]{:S(2)}, u32[]{:S(2)}) collective-permute-start(bf16[2064,128]{1,0:T(8,128)(2,1)S(1)} %shard_map.29.refs_3_), channel_id=1, source_target_pairs={{1,0},{2,3},{5,4},{6,7},{9,8},{10,11},{13,12},{14,15},{17,16},{18,... | collective-permute-start | bytes 1585160 | tf_op jit(solution)/shard_map/ppermute | solution.py:339
  66.9 11.2 %collective-permute-start.17 = (bf16[2064,128]{1,0:T(8,128)(2,1)S(1)}, bf16[2064,128]{1,0:T(8,128)(2,1)S(1)}, u32[]{:S(2)}, u32[]{:S(2)}) collective-permute-start(bf16[2064,128]{1,0:T(8,128)(2,1)S(1)} %shard_map.30.refs_3_), channel_id=1, source_target_pairs={{1,2},{2,1},{5,6},{6,5},{9,10},{10,9},{13,14},{14,13},{17,18},{18,... | collective-permute-start | bytes 1585160 | tf_op jit(solution)/shard_map/ppermute | solution.py:339
  69.3 21.8 %collective-permute-start.15 = (bf16[3088,128]{1,0:T(8,128)(2,1)S(1)}, bf16[3088,128]{1,0:T(8,128)(2,1)S(1)}, u32[]{:S(2)}, u32[]{:S(2)}) collective-permute-start(bf16[3088,128]{1,0:T(8,128)(2,1)S(1)} %shard_map.31.refs_3_), channel_id=1, source_target_pairs={{0,1},{3,2},{4,5},{7,6},{8,9},{11,10},{12,13},{15,14},{16,17},{19,... | collective-permute-start | bytes 2371592 | tf_op jit(solution)/shard_map/ppermute | solution.py:339
  76.1 17.2 %collective-permute-start.16 = (bf16[2064,128]{1,0:T(8,128)(2,1)S(1)}, bf16[2064,128]{1,0:T(8,128)(2,1)S(1)}, u32[]{:S(2)}, u32[]{:S(2)}) collective-permute-start(bf16[2064,128]{1,0:T(8,128)(2,1)S(1)} %shard_map.32.refs_3_), channel_id=1, source_target_pairs={{1,8},{2,11},{5,12},{6,15},{9,0},{10,3},{13,4},{14,7},{17,24},{18,... | collective-permute-start | bytes 1585160 | tf_op jit(solution)/shard_map/ppermute | solution.py:339
  77.4 15.9 %collective-permute-start.14 = (bf16[1552,128]{1,0:T(8,128)(2,1)S(1)}, bf16[1552,128]{1,0:T(8,128)(2,1)S(1)}, u32[]{:S(2)}, u32[]{:S(2)}) collective-permute-start(bf16[1552,128]{1,0:T(8,128)(2,1)S(1)} %shard_map.33.refs_6_), channel_id=1, source_target_pairs={{1,10},{2,9},{5,14},{6,13},{9,2},{10,1},{13,6},{14,5},{17,26},{18,... | collective-permute-start | bytes 1191944 | tf_op jit(solution)/shard_map/ppermute | solution.py:339

commit v4 on v3

--- a/solution.py
+++ b/solution.py
@@ -16,7 +16,7 @@
 TAIL = 16
 SPREAD = 13777.0
 SMALLEST = 1e-30
-COSTS = tuple(1_000_000_000 * cost for cost in (6, 6, 6, 6, 6, 6, 6, 6, 6, 6, 6, 6, 6, 6, 6, 6, 6, 6, 6))
+COSTS = (6_000_000_000,) * 20
 VMEM_BYTES = 24 * 1024 * 1024
 
 
@@ -259,44 +259,101 @@
     out_ref[0, 0, :, at] = value
 
 
-def finish_kernel(near_at, folds, packs, rights, inverse, left_ref, *refs):
-    right_refs, (next_ref, near_ref, back_ref) = refs[:rights], refs[rights : rights + 3]
-    *turned_refs, token_ref, out_ref = refs[rights + 3 :]
+def finish_kernel(inverse, keys_ref, next_ref, rest_ref, back_ref, far_ref, across_ref, token_ref, out_ref):
     token_ref[...] = jnp.zeros_like(token_ref)
+    rows = keys_ref.shape[1] // 4
+    upper, inner = fold()
+
+    def own_sums(row, column):
+        return product(inverse, keys_ref, keys_ref, upper, row, column, rows)
+
+    @pl.when(jnp.logical_not(inner))
+    def _():
+        for column in range(4):
+            put(out_ref, upper, column, rows, own_sums(0, column) + read_block(back_ref, column, rows))
+
+    @pl.when(inner)
+    def _():
+        row, column = place_in_block(rows)
+        across = read_block(next_ref, 2, rows)
+        blocks = [
+            read_block(rest_ref, 3, rows) + read_block(across_ref, 2, rows).T,
+            read_packed(rest_ref, 2, rows) + jnp.where(row >= column, across, across.T),
+            read_block(rest_ref, 1, rows).T + read_block(next_ref, 1, rows),
+            read_block(far_ref, 1, rows).T + read_block(next_ref, 0, rows),
+        ]
+        for column, block in enumerate(blocks):
+            put(out_ref, upper, column, rows, own_sums(1, column) + block)
+
+
+def partial_kernel(inverse, left_ref, *refs):
+    plain_ref, *folded_refs, next_ref, back_ref, far_ref, beside_ref, across_ref, plain_out, folded_out = refs
     rows = left_ref.shape[1] // 4
     upper, inner = fold()
 
-    def own_sums(row, column):
-        right_ref = right_refs[-1] if column == FAR else right_refs[0]
+    def own_sums(right_ref, row, column):
         return product(inverse, left_ref, right_ref, upper, row, column, rows)
 
-    def turned_block(number):
-        return read_block(turned_refs[number], (1, 1, 2)[number], rows).T
-
-    @pl.when(jnp.logical_not(inner))
-    def _():
-        for column in range(4):
-            put(out_ref, upper, column, rows, own_sums(0, column) + read_block(back_ref, column, rows))
-
-    @pl.when(inner)
-    def _():
-        for column in range(4):
-            own = own_sums(1, column)
-            if folds and column >= 2:
-                own = own + turned_block(3 - column)
-            elif packs and column == 1:
-                own = own + read_packed(near_ref, 2, rows)
-            else:
-                own = own + read_block(near_ref, near_at + column, rows)
-            if folds and column == 0:
-                own = own + turned_block(2)
-            elif packs and column == 1:
-                across = read_block(next_ref, 2, rows)
-                row, place = place_in_block(rows)
-                own = own + jnp.where(row >= place, across, across.T)
-            else:
-                own = own + read_block(next_ref, 3 - column, rows)
-            put(out_ref, upper, column, rows, own)
+    def folded_sums(row, column):
+        return own_sums(folded_refs[-1] if column == FAR else folded_refs[0], row, column)
+
+    def block(column):
+        return slice(column * rows, (column + 1) * rows)
+
+    @pl.when(jnp.logical_not(inner))
+    def _():
+        for column in range(4):
+            plain_out[:, block(column)] = own_sums(plain_ref, 0, column) + read_block(back_ref, column, rows)
+            folded_out[:, block(column)] = folded_sums(0, column)
+
+    @pl.when(inner)
+    def _():
+        turned = {3: (far_ref, 1), 2: (beside_ref, 1), 0: (across_ref, 2)}
+        for column in range(4):
+            plain_out[:, block(column)] = own_sums(plain_ref, 1, column) + read_block(next_ref, 3 - column, rows)
+            sums = folded_sums(1, column)
+            if column in turned:
+                sums = sums + read_block(*turned[column], rows).T
+            folded_out[:, block(column)] = sums
+
+
+def last_plain_kernel(inverse, sums_ref, near_ref, token_ref, out_ref):
+    rows = sums_ref.shape[0]
+    upper, inner = fold()
+    token_ref[...] = jnp.zeros_like(token_ref)
+
+    @pl.when(jnp.logical_not(inner))
+    def _():
+        for column in range(4):
+            put(out_ref, upper, column, rows, sums_ref[:, column * rows : (column + 1) * rows])
+
+    @pl.when(inner)
+    def _():
+        for column in range(4):
+            sums = sums_ref[:, column * rows : (column + 1) * rows]
+            put(out_ref, upper, column, rows, sums + read_block(near_ref, column, rows))
+
+
+def last_folded_kernel(inverse, sums_ref, near_ref, next_ref, back_ref, token_ref, out_ref):
+    rows = sums_ref.shape[0]
+    upper, inner = fold()
+    token_ref[...] = jnp.zeros_like(token_ref)
+
+    @pl.when(jnp.logical_not(inner))
+    def _():
+        for column in range(4):
+            sums = sums_ref[:, column * rows : (column + 1) * rows]
+            put(out_ref, upper, column, rows, sums + read_block(back_ref, column, rows))
+
+    @pl.when(inner)
+    def _():
+        for column in range(4):
+            sums = sums_ref[:, column * rows : (column + 1) * rows]
+            if column < 2:
+                sums = sums + read_block(near_ref, 4 + column, rows)
+            if column > 0:
+                sums = sums + read_block(next_ref, 3 - column, rows)
+            put(out_ref, upper, column, rows, sums)
 
 
 def ordered(body, count, held, *refs):
@@ -354,20 +411,26 @@
     tile = jax.ShapeDtypeStruct((1, 3, rows, width), jnp.float32)
     token = jax.ShapeDtypeStruct((TAIL, HALF), jnp.bfloat16)
 
-    def tile_specs(distance):
-        return [
-            pl.BlockSpec((TAIL, HALF), lambda step: (0, 0)),
-            pl.BlockSpec((1, 1, rows, width), lambda step: (0, distance, 0, 0)),
-        ]
-
-    def finish(out, distance, rights, next_across, near, returned, turned=(), near_at=0, packs=False, held=()):
-        operands = (own_keys, *rights, next_across, near, returned, *turned)
-        options = {"held": held}
+    def write_tile(distance, out, body, operands):
+        options = {}
         if out is not None:
-            options = {"held": (out, *held), "input_output_aliases": {len(operands): 1}}
-        body = functools.partial(finish_kernel, near_at, len(turned) > 0, packs, len(rights))
-        _, out = run(body, operands, [token, tile], grid=(1,), out_specs=tile_specs(distance), **options)
+            options = {"held": (out,), "input_output_aliases": {len(operands): 1}}
+        _, out = run(
+            body,
+            operands,
+            [token, tile],
+            grid=(1,),
+            out_specs=[
+                pl.BlockSpec((TAIL, HALF), lambda step: (0, 0)),
+                pl.BlockSpec((1, 1, rows, width), lambda step: (0, distance, 0, 0)),
+            ],
+            **options,
+        )
         return out
+
+
+    def part_of_keys(count):
+        return jax.ShapeDtypeStruct((own_keys.shape[0], count * rows), own_keys.dtype)
 
     second_keys = shifted(own_keys, "layer", -1)
     far_0 = send(own_keys, own_keys, FAR, 4)
@@ -377,8 +440,7 @@
     far_1, far_part, rest_part = run(
         functools.partial(pass_on_kernel, FAR, 4),
         (own_keys, second_keys),
-        [message_shape(4, rows)]
-        + [jax.ShapeDtypeStruct((own_keys.shape[0], count * rows), own_keys.dtype) for count in (1, 3)],
+        [message_shape(4, rows), part_of_keys(1), part_of_keys(3)],
     )
     far_1 = hop(far_1, OUTER_TO_INNER)
     far_part = shifted(far_part, "layer", -1)
@@ -388,8 +450,9 @@
     back_0 = back(own_keys, own_keys, far_across_0)
     far_across_1 = cross(own_keys, second_keys, FAR, 4, far_1)
     next_1 = send(own_keys, second_keys, NEXT, 4)
-    turned = (far_0, rest_0, far_across_0)
-    out = finish(None, 0, (own_keys,), next_across_0, rest_0, back_0, turned, 3, True)
+    out = write_tile(
+        0, None, finish_kernel, (own_keys, next_across_0, rest_0, back_0, far_0, far_across_0)
+    )
     far_across_2 = cross(far_part, own_keys, FAR, 4, far_2)
     next_2 = send(rest_part, own_keys, NEXT, 3)
     back_1 = back(own_keys, second_keys, far_across_1)
@@ -398,9 +461,15 @@
     near = hop(near, OUTER_TO_INNER)
     back_2 = back(rest_part, own_keys, far_across_2, 2)
     next_across_2 = cross(rest_part, own_keys, NEXT, 3, next_2, 2)
+    part = jax.ShapeDtypeStruct((rows, width), jnp.float32)
     turned = (far_2, next_2, far_across_2)
-    out = finish(out, 1, (second_keys,), next_across_1, near, back_1)
-    return finish(out, 2, (rest_part, far_part), next_across_2, near, back_2, turned, 4)
+    parts = run(
+        partial_kernel,
+        (own_keys, second_keys, rest_part, far_part, next_across_1, back_1, *turned),
+        [part, part],
+    )
+    out = write_tile(1, out, last_plain_kernel, (parts[0], near))
+    return write_tile(2, out, last_folded_kernel, (parts[1], near, next_across_2, back_2))
 
 
 def per_device(keys):

time: 96.2 us -> 95 us (0.988)
  waiting for transfers between devices: 36.6 us -> 35.3 us
    ppermute x16, waiting for transfers between devices: 27.6 us -> 26.3 us  [hop(): return lax.ppermute(message, ('layer', 'tok'), pairs)]
    pallas_call x19 -> x20, Pallas kernels: 16 us -> 15.8 us  [call(): pl.pallas_call(functools.partial(ordered, body, len(operands), len(held))...]
  transfers between devices with their start and end apart: 19 -> 19, of which waited for: 7 -> 8; matrix products, arithmetic and copies ran while one was open for 0% -> 0% of each run, Pallas kernels for 15% -> 15%
where the time goes in v4:
time: 95 us; the launch traced here: 93.9 us
  starting transfers between devices  40.9 us (43%)
  waiting for transfers between devices  35.3 us (37%)
  Pallas kernels  15.8 us (17%)
  local copies, waits for them, and re-layouts  1.62 us (2%)
    ppermute x16, starting transfers between devices, hop(): return lax.ppermute(message, ('layer', 'tok'), pairs)  36.6 us
    ppermute x16, waiting for transfers between devices, hop(): return lax.ppermute(message, ('layer', 'tok'), pairs)  26.3 us
    pallas_call x20, Pallas kernels, call(): pl.pallas_call(functools.partial(ordered, body, len(operands), len(held))...  15.8 us
    ppermute x3, waiting for transfers between devices, shifted(): return lax.ppermute(value, axis, pairs)  8.96 us
    ppermute x3, starting transfers between devices, shifted(): return lax.ppermute(value, axis, pairs)  4.28 us
  transfers between devices with their start and end apart: 19, of which 8 were waited for; matrix products, arithmetic and copies ran while one was open for 0% of the time, Pallas kernels for 15%

profile of v4, /device:TPU:0, one launch (start us, length us, event | category | flops | bytes accessed | tf_op | source)
XLA Modules:
  0.0 93.9 jit_solution(7237035100710538067)
XLA Ops:
  0.0 2.4 %collective-permute-start = (bf16[1024,1024]{1,0:T(8,128)(2,1)}, bf16[1024,1024]{1,0:T(8,128)(2,1)S(1)}, u32[]{:S(2)}, u32[]{:S(2)}) collective-permute-start(bf16[1024,1024]{1,0:T(8,128)(2,1)} %bitcast.1), channel_id=1, source_target_pairs={{0,12},{4,0},{8,4},{12,8},{1,13},{5,1},{9,5},{13,9},{2,14},{6,2},{... | collective-permute-start | bytes 6291464 | tf_op jit(solution)/shard_map/ppermute | solution.py:26
  2.4 1.6 %copy-done = bf16[1,1024,1024]{2,1,0:T(8,128)(2,1)S(1)} copy-done((bf16[1,1024,1024]{2,1,0:T(8,128)(2,1)S(1)}, bf16[1,1024,1024]{2,1,0:T(8,128)(2,1)}, u32[]{:S(2)}) %copy-start) | copy-done | bytes 2097176
  4.0 1.2 %shard_map.17.refs_2_ = bf16[2064,128]{1,0:T(8,128)(2,1)S(1)} custom-call(bf16[1024,1024]{1,0:T(8,128)(2,1)S(1)} %bitcast.2, bf16[1024,1024]{1,0:T(8,128)(2,1)S(1)} %bitcast.3, bf16[1024,1024]{1,0:T(8,128)(2,1)S(1)} %bitcast.4), custom_call_target="tpu_custom_call" | custom-call | flops 6000000000 | bytes 6000000 | tf_op jit(solution)/shard_map/pallas_call | solution.py:366
  5.2 2.3 %collective-permute-start.1 = (bf16[2064,128]{1,0:T(8,128)(2,1)S(1)}, bf16[2064,128]{1,0:T(8,128)(2,1)S(1)}, u32[]{:S(2)}, u32[]{:S(2)}) collective-permute-start(bf16[2064,128]{1,0:T(8,128)(2,1)S(1)} %shard_map.17.refs_2_), channel_id=1, source_target_pairs={{0,1},{3,2},{4,5},{7,6},{8,9},{11,10},{12,13},{15,14},{16,17},{19,... | collective-permute-start | bytes 1585160 | tf_op jit(solution)/shard_map/ppermute | solution.py:396
  7.5 1.4 %shard_map.18.refs_3_ = bf16[2096,128]{1,0:T(8,128)(2,1)S(1)} custom-call(bf16[1024,1024]{1,0:T(8,128)(2,1)S(1)} %bitcast.5, bf16[1024,1024]{1,0:T(8,128)(2,1)S(1)} %bitcast.6, bf16[2064,128]{1,0:T(8,128)(2,1)S(1)} %shard_map.17.refs_2_), custom_call_target="tpu_custom_call" | custom-call | flops 6000000000 | bytes 6000000 | tf_op jit(solution)/shard_map/pallas_call | solution.py:366
  8.9 1.3 %collective-permute-start.6 = (bf16[2096,128]{1,0:T(8,128)(2,1)S(1)}, bf16[2096,128]{1,0:T(8,128)(2,1)S(1)}, u32[]{:S(2)}, u32[]{:S(2)}) collective-permute-start(bf16[2096,128]{1,0:T(8,128)(2,1)S(1)} %shard_map.18.refs_3_), channel_id=1, source_target_pairs={{0,1},{3,2},{4,5},{7,6},{8,9},{11,10},{12,13},{15,14},{16,17},{19,... | collective-permute-start | bytes 1609736 | tf_op jit(solution)/shard_map/ppermute | solution.py:396
  10.3 9.7 %collective-permute-done.1.refs_2_.refs_4_ = bf16[2064,128]{1,0:T(8,128)(2,1)S(1)} collective-permute-done((bf16[2064,128]{1,0:T(8,128)(2,1)S(1)}, bf16[2064,128]{1,0:T(8,128)(2,1)S(1)}, u32[]{:S(2)}, u32[]{:S(2)}) %collective-permute-start.1) | collective-permute-done | bytes 528416 | tf_op jit(solution)/shard_map/ppermute | solution.py:396
  20.6 5.6 %collective-permute-done.refs_1_ = bf16[1024,1024]{1,0:T(8,128)(2,1)S(1)} collective-permute-done((bf16[1024,1024]{1,0:T(8,128)(2,1)}, bf16[1024,1024]{1,0:T(8,128)(2,1)S(1)}, u32[]{:S(2)}, u32[]{:S(2)}) %collective-permute-start) | collective-permute-done | bytes 2097184 | tf_op jit(solution)/shard_map/ppermute | solution.py:26
  26.2 1.4 %shard_map.20 = (bf16[2064,128]{1,0:T(8,128)(2,1)S(1)}, bf16[1024,256]{1,0:T(8,128)(2,1)S(1)}, bf16[1024,768]{1,0:T(8,128)(2,1)S(1)}) custom-call(bf16[1024,1024]{1,0:T(8,128)(2,1)S(1)} %bitcast.9, bf16[1024,1024]{1,0:T(8,128)(2,1)S(1)} %collective-permute-done.refs_1_, bf16[2064,128]{1,0:T(8,128)(2,1)S(1)} %shard_map.19.refs_2_), custom_call_target="tpu_custom_call" | custom-call | flops 6000000000 | bytes 6000000 | tf_op jit(solution)/shard_map/pallas_call | solution.py:366
  27.6 1.8 %collective-permute-start.3 = (bf16[1024,256]{1,0:T(8,128)(2,1)S(1)}, bf16[1024,256]{1,0:T(8,128)(2,1)S(1)}, u32[]{:S(2)}, u32[]{:S(2)}) collective-permute-start(bf16[1024,256]{1,0:T(8,128)(2,1)S(1)} %get-tuple-element.16), channel_id=1, source_target_pairs={{0,12},{4,0},{8,4},{12,8},{1,13},{5,1},{9,5},{13,9},{2,14},{6,2},{... | collective-permute-start | bytes 1572872 | tf_op jit(solution)/shard_map/ppermute | solution.py:26
  29.5 2.6 %collective-permute-start.4 = (bf16[2064,128]{1,0:T(8,128)(2,1)S(1)}, bf16[2064,128]{1,0:T(8,128)(2,1)S(1)}, u32[]{:S(2)}, u32[]{:S(2)}) collective-permute-start(bf16[2064,128]{1,0:T(8,128)(2,1)S(1)} %get-tuple-element.17.refs_3_), channel_id=1, source_target_pairs={{0,1},{3,2},{4,5},{7,6},{8,9},{11,10},{12,13},{15,14},{16,17},{19,... | collective-permute-start | bytes 1585160 | tf_op jit(solution)/shard_map/ppermute | solution.py:396
  32.9 3.3 %collective-permute-done.3.refs_0_.refs_3_ = bf16[1024,256]{1,0:T(8,128)(2,1)S(1)} collective-permute-done((bf16[1024,256]{1,0:T(8,128)(2,1)S(1)}, bf16[1024,256]{1,0:T(8,128)(2,1)S(1)}, u32[]{:S(2)}, u32[]{:S(2)}) %collective-permute-start.3) | collective-permute-done | bytes 524320 | tf_op jit(solution)/shard_map/ppermute | solution.py:26
  36.2 1.2 %shard_map.22.refs_3_ = bf16[2064,128]{1,0:T(8,128)(2,1)S(1)} custom-call(bf16[1024,256]{1,0:T(8,128)(2,1)S(1)} %collective-permute-done.3.refs_0_.refs_3_, bf16[1024,1024]{1,0:T(8,128)(2,1)S(1)} %bitcast.12, bf16[1552,128]{1,0:T(8,128)(2,1)S(1)} %shard_map.21.refs_2_), custom_call_target="tpu_custom_call" | custom-call | flops 6000000000 | bytes 6000000 | tf_op jit(solution)/shard_map/pallas_call | solution.py:366
  37.4 2.9 %collective-permute-start.9 = (bf16[2064,128]{1,0:T(8,128)(2,1)S(1)}, bf16[2064,128]{1,0:T(8,128)(2,1)S(1)}, u32[]{:S(2)}, u32[]{:S(2)}) collective-permute-start(bf16[2064,128]{1,0:T(8,128)(2,1)S(1)} %shard_map.22.refs_3_), channel_id=1, source_target_pairs={{0,1},{3,2},{4,5},{7,6},{8,9},{11,10},{12,13},{15,14},{16,17},{19,... | collective-permute-start | bytes 1585160 | tf_op jit(solution)/shard_map/ppermute | solution.py:396
  40.3 1.3 %collective-permute-start.11 = (bf16[2064,128]{1,0:T(8,128)(2,1)S(1)}, bf16[2064,128]{1,0:T(8,128)(2,1)S(1)}, u32[]{:S(2)}, u32[]{:S(2)}) collective-permute-start(bf16[2064,128]{1,0:T(8,128)(2,1)S(1)} %shard_map.23.refs_3_), channel_id=1, source_target_pairs={{1,0},{2,3},{5,4},{6,7},{9,8},{10,11},{13,12},{14,15},{17,16},{18,... | collective-permute-start | bytes 1585160 | tf_op jit(solution)/shard_map/ppermute | solution.py:396
  41.6 2.9 %collective-permute-done.4.refs_2_ = bf16[2064,128]{1,0:T(8,128)(2,1)S(1)} collective-permute-done((bf16[2064,128]{1,0:T(8,128)(2,1)S(1)}, bf16[2064,128]{1,0:T(8,128)(2,1)S(1)}, u32[]{:S(2)}, u32[]{:S(2)}) %collective-permute-start.4) | collective-permute-done | bytes 528416 | tf_op jit(solution)/shard_map/ppermute | solution.py:396
  45.2 1.4 %shard_map.25.refs_6_ = bf16[2064,128]{1,0:T(8,128)(2,1)S(1)} custom-call(bf16[1024,1024]{1,0:T(8,128)(2,1)S(1)} %bitcast.16, bf16[1024,1024]{1,0:T(8,128)(2,1)S(1)} %collective-permute-done.refs_1_, bf16[2064,128]{1,0:T(8,128)(2,1)S(1)} %shard_map.24.refs_2_), custom_call_target="tpu_custom_call" | custom-call | flops 6000000000 | bytes 6000000 | tf_op jit(solution)/shard_map/pallas_call | solution.py:366
  46.6 7.0 %collective-permute-start.7 = (bf16[2064,128]{1,0:T(8,128)(2,1)S(1)}, bf16[2064,128]{1,0:T(8,128)(2,1)S(1)}, u32[]{:S(2)}, u32[]{:S(2)}) collective-permute-start(bf16[2064,128]{1,0:T(8,128)(2,1)S(1)} %shard_map.25.refs_6_), channel_id=1, source_target_pairs={{0,1},{3,2},{4,5},{7,6},{8,9},{11,10},{12,13},{15,14},{16,17},{19,... | collective-permute-start | bytes 1585160 | tf_op jit(solution)/shard_map/ppermute | solution.py:396
  53.7 2.0 %collective-permute-done.11.refs_3_ = bf16[2064,128]{1,0:T(8,128)(2,1)S(1)} collective-permute-done((bf16[2064,128]{1,0:T(8,128)(2,1)S(1)}, bf16[2064,128]{1,0:T(8,128)(2,1)S(1)}, u32[]{:S(2)}, u32[]{:S(2)}) %collective-permute-start.11) | collective-permute-done | bytes 528416 | tf_op jit(solution)/shard_map/ppermute | solution.py:396
  55.6 2.1 %shard_map.26 = (bf16[16,128]{1,0:T(8,128)(2,1)S(1)}, f32[1,3,256,1024]{3,2,1,0:T(8,128)}) custom-call(bf16[1024,1024]{1,0:T(8,128)(2,1)S(1)} %bitcast.17, bf16[1552,128]{1,0:T(8,128)(2,1)S(1)} %collective-permute-done.10.refs_1_, bf16[2096,128]{1,0:T(8,128)(2,1)S(1)} %collective-permute-done.6.refs_2_, ...), custom_call_target="tpu_custom_call" | custom-call | flops 6000000000 | bytes 6000000 | tf_op jit(solution)/shard_map/pallas_call | solution.py:366
  58.5 1.0 %shard_map.28.refs_3_ = bf16[1552,128]{1,0:T(8,128)(2,1)S(1)} custom-call(bf16[1024,768]{1,0:T(8,128)(2,1)S(1)} %collective-permute-done.2.refs_0_.refs_2_, bf16[1024,1024]{1,0:T(8,128)(2,1)S(1)} %bitcast.19, bf16[2064,128]{1,0:T(8,128)(2,1)S(1)} %shard_map.27.refs_2_), custom_call_target="tpu_custom_call" | custom-call | flops 6000000000 | bytes 6000000 | tf_op jit(solution)/shard_map/pallas_call | solution.py:366
  59.5 6.0 %collective-permute-start.14 = (bf16[1552,128]{1,0:T(8,128)(2,1)S(1)}, bf16[1552,128]{1,0:T(8,128)(2,1)S(1)}, u32[]{:S(2)}, u32[]{:S(2)}) collective-permute-start(bf16[1552,128]{1,0:T(8,128)(2,1)S(1)} %shard_map.28.refs_3_), channel_id=1, source_target_pairs={{0,1},{3,2},{4,5},{7,6},{8,9},{11,10},{12,13},{15,14},{16,17},{19,... | collective-permute-start | bytes 1191944 | tf_op jit(solution)/shard_map/ppermute | solution.py:396
  65.6 1.3 %collective-permute-start.13 = (bf16[2064,128]{1,0:T(8,128)(2,1)S(1)}, bf16[2064,128]{1,0:T(8,128)(2,1)S(1)}, u32[]{:S(2)}, u32[]{:S(2)}) collective-permute-start(bf16[2064,128]{1,0:T(8,128)(2,1)S(1)} %shard_map.29.refs_3_), channel_id=1, source_target_pairs={{1,0},{2,3},{5,4},{6,7},{9,8},{10,11},{13,12},{14,15},{17,16},{18,... | collective-permute-start | bytes 1585160 | tf_op jit(solution)/shard_map/ppermute | solution.py:396
  66.9 0.7 collective-permute-start.12
  67.6 1.7 %shard_map.31.refs_3_ = bf16[3088,128]{1,0:T(8,128)(2,1)S(1)} custom-call(bf16[1024,1024]{1,0:T(8,128)(2,1)S(1)} %bitcast.22, bf16[1024,1024]{1,0:T(8,128)(2,1)S(1)} %collective-permute-done.refs_1_, bf16[1024,768]{1,0:T(8,128)(2,1)S(1)} %collective-permute-done.2.refs_0_.refs_2_, bf16[2064,128]{1,0:T(8,128)(2,1)S(1)} %shard_map.30.refs_3_), custom_call_target="tpu_custom_call" | custom-call | flops 6000000000 | bytes 6000000 | tf_op jit(solution)/shard_map/pallas_call | solution.py:366
  69.3 6.5 %collective-permute-start.16 = (bf16[3088,128]{1,0:T(8,128)(2,1)S(1)}, bf16[3088,128]{1,0:T(8,128)(2,1)S(1)}, u32[]{:S(2)}, u32[]{:S(2)}) collective-permute-start(bf16[3088,128]{1,0:T(8,128)(2,1)S(1)} %shard_map.31.refs_3_), channel_id=1, source_target_pairs={{0,1},{3,2},{4,5},{7,6},{8,9},{11,10},{12,13},{15,14},{16,17},{19,... | collective-permute-start | bytes 2371592 | tf_op jit(solution)/shard_map/ppermute | solution.py:396
  76.0 1.3 %collective-permute-start.18 = (bf16[2064,128]{1,0:T(8,128)(2,1)S(1)}, bf16[2064,128]{1,0:T(8,128)(2,1)S(1)}, u32[]{:S(2)}, u32[]{:S(2)}) collective-permute-start(bf16[2064,128]{1,0:T(8,128)(2,1)S(1)} %shard_map.32.refs_3_), channel_id=1, source_target_pairs={{1,8},{2,11},{5,12},{6,15},{9,0},{10,3},{13,4},{14,7},{17,24},{18,... | collective-permute-start | bytes 1585160 | tf_op jit(solution)/shard_map/ppermute | solution.py:396
  78.1 4.3 %collective-permute-done.13.refs_5_ = bf16[2064,128]{1,0:T(8,128)(2,1)S(1)} collective-permute-done((bf16[2064,128]{1,0:T(8,128)(2,1)S(1)}, bf16[2064,128]{1,0:T(8,128)(2,1)S(1)}, u32[]{:S(2)}, u32[]{:S(2)}) %collective-permute-start.13) | collective-permute-done | bytes 528416 | tf_op jit(solution)/shard_map/ppermute | solution.py:396
  82.4 1.4 %shard_map.34 = (f32[256,1024]{1,0:T(8,128)S(1)}, f32[256,1024]{1,0:T(8,128)S(1)}) custom-call(bf16[1024,1024]{1,0:T(8,128)(2,1)S(1)} %bitcast.25, bf16[1024,1024]{1,0:T(8,128)(2,1)S(1)} %collective-permute-done.refs_1_, bf16[1024,768]{1,0:T(8,128)(2,1)S(1)} %collective-permute-done.2.refs_0_.refs_2_, ...), custom_call_target="tpu_custom_call" | custom-call | flops 6000000000 | bytes 6000000 | tf_op jit(solution)/shard_map/pallas_call | solution.py:366
  83.9 7.3 %collective-permute-done.16.refs_1_ = bf16[3088,128]{1,0:T(8,128)(2,1)S(1)} collective-permute-done((bf16[3088,128]{1,0:T(8,128)(2,1)S(1)}, bf16[3088,128]{1,0:T(8,128)(2,1)S(1)}, u32[]{:S(2)}, u32[]{:S(2)}) %collective-permute-start.16) | collective-permute-done | bytes 790560 | tf_op jit(solution)/shard_map/ppermute | solution.py:396
  91.1 1.1 %shard_map.35 = (bf16[16,128]{1,0:T(8,128)(2,1)S(1)}, f32[1,3,256,1024]{3,2,1,0:T(8,128)}) custom-call(f32[256,1024]{1,0:T(8,128)S(1)} %get-tuple-element.20.refs_0_.refs_3_, bf16[3088,128]{1,0:T(8,128)(2,1)S(1)} %collective-permute-done.16.refs_1_, f32[1,3,256,1024]{3,2,1,0:T(8,128)} %get-tuple-element.21.refs_2_, ...), custom_call_target="tpu_custom_call", output_to_operand_aliasing={{1}: (2, {})} | custom-call | flops 6000000000 | bytes 6000000 | tf_op jit(solution)/shard_map/pallas_call | solution.py:366
  92.4 1.5 %shard_map.36 = (bf16[16,128]{1,0:T(8,128)(2,1)}, f32[1,3,256,1024]{3,2,1,0:T(8,128)}) custom-call(f32[256,1024]{1,0:T(8,128)S(1)} %get-tuple-element.19.refs_0_, bf16[3088,128]{1,0:T(8,128)(2,1)S(1)} %collective-permute-done.16.refs_1_, bf16[1552,128]{1,0:T(8,128)(2,1)S(1)} %collective-permute-done.17.refs_2_, ...), custom_call_target="tpu_custom_call", output_to_operand_aliasing={{1}: (4, {})} | custom-call | flops 6000000000 | bytes 6000000 | tf_op jit(solution)/shard_map/pallas_call | solution.py:366
  (28 shorter events, 4.0 us)
Async XLA Ops:
  0.0 26.2 %collective-permute-start = (bf16[1024,1024]{1,0:T(8,128)(2,1)}, bf16[1024,1024]{1,0:T(8,128)(2,1)S(1)}, u32[]{:S(2)}, u32[]{:S(2)}) collective-permute-start(bf16[1024,1024]{1,0:T(8,128)(2,1)} %bitcast.1), channel_id=1, source_target_pairs={{0,12},{4,0},{8,4},{12,8},{1,13},{5,1},{9,5},{13,9},{2,14},{6,2},{... | collective-permute-start | bytes 6291464 | tf_op jit(solution)/shard_map/ppermute | solution.py:26
  2.4 1.6 %copy-start = (bf16[1,1024,1024]{2,1,0:T(8,128)(2,1)S(1)}, bf16[1,1024,1024]{2,1,0:T(8,128)(2,1)}, u32[]{:S(2)}) copy-start(bf16[1,1024,1024]{2,1,0:T(8,128)(2,1)} %param.1) | copy-start | bytes 6291460
  5.2 14.7 %collective-permute-start.1 = (bf16[2064,128]{1,0:T(8,128)(2,1)S(1)}, bf16[2064,128]{1,0:T(8,128)(2,1)S(1)}, u32[]{:S(2)}, u32[]{:S(2)}) collective-permute-start(bf16[2064,128]{1,0:T(8,128)(2,1)S(1)} %shard_map.17.refs_2_), channel_id=1, source_target_pairs={{0,1},{3,2},{4,5},{7,6},{8,9},{11,10},{12,13},{15,14},{16,17},{19,... | collective-permute-start | bytes 1585160 | tf_op jit(solution)/shard_map/ppermute | solution.py:396
  8.9 23.1 %collective-permute-start.6 = (bf16[2096,128]{1,0:T(8,128)(2,1)S(1)}, bf16[2096,128]{1,0:T(8,128)(2,1)S(1)}, u32[]{:S(2)}, u32[]{:S(2)}) collective-permute-start(bf16[2096,128]{1,0:T(8,128)(2,1)S(1)} %shard_map.18.refs_3_), channel_id=1, source_target_pairs={{0,1},{3,2},{4,5},{7,6},{8,9},{11,10},{12,13},{15,14},{16,17},{19,... | collective-permute-start | bytes 1609736 | tf_op jit(solution)/shard_map/ppermute | solution.py:396
  19.9 20.4 %collective-permute-start.5 = (bf16[2064,128]{1,0:T(8,128)(2,1)S(1)}, bf16[2064,128]{1,0:T(8,128)(2,1)S(1)}, u32[]{:S(2)}, u32[]{:S(2)}) collective-permute-start(bf16[2064,128]{1,0:T(8,128)(2,1)S(1)} %shard_map.19.refs_2_), channel_id=1, source_target_pairs={{1,2},{2,1},{5,6},{6,5},{9,10},{10,9},{13,14},{14,13},{17,18},{18,... | collective-permute-start | bytes 1585160 | tf_op jit(solution)/shard_map/ppermute | solution.py:396
  27.6 8.5 %collective-permute-start.3 = (bf16[1024,256]{1,0:T(8,128)(2,1)S(1)}, bf16[1024,256]{1,0:T(8,128)(2,1)S(1)}, u32[]{:S(2)}, u32[]{:S(2)}) collective-permute-start(bf16[1024,256]{1,0:T(8,128)(2,1)S(1)} %get-tuple-element.16), channel_id=1, source_target_pairs={{0,12},{4,0},{8,4},{12,8},{1,13},{5,1},{9,5},{13,9},{2,14},{6,2},{... | collective-permute-start | bytes 1572872 | tf_op jit(solution)/shard_map/ppermute | solution.py:26
  29.5 15.0 %collective-permute-start.4 = (bf16[2064,128]{1,0:T(8,128)(2,1)S(1)}, bf16[2064,128]{1,0:T(8,128)(2,1)S(1)}, u32[]{:S(2)}, u32[]{:S(2)}) collective-permute-start(bf16[2064,128]{1,0:T(8,128)(2,1)S(1)} %get-tuple-element.17.refs_3_), channel_id=1, source_target_pairs={{0,1},{3,2},{4,5},{7,6},{8,9},{11,10},{12,13},{15,14},{16,17},{19,... | collective-permute-start | bytes 1585160 | tf_op jit(solution)/shard_map/ppermute | solution.py:396
  32.1 14.5 %collective-permute-start.10 = (bf16[1552,128]{1,0:T(8,128)(2,1)S(1)}, bf16[1552,128]{1,0:T(8,128)(2,1)S(1)}, u32[]{:S(2)}, u32[]{:S(2)}) collective-permute-start(bf16[1552,128]{1,0:T(8,128)(2,1)S(1)} %shard_map.21.refs_2_), channel_id=1, source_target_pairs={{1,2},{2,1},{5,6},{6,5},{9,10},{10,9},{13,14},{14,13},{17,18},{18,... | collective-permute-start | bytes 1191944 | tf_op jit(solution)/shard_map/ppermute | solution.py:396
  32.8 25.7 %collective-permute-start.2 = (bf16[1024,768]{1,0:T(8,128)(2,1)S(1)}, bf16[1024,768]{1,0:T(8,128)(2,1)S(1)}, u32[]{:S(2)}, u32[]{:S(2)}) collective-permute-start(bf16[1024,768]{1,0:T(8,128)(2,1)S(1)} %get-tuple-element.15), channel_id=1, source_target_pairs={{0,12},{4,0},{8,4},{12,8},{1,13},{5,1},{9,5},{13,9},{2,14},{6,2},{... | collective-permute-start | bytes 4718600 | tf_op jit(solution)/shard_map/ppermute | solution.py:26
  37.4 20.4 %collective-permute-start.9 = (bf16[2064,128]{1,0:T(8,128)(2,1)S(1)}, bf16[2064,128]{1,0:T(8,128)(2,1)S(1)}, u32[]{:S(2)}, u32[]{:S(2)}) collective-permute-start(bf16[2064,128]{1,0:T(8,128)(2,1)S(1)} %shard_map.22.refs_3_), channel_id=1, source_target_pairs={{0,1},{3,2},{4,5},{7,6},{8,9},{11,10},{12,13},{15,14},{16,17},{19,... | collective-permute-start | bytes 1585160 | tf_op jit(solution)/shard_map/ppermute | solution.py:396
  40.3 15.3 %collective-permute-start.11 = (bf16[2064,128]{1,0:T(8,128)(2,1)S(1)}, bf16[2064,128]{1,0:T(8,128)(2,1)S(1)}, u32[]{:S(2)}, u32[]{:S(2)}) collective-permute-start(bf16[2064,128]{1,0:T(8,128)(2,1)S(1)} %shard_map.23.refs_3_), channel_id=1, source_target_pairs={{1,0},{2,3},{5,4},{6,7},{9,8},{10,11},{13,12},{14,15},{17,16},{18,... | collective-permute-start | bytes 1585160 | tf_op jit(solution)/shard_map/ppermute | solution.py:396
  44.5 21.1 %collective-permute-start.8 = (bf16[2064,128]{1,0:T(8,128)(2,1)S(1)}, bf16[2064,128]{1,0:T(8,128)(2,1)S(1)}, u32[]{:S(2)}, u32[]{:S(2)}) collective-permute-start(bf16[2064,128]{1,0:T(8,128)(2,1)S(1)} %shard_map.24.refs_2_), channel_id=1, source_target_pairs={{1,2},{2,1},{5,6},{6,5},{9,10},{10,9},{13,14},{14,13},{17,18},{18,... | collective-permute-start | bytes 1585160 | tf_op jit(solution)/shard_map/ppermute | solution.py:396
  46.6 20.3 %collective-permute-start.7 = (bf16[2064,128]{1,0:T(8,128)(2,1)S(1)}, bf16[2064,128]{1,0:T(8,128)(2,1)S(1)}, u32[]{:S(2)}, u32[]{:S(2)}) collective-permute-start(bf16[2064,128]{1,0:T(8,128)(2,1)S(1)} %shard_map.25.refs_6_), channel_id=1, source_target_pairs={{0,1},{3,2},{4,5},{7,6},{8,9},{11,10},{12,13},{15,14},{16,17},{19,... | collective-permute-start | bytes 1585160 | tf_op jit(solution)/shard_map/ppermute | solution.py:396
  57.8 18.0 %collective-permute-start.15 = (bf16[2064,128]{1,0:T(8,128)(2,1)S(1)}, bf16[2064,128]{1,0:T(8,128)(2,1)S(1)}, u32[]{:S(2)}, u32[]{:S(2)}) collective-permute-start(bf16[2064,128]{1,0:T(8,128)(2,1)S(1)} %shard_map.27.refs_2_), channel_id=1, source_target_pairs={{1,2},{2,1},{5,6},{6,5},{9,10},{10,9},{13,14},{14,13},{17,18},{18,... | collective-permute-start | bytes 1585160 | tf_op jit(solution)/shard_map/ppermute | solution.py:396
  59.5 17.9 %collective-permute-start.14 = (bf16[1552,128]{1,0:T(8,128)(2,1)S(1)}, bf16[1552,128]{1,0:T(8,128)(2,1)S(1)}, u32[]{:S(2)}, u32[]{:S(2)}) collective-permute-start(bf16[1552,128]{1,0:T(8,128)(2,1)S(1)} %shard_map.28.refs_3_), channel_id=1, source_target_pairs={{0,1},{3,2},{4,5},{7,6},{8,9},{11,10},{12,13},{15,14},{16,17},{19,... | collective-permute-start | bytes 1191944 | tf_op jit(solution)/shard_map/ppermute | solution.py:396
  65.6 16.8 %collective-permute-start.13 = (bf16[2064,128]{1,0:T(8,128)(2,1)S(1)}, bf16[2064,128]{1,0:T(8,128)(2,1)S(1)}, u32[]{:S(2)}, u32[]{:S(2)}) collective-permute-start(bf16[2064,128]{1,0:T(8,128)(2,1)S(1)} %shard_map.29.refs_3_), channel_id=1, source_target_pairs={{1,0},{2,3},{5,4},{6,7},{9,8},{10,11},{13,12},{14,15},{17,16},{18,... | collective-permute-start | bytes 1585160 | tf_op jit(solution)/shard_map/ppermute | solution.py:396
  66.9 11.2 %collective-permute-start.12 = (bf16[2064,128]{1,0:T(8,128)(2,1)S(1)}, bf16[2064,128]{1,0:T(8,128)(2,1)S(1)}, u32[]{:S(2)}, u32[]{:S(2)}) collective-permute-start(bf16[2064,128]{1,0:T(8,128)(2,1)S(1)} %shard_map.30.refs_3_), channel_id=1, source_target_pairs={{1,2},{2,1},{5,6},{6,5},{9,10},{10,9},{13,14},{14,13},{17,18},{18,... | collective-permute-start | bytes 1585160 | tf_op jit(solution)/shard_map/ppermute | solution.py:396
  69.3 21.8 %collective-permute-start.16 = (bf16[3088,128]{1,0:T(8,128)(2,1)S(1)}, bf16[3088,128]{1,0:T(8,128)(2,1)S(1)}, u32[]{:S(2)}, u32[]{:S(2)}) collective-permute-start(bf16[3088,128]{1,0:T(8,128)(2,1)S(1)} %shard_map.31.refs_3_), channel_id=1, source_target_pairs={{0,1},{3,2},{4,5},{7,6},{8,9},{11,10},{12,13},{15,14},{16,17},{19,... | collective-permute-start | bytes 2371592 | tf_op jit(solution)/shard_map/ppermute | solution.py:396
  76.0 16.4 %collective-permute-start.18 = (bf16[2064,128]{1,0:T(8,128)(2,1)S(1)}, bf16[2064,128]{1,0:T(8,128)(2,1)S(1)}, u32[]{:S(2)}, u32[]{:S(2)}) collective-permute-start(bf16[2064,128]{1,0:T(8,128)(2,1)S(1)} %shard_map.32.refs_3_), channel_id=1, source_target_pairs={{1,8},{2,11},{5,12},{6,15},{9,0},{10,3},{13,4},{14,7},{17,24},{18,... | collective-permute-start | bytes 1585160 | tf_op jit(solution)/shard_map/ppermute | solution.py:396
  77.4 15.0 %collective-permute-start.17 = (bf16[1552,128]{1,0:T(8,128)(2,1)S(1)}, bf16[1552,128]{1,0:T(8,128)(2,1)S(1)}, u32[]{:S(2)}, u32[]{:S(2)}) collective-permute-start(bf16[1552,128]{1,0:T(8,128)(2,1)S(1)} %shard_map.33.refs_9_), channel_id=1, source_target_pairs={{1,10},{2,9},{5,14},{6,13},{9,2},{10,1},{13,6},{14,5},{17,26},{18,... | collective-permute-start | bytes 1191944 | tf_op jit(solution)/shard_map/ppermute | solution.py:396

commit v5 on v4

--- a/solution.py
+++ b/solution.py
@@ -16,7 +16,7 @@
 TAIL = 16
 SPREAD = 13777.0
 SMALLEST = 1e-30
-COSTS = (6_000_000_000,) * 20
+COSTS = (6_000_000_000,) * 22
 VMEM_BYTES = 24 * 1024 * 1024
 
 
@@ -182,13 +182,16 @@
         )
 
 
-def pass_on_kernel(row, count, inverse, left_ref, right_ref, message_ref, far_ref, rest_ref):
-    rows = right_ref.shape[1] // 4
-    upper, inner = fold()
-    far_ref[...] = block_of(right_ref, upper, FAR, rows)
+def far_part_kernel(inverse, keys_ref, part_ref):
+    upper, inner = fold()
+    part_ref[...] = block_of(keys_ref, upper, FAR, keys_ref.shape[1] // 4)
+
+
+def rest_part_kernel(inverse, keys_ref, part_ref):
+    rows = keys_ref.shape[1] // 4
+    upper, inner = fold()
     rest_at = pl.multiple_of(jnp.where(upper, rows, 0), rows)
-    rest_ref[...] = right_ref[:, pl.ds(rest_at, 3 * rows)]
-    send_kernel(row, count, inverse, left_ref, right_ref, message_ref)
+    part_ref[...] = keys_ref[:, pl.ds(rest_at, 3 * rows)]
 
 
 def near_kernel(inverse, left_ref, plain_ref, folded_ref, message_ref):
@@ -317,43 +320,48 @@
             folded_out[:, block(column)] = sums
 
 
-def last_plain_kernel(inverse, sums_ref, near_ref, token_ref, out_ref):
-    rows = sums_ref.shape[0]
-    upper, inner = fold()
-    token_ref[...] = jnp.zeros_like(token_ref)
-
-    @pl.when(jnp.logical_not(inner))
-    def _():
-        for column in range(4):
-            put(out_ref, upper, column, rows, sums_ref[:, column * rows : (column + 1) * rows])
-
-    @pl.when(inner)
-    def _():
-        for column in range(4):
-            sums = sums_ref[:, column * rows : (column + 1) * rows]
-            put(out_ref, upper, column, rows, sums + read_block(near_ref, column, rows))
-
-
-def last_folded_kernel(inverse, sums_ref, near_ref, next_ref, back_ref, token_ref, out_ref):
-    rows = sums_ref.shape[0]
-    upper, inner = fold()
-    token_ref[...] = jnp.zeros_like(token_ref)
-
-    @pl.when(jnp.logical_not(inner))
-    def _():
-        for column in range(4):
-            sums = sums_ref[:, column * rows : (column + 1) * rows]
-            put(out_ref, upper, column, rows, sums + read_block(back_ref, column, rows))
-
-    @pl.when(inner)
-    def _():
-        for column in range(4):
-            sums = sums_ref[:, column * rows : (column + 1) * rows]
+def plain_tile_kernel(inverse, plain_ref, folded_ref, near_ref, back_ref, sums_ref, out_ref):
+    rows = plain_ref.shape[0]
+    upper, inner = fold()
+
+    def block(column):
+        return slice(column * rows, (column + 1) * rows)
+
+    @pl.when(jnp.logical_not(inner))
+    def _():
+        for column in range(4):
+            put(out_ref, upper, column, rows, plain_ref[:, block(column)])
+            sums_ref[:, block(column)] = folded_ref[:, block(column)] + read_block(back_ref, column, rows)
+
+    @pl.when(inner)
+    def _():
+        for column in range(4):
+            sums = plain_ref[:, block(column)] + read_block(near_ref, column, rows)
+            put(out_ref, upper, column, rows, sums)
+            sums = folded_ref[:, block(column)]
             if column < 2:
                 sums = sums + read_block(near_ref, 4 + column, rows)
-            if column > 0:
-                sums = sums + read_block(next_ref, 3 - column, rows)
-            put(out_ref, upper, column, rows, sums)
+            sums_ref[:, block(column)] = sums
+
+
+def folded_tile_kernel(inverse, sums_ref, next_ref, token_ref, out_ref):
+    rows = sums_ref.shape[0]
+    upper, inner = fold()
+    token_ref[...] = jnp.zeros_like(token_ref)
+
+    def sums(column):
+        return sums_ref[:, column * rows : (column + 1) * rows]
+
+    @pl.when(jnp.logical_not(inner))
+    def _():
+        for column in range(4):
+            put(out_ref, upper, column, rows, sums(column))
+
+    @pl.when(inner)
+    def _():
+        put(out_ref, upper, 0, rows, sums(0))
+        for column in range(1, 4):
+            put(out_ref, upper, column, rows, sums(column) + read_block(next_ref, 3 - column, rows))
 
 
 def ordered(body, count, held, *refs):
@@ -395,9 +403,9 @@
         ]
         return lax.ppermute(message, ("layer", "tok"), pairs)
 
-    def send(left, right, row, count):
+    def send(left, right, row, count, held=()):
         body = functools.partial(send_kernel, row, count)
-        return hop(run(body, (left, right), message_shape(count, rows)), OUTER_TO_INNER)
+        return hop(run(body, (left, right), message_shape(count, rows), held), OUTER_TO_INNER)
 
     def cross(left, right, row, count, arrived, layers=0):
         body = functools.partial(cross_kernel, row, count)
@@ -411,22 +419,21 @@
     tile = jax.ShapeDtypeStruct((1, 3, rows, width), jnp.float32)
     token = jax.ShapeDtypeStruct((TAIL, HALF), jnp.bfloat16)
 
-    def write_tile(distance, out, body, operands):
+    def write_tile(distance, out, body, operands, beside=token):
         options = {}
         if out is not None:
             options = {"held": (out,), "input_output_aliases": {len(operands): 1}}
-        _, out = run(
+        return run(
             body,
             operands,
-            [token, tile],
+            [beside, tile],
             grid=(1,),
             out_specs=[
-                pl.BlockSpec((TAIL, HALF), lambda step: (0, 0)),
+                pl.BlockSpec(beside.shape, lambda step: (0, 0)),
                 pl.BlockSpec((1, 1, rows, width), lambda step: (0, distance, 0, 0)),
             ],
             **options,
         )
-        return out
 
 
     def part_of_keys(count):
@@ -437,30 +444,25 @@
     rest_0 = run(rest_kernel, (own_keys, own_keys), message_shape(4, rows, 1))
     rest_0 = hop(rest_0, OUTER_TO_INNER)
     far_across_0 = cross(own_keys, own_keys, FAR, 4, far_0)
-    far_1, far_part, rest_part = run(
-        functools.partial(pass_on_kernel, FAR, 4),
-        (own_keys, second_keys),
-        [message_shape(4, rows), part_of_keys(1), part_of_keys(3)],
-    )
-    far_1 = hop(far_1, OUTER_TO_INNER)
-    far_part = shifted(far_part, "layer", -1)
-    rest_part = shifted(rest_part, "layer", -1)
+    far_1 = send(own_keys, second_keys, FAR, 4)
+    far_part = shifted(run(far_part_kernel, (second_keys,), part_of_keys(1)), "layer", -1)
     next_across_0 = cross(own_keys, own_keys, NEXT, 3, rest_0)
     far_2 = send(far_part, own_keys, FAR, 4)
+    rest_part = shifted(run(rest_part_kernel, (second_keys,), part_of_keys(3)), "layer", -1)
+    far_across_1 = cross(own_keys, second_keys, FAR, 4, far_1)
+    next_1 = send(own_keys, second_keys, NEXT, 4, held=(next_across_0,))
     back_0 = back(own_keys, own_keys, far_across_0)
-    far_across_1 = cross(own_keys, second_keys, FAR, 4, far_1)
-    next_1 = send(own_keys, second_keys, NEXT, 4)
-    out = write_tile(
-        0, None, finish_kernel, (own_keys, next_across_0, rest_0, back_0, far_0, far_across_0)
-    )
     far_across_2 = cross(far_part, own_keys, FAR, 4, far_2)
     next_2 = send(rest_part, own_keys, NEXT, 3)
     back_1 = back(own_keys, second_keys, far_across_1)
+    near = run(near_kernel, (own_keys, second_keys, rest_part), message_shape(6, rows), (back_0,))
+    near = hop(near, OUTER_TO_INNER)
     next_across_1 = cross(own_keys, second_keys, NEXT, 4, next_1)
-    near = run(near_kernel, (own_keys, second_keys, rest_part), message_shape(6, rows))
-    near = hop(near, OUTER_TO_INNER)
     back_2 = back(rest_part, own_keys, far_across_2, 2)
     next_across_2 = cross(rest_part, own_keys, NEXT, 3, next_2, 2)
+    _, out = write_tile(
+        0, None, finish_kernel, (own_keys, next_across_0, rest_0, back_0, far_0, far_across_0)
+    )
     part = jax.ShapeDtypeStruct((rows, width), jnp.float32)
     turned = (far_2, next_2, far_across_2)
     parts = run(
@@ -468,8 +470,9 @@
         (own_keys, second_keys, rest_part, far_part, next_across_1, back_1, *turned),
         [part, part],
     )
-    out = write_tile(1, out, last_plain_kernel, (parts[0], near))
-    return write_tile(2, out, last_folded_kernel, (parts[1], near, next_across_2, back_2))
+    sums, out = write_tile(1, out, plain_tile_kernel, (*parts, near, back_2), part)
+    _, out = write_tile(2, out, folded_tile_kernel, (sums, next_across_2))
+    return out
 
 
 def per_device(keys):

time: 95 us -> 94.7 us (level)
  starting transfers between devices: 40.9 us -> 30.9 us
  waiting for transfers between devices: 35.3 us -> 44.4 us
    ppermute x16, starting transfers between devices: 36.6 us -> 24.7 us  [hop(): return lax.ppermute(message, ('layer', 'tok'), pairs)]
    ppermute x3, waiting for transfers between devices: 8.96 us -> 18.6 us  [shifted(): return lax.ppermute(value, axis, pairs)]
    ppermute x3, starting transfers between devices: 4.28 us -> 6.2 us  [shifted(): return lax.ppermute(value, axis, pairs)]
    pallas_call x20 -> x22, Pallas kernels: 15.8 us -> 15.9 us  [call(): pl.pallas_call(functools.partial(ordered, body, len(operands), len(held))...]
  transfers between devices with their start and end apart: 19 -> 19, of which waited for: 8 -> 9; matrix products, arithmetic and copies ran while one was open for 0% -> 0% of each run, Pallas kernels for 15% -> 16%
where the time goes in v5:
time: 94.7 us; the launch traced here: 93.1 us
  waiting for transfers between devices  44.4 us (47%)
  starting transfers between devices  30.9 us (33%)
  Pallas kernels  15.9 us (17%)
  local copies, waits for them, and re-layouts  1.63 us (2%)
    ppermute x16, waiting for transfers between devices, hop(): return lax.ppermute(message, ('layer', 'tok'), pairs)  25.9 us
    ppermute x16, starting transfers between devices, hop(): return lax.ppermute(message, ('layer', 'tok'), pairs)  24.7 us
    ppermute x3, waiting for transfers between devices, shifted(): return lax.ppermute(value, axis, pairs)  18.6 us
    pallas_call x22, Pallas kernels, call(): pl.pallas_call(functools.partial(ordered, body, len(operands), len(held))...  15.9 us
    ppermute x3, starting transfers between devices, shifted(): return lax.ppermute(value, axis, pairs)  6.2 us
  transfers between devices with their start and end apart: 19, of which 9 were waited for; matrix products, arithmetic and copies ran while one was open for 0% of the time, Pallas kernels for 16%

profile of v5, /device:TPU:0, one launch (start us, length us, event | category | flops | bytes accessed | tf_op | source)
XLA Modules:
  0.0 93.1 jit_solution(3261018343447548379)
XLA Ops:
  0.0 2.4 %collective-permute-start = (bf16[1024,1024]{1,0:T(8,128)(2,1)}, bf16[1024,1024]{1,0:T(8,128)(2,1)S(1)}, u32[]{:S(2)}, u32[]{:S(2)}) collective-permute-start(bf16[1024,1024]{1,0:T(8,128)(2,1)} %bitcast.1), channel_id=1, source_target_pairs={{0,12},{4,0},{8,4},{12,8},{1,13},{5,1},{9,5},{13,9},{2,14},{6,2},{... | collective-permute-start | bytes 6291464 | tf_op jit(solution)/shard_map/ppermute | solution.py:26
  2.4 1.6 %copy-done = bf16[1,1024,1024]{2,1,0:T(8,128)(2,1)S(1)} copy-done((bf16[1,1024,1024]{2,1,0:T(8,128)(2,1)S(1)}, bf16[1,1024,1024]{2,1,0:T(8,128)(2,1)}, u32[]{:S(2)}) %copy-start) | copy-done | bytes 2097176
  4.0 1.2 %shard_map.17.refs_2_ = bf16[2064,128]{1,0:T(8,128)(2,1)S(1)} custom-call(bf16[1024,1024]{1,0:T(8,128)(2,1)S(1)} %bitcast.2, bf16[1024,1024]{1,0:T(8,128)(2,1)S(1)} %bitcast.3, bf16[1024,1024]{1,0:T(8,128)(2,1)S(1)} %bitcast.4), custom_call_target="tpu_custom_call" | custom-call | flops 6000000000 | bytes 6000000 | tf_op jit(solution)/shard_map/pallas_call | solution.py:374
  5.2 2.3 %collective-permute-start.1 = (bf16[2064,128]{1,0:T(8,128)(2,1)S(1)}, bf16[2064,128]{1,0:T(8,128)(2,1)S(1)}, u32[]{:S(2)}, u32[]{:S(2)}) collective-permute-start(bf16[2064,128]{1,0:T(8,128)(2,1)S(1)} %shard_map.17.refs_2_), channel_id=1, source_target_pairs={{0,1},{3,2},{4,5},{7,6},{8,9},{11,10},{12,13},{15,14},{16,17},{19,... | collective-permute-start | bytes 1585160 | tf_op jit(solution)/shard_map/ppermute | solution.py:404
  7.5 1.4 %shard_map.18.refs_3_ = bf16[2096,128]{1,0:T(8,128)(2,1)S(1)} custom-call(bf16[1024,1024]{1,0:T(8,128)(2,1)S(1)} %bitcast.5, bf16[1024,1024]{1,0:T(8,128)(2,1)S(1)} %bitcast.6, bf16[2064,128]{1,0:T(8,128)(2,1)S(1)} %shard_map.17.refs_2_), custom_call_target="tpu_custom_call" | custom-call | flops 6000000000 | bytes 6000000 | tf_op jit(solution)/shard_map/pallas_call | solution.py:374
  8.9 1.3 %collective-permute-start.3 = (bf16[2096,128]{1,0:T(8,128)(2,1)S(1)}, bf16[2096,128]{1,0:T(8,128)(2,1)S(1)}, u32[]{:S(2)}, u32[]{:S(2)}) collective-permute-start(bf16[2096,128]{1,0:T(8,128)(2,1)S(1)} %shard_map.18.refs_3_), channel_id=1, source_target_pairs={{0,1},{3,2},{4,5},{7,6},{8,9},{11,10},{12,13},{15,14},{16,17},{19,... | collective-permute-start | bytes 1609736 | tf_op jit(solution)/shard_map/ppermute | solution.py:404
  10.3 9.7 %collective-permute-done.1.refs_2_.refs_4_ = bf16[2064,128]{1,0:T(8,128)(2,1)S(1)} collective-permute-done((bf16[2064,128]{1,0:T(8,128)(2,1)S(1)}, bf16[2064,128]{1,0:T(8,128)(2,1)S(1)}, u32[]{:S(2)}, u32[]{:S(2)}) %collective-permute-start.1) | collective-permute-done | bytes 528416 | tf_op jit(solution)/shard_map/ppermute | solution.py:404
  20.6 5.6 %collective-permute-done.refs_1_.refs_0_ = bf16[1024,1024]{1,0:T(8,128)(2,1)S(1)} collective-permute-done((bf16[1024,1024]{1,0:T(8,128)(2,1)}, bf16[1024,1024]{1,0:T(8,128)(2,1)S(1)}, u32[]{:S(2)}, u32[]{:S(2)}) %collective-permute-start) | collective-permute-done | bytes 2097184 | tf_op jit(solution)/shard_map/ppermute | solution.py:26
  26.2 1.2 %shard_map.20.refs_1_ = bf16[2064,128]{1,0:T(8,128)(2,1)S(1)} custom-call(bf16[1024,1024]{1,0:T(8,128)(2,1)S(1)} %bitcast.9, bf16[1024,1024]{1,0:T(8,128)(2,1)S(1)} %collective-permute-done.refs_1_.refs_0_, bf16[2064,128]{1,0:T(8,128)(2,1)S(1)} %shard_map.19.refs_2_), custom_call_target="tpu_custom_call" | custom-call | flops 6000000000 | bytes 6000000 | tf_op jit(solution)/shard_map/pallas_call | solution.py:374
  27.5 2.4 %collective-permute-start.6 = (bf16[2064,128]{1,0:T(8,128)(2,1)S(1)}, bf16[2064,128]{1,0:T(8,128)(2,1)S(1)}, u32[]{:S(2)}, u32[]{:S(2)}) collective-permute-start(bf16[2064,128]{1,0:T(8,128)(2,1)S(1)} %shard_map.20.refs_1_), channel_id=1, source_target_pairs={{0,1},{3,2},{4,5},{7,6},{8,9},{11,10},{12,13},{15,14},{16,17},{19,... | collective-permute-start | bytes 1585160 | tf_op jit(solution)/shard_map/ppermute | solution.py:404
  30.0 1.9 %collective-permute-start.2 = (bf16[1024,256]{1,0:T(8,128)(2,1)S(1)}, bf16[1024,256]{1,0:T(8,128)(2,1)S(1)}, u32[]{:S(2)}, u32[]{:S(2)}) collective-permute-start(bf16[1024,256]{1,0:T(8,128)(2,1)S(1)} %shard_map.21.refs_3_), channel_id=1, source_target_pairs={{0,12},{4,0},{8,4},{12,8},{1,13},{5,1},{9,5},{13,9},{2,14},{6,2},{... | collective-permute-start | bytes 1572872 | tf_op jit(solution)/shard_map/ppermute | solution.py:26
  32.5 6.0 %collective-permute-done.2.refs_0_.refs_3_ = bf16[1024,256]{1,0:T(8,128)(2,1)S(1)} collective-permute-done((bf16[1024,256]{1,0:T(8,128)(2,1)S(1)}, bf16[1024,256]{1,0:T(8,128)(2,1)S(1)}, u32[]{:S(2)}, u32[]{:S(2)}) %collective-permute-start.2) | collective-permute-done | bytes 524320 | tf_op jit(solution)/shard_map/ppermute | solution.py:26
  38.5 1.2 %shard_map.23.refs_1_ = bf16[2064,128]{1,0:T(8,128)(2,1)S(1)} custom-call(bf16[1024,256]{1,0:T(8,128)(2,1)S(1)} %collective-permute-done.2.refs_0_.refs_3_, bf16[1024,1024]{1,0:T(8,128)(2,1)S(1)} %bitcast.12, bf16[1552,128]{1,0:T(8,128)(2,1)S(1)} %shard_map.22.refs_2_), custom_call_target="tpu_custom_call" | custom-call | flops 6000000000 | bytes 6000000 | tf_op jit(solution)/shard_map/pallas_call | solution.py:374
  39.8 1.3 %collective-permute-start.11 = (bf16[2064,128]{1,0:T(8,128)(2,1)S(1)}, bf16[2064,128]{1,0:T(8,128)(2,1)S(1)}, u32[]{:S(2)}, u32[]{:S(2)}) collective-permute-start(bf16[2064,128]{1,0:T(8,128)(2,1)S(1)} %shard_map.23.refs_1_), channel_id=1, source_target_pairs={{0,1},{3,2},{4,5},{7,6},{8,9},{11,10},{12,13},{15,14},{16,17},{19,... | collective-permute-start | bytes 1585160 | tf_op jit(solution)/shard_map/ppermute | solution.py:404
  41.2 2.0 %collective-permute-start.4 = (bf16[1024,768]{1,0:T(8,128)(2,1)S(1)}, bf16[1024,768]{1,0:T(8,128)(2,1)S(1)}, u32[]{:S(2)}, u32[]{:S(2)}) collective-permute-start(bf16[1024,768]{1,0:T(8,128)(2,1)S(1)} %shard_map.24.refs_3_), channel_id=1, source_target_pairs={{0,12},{4,0},{8,4},{12,8},{1,13},{5,1},{9,5},{13,9},{2,14},{6,2},{... | collective-permute-start | bytes 4718600 | tf_op jit(solution)/shard_map/ppermute | solution.py:26
  43.9 1.2 %shard_map.26.refs_3_ = bf16[2064,128]{1,0:T(8,128)(2,1)S(1)} custom-call(bf16[1024,1024]{1,0:T(8,128)(2,1)S(1)} %bitcast.14, bf16[1024,1024]{1,0:T(8,128)(2,1)S(1)} %collective-permute-done.refs_1_.refs_0_, bf16[1552,128]{1,0:T(8,128)(2,1)S(1)} %collective-permute-done.5.refs_2_.refs_1_, bf16[2064,128]{1,0:T(8,128)(2,1)S(1)} %shard_map.25.refs_3_), custom_call_target="tpu_custom_call" | custom-call | flops 6000000000 | bytes 6000000 | tf_op jit(solution)/shard_map/pallas_call | solution.py:374
  45.1 6.7 %collective-permute-start.7 = (bf16[2064,128]{1,0:T(8,128)(2,1)S(1)}, bf16[2064,128]{1,0:T(8,128)(2,1)S(1)}, u32[]{:S(2)}, u32[]{:S(2)}) collective-permute-start(bf16[2064,128]{1,0:T(8,128)(2,1)S(1)} %shard_map.26.refs_3_), channel_id=1, source_target_pairs={{0,1},{3,2},{4,5},{7,6},{8,9},{11,10},{12,13},{15,14},{16,17},{19,... | collective-permute-start | bytes 1585160 | tf_op jit(solution)/shard_map/ppermute | solution.py:404
  52.1 1.3 %collective-permute-start.9 = (bf16[2064,128]{1,0:T(8,128)(2,1)S(1)}, bf16[2064,128]{1,0:T(8,128)(2,1)S(1)}, u32[]{:S(2)}, u32[]{:S(2)}) collective-permute-start(bf16[2064,128]{1,0:T(8,128)(2,1)S(1)} %shard_map.27.refs_3_), channel_id=1, source_target_pairs={{1,0},{2,3},{5,4},{6,7},{9,8},{10,11},{13,12},{14,15},{17,16},{18,... | collective-permute-start | bytes 1585160 | tf_op jit(solution)/shard_map/ppermute | solution.py:404
  54.2 6.9 %collective-permute-done.4.refs_0_.refs_2_ = bf16[1024,768]{1,0:T(8,128)(2,1)S(1)} collective-permute-done((bf16[1024,768]{1,0:T(8,128)(2,1)S(1)}, bf16[1024,768]{1,0:T(8,128)(2,1)S(1)}, u32[]{:S(2)}, u32[]{:S(2)}) %collective-permute-start.4) | collective-permute-done | bytes 1572896 | tf_op jit(solution)/shard_map/ppermute | solution.py:26
  61.1 1.0 %shard_map.29.refs_3_ = bf16[1552,128]{1,0:T(8,128)(2,1)S(1)} custom-call(bf16[1024,768]{1,0:T(8,128)(2,1)S(1)} %collective-permute-done.4.refs_0_.refs_2_, bf16[1024,1024]{1,0:T(8,128)(2,1)S(1)} %bitcast.18, bf16[2064,128]{1,0:T(8,128)(2,1)S(1)} %shard_map.28.refs_2_), custom_call_target="tpu_custom_call" | custom-call | flops 6000000000 | bytes 6000000 | tf_op jit(solution)/shard_map/pallas_call | solution.py:374
  62.1 1.3 %collective-permute-start.14 = (bf16[1552,128]{1,0:T(8,128)(2,1)S(1)}, bf16[1552,128]{1,0:T(8,128)(2,1)S(1)}, u32[]{:S(2)}, u32[]{:S(2)}) collective-permute-start(bf16[1552,128]{1,0:T(8,128)(2,1)S(1)} %shard_map.29.refs_3_), channel_id=1, source_target_pairs={{0,1},{3,2},{4,5},{7,6},{8,9},{11,10},{12,13},{15,14},{16,17},{19,... | collective-permute-start | bytes 1191944 | tf_op jit(solution)/shard_map/ppermute | solution.py:404
  63.5 1.3 %collective-permute-start.13 = (bf16[2064,128]{1,0:T(8,128)(2,1)S(1)}, bf16[2064,128]{1,0:T(8,128)(2,1)S(1)}, u32[]{:S(2)}, u32[]{:S(2)}) collective-permute-start(bf16[2064,128]{1,0:T(8,128)(2,1)S(1)} %shard_map.30.refs_4_), channel_id=1, source_target_pairs={{1,0},{2,3},{5,4},{6,7},{9,8},{10,11},{13,12},{14,15},{17,16},{18,... | collective-permute-start | bytes 1585160 | tf_op jit(solution)/shard_map/ppermute | solution.py:404
  64.8 2.8 %collective-permute-done.9.refs_3_ = bf16[2064,128]{1,0:T(8,128)(2,1)S(1)} collective-permute-done((bf16[2064,128]{1,0:T(8,128)(2,1)S(1)}, bf16[2064,128]{1,0:T(8,128)(2,1)S(1)}, u32[]{:S(2)}, u32[]{:S(2)}) %collective-permute-start.9) | collective-permute-done | bytes 528416 | tf_op jit(solution)/shard_map/ppermute | solution.py:404
  67.5 1.7 %shard_map.31.refs_3_ = bf16[3088,128]{1,0:T(8,128)(2,1)S(1)} custom-call(bf16[1024,1024]{1,0:T(8,128)(2,1)S(1)} %bitcast.20, bf16[1024,1024]{1,0:T(8,128)(2,1)S(1)} %collective-permute-done.refs_1_.refs_0_, bf16[1024,768]{1,0:T(8,128)(2,1)S(1)} %collective-permute-done.4.refs_0_.refs_2_, bf16[2064,128]{1,0:T(8,128)(2,1)S(1)} %collective-permute-done.9.refs_3_, ...), custom_call_target="tpu_custom_call" | custom-call | flops 6000000000 | bytes 6000000 | tf_op jit(solution)/shard_map/pallas_call | solution.py:374
  69.2 1.3 %collective-permute-start.16 = (bf16[3088,128]{1,0:T(8,128)(2,1)S(1)}, bf16[3088,128]{1,0:T(8,128)(2,1)S(1)}, u32[]{:S(2)}, u32[]{:S(2)}) collective-permute-start(bf16[3088,128]{1,0:T(8,128)(2,1)S(1)} %shard_map.31.refs_3_), channel_id=1, source_target_pairs={{0,1},{3,2},{4,5},{7,6},{8,9},{11,10},{12,13},{15,14},{16,17},{19,... | collective-permute-start | bytes 2371592 | tf_op jit(solution)/shard_map/ppermute | solution.py:404
  71.3 1.3 %collective-permute-start.17 = (bf16[2064,128]{1,0:T(8,128)(2,1)S(1)}, bf16[2064,128]{1,0:T(8,128)(2,1)S(1)}, u32[]{:S(2)}, u32[]{:S(2)}) collective-permute-start(bf16[2064,128]{1,0:T(8,128)(2,1)S(1)} %shard_map.33.refs_3_), channel_id=1, source_target_pairs={{1,8},{2,11},{5,12},{6,15},{9,0},{10,3},{13,4},{14,7},{17,24},{18,... | collective-permute-start | bytes 1585160 | tf_op jit(solution)/shard_map/ppermute | solution.py:404
  74.0 2.4 %shard_map.35 = (bf16[16,128]{1,0:T(8,128)(2,1)S(1)}, f32[1,3,256,1024]{3,2,1,0:T(8,128)}) custom-call(bf16[1024,1024]{1,0:T(8,128)(2,1)S(1)} %bitcast.24, bf16[1552,128]{1,0:T(8,128)(2,1)S(1)} %collective-permute-done.5.refs_2_.refs_1_, bf16[2096,128]{1,0:T(8,128)(2,1)S(1)} %collective-permute-done.3.refs_2_, ...), custom_call_target="tpu_custom_call" | custom-call | flops 6000000000 | bytes 6000000 | tf_op jit(solution)/shard_map/pallas_call | solution.py:374
  76.4 3.7 %collective-permute-done.13.refs_5_ = bf16[2064,128]{1,0:T(8,128)(2,1)S(1)} collective-permute-done((bf16[2064,128]{1,0:T(8,128)(2,1)S(1)}, bf16[2064,128]{1,0:T(8,128)(2,1)S(1)}, u32[]{:S(2)}, u32[]{:S(2)}) %collective-permute-start.13) | collective-permute-done | bytes 528416 | tf_op jit(solution)/shard_map/ppermute | solution.py:404
  80.1 1.5 %shard_map.36 = (f32[256,1024]{1,0:T(8,128)S(1)}, f32[256,1024]{1,0:T(8,128)S(1)}) custom-call(bf16[1024,1024]{1,0:T(8,128)(2,1)S(1)} %bitcast.25, bf16[1024,1024]{1,0:T(8,128)(2,1)S(1)} %collective-permute-done.refs_1_.refs_0_, bf16[1024,768]{1,0:T(8,128)(2,1)S(1)} %collective-permute-done.4.refs_0_.refs_2_, ...), custom_call_target="tpu_custom_call" | custom-call | flops 6000000000 | bytes 6000000 | tf_op jit(solution)/shard_map/pallas_call | solution.py:374
  81.5 8.9 %collective-permute-done.17.refs_3_ = bf16[2064,128]{1,0:T(8,128)(2,1)S(1)} collective-permute-done((bf16[2064,128]{1,0:T(8,128)(2,1)S(1)}, bf16[2064,128]{1,0:T(8,128)(2,1)S(1)}, u32[]{:S(2)}, u32[]{:S(2)}) %collective-permute-start.17) | collective-permute-done | bytes 528416 | tf_op jit(solution)/shard_map/ppermute | solution.py:404
  90.5 1.5 %shard_map.37 = (f32[256,1024]{1,0:T(8,128)S(1)}, f32[1,3,256,1024]{3,2,1,0:T(8,128)}) custom-call(f32[256,1024]{1,0:T(8,128)S(1)} %get-tuple-element.13.refs_0_.refs_5_, f32[256,1024]{1,0:T(8,128)S(1)} %get-tuple-element.14.refs_1_, bf16[3088,128]{1,0:T(8,128)(2,1)S(1)} %collective-permute-done.16.refs_2_, ...), custom_call_target="tpu_custom_call", output_to_operand_aliasing={{1}: (4, {})} | custom-call | flops 6000000000 | bytes 6000000 | tf_op jit(solution)/shard_map/pallas_call | solution.py:374
  92.0 1.1 %shard_map.38 = (bf16[16,128]{1,0:T(8,128)(2,1)}, f32[1,3,256,1024]{3,2,1,0:T(8,128)}) custom-call(f32[256,1024]{1,0:T(8,128)S(1)} %get-tuple-element.16.refs_0_.refs_3_, bf16[1552,128]{1,0:T(8,128)(2,1)S(1)} %collective-permute-done.18.refs_1_, f32[1,3,256,1024]{3,2,1,0:T(8,128)} %get-tuple-element.17.refs_2_, ...), custom_call_target="tpu_custom_call", output_to_operand_aliasing={{1}: (2, {})} | custom-call | flops 6000000000 | bytes 6000000 | tf_op jit(solution)/shard_map/pallas_call | solution.py:374
  (32 shorter events, 5.4 us)
Async XLA Ops:
  0.0 26.2 %collective-permute-start = (bf16[1024,1024]{1,0:T(8,128)(2,1)}, bf16[1024,1024]{1,0:T(8,128)(2,1)S(1)}, u32[]{:S(2)}, u32[]{:S(2)}) collective-permute-start(bf16[1024,1024]{1,0:T(8,128)(2,1)} %bitcast.1), channel_id=1, source_target_pairs={{0,12},{4,0},{8,4},{12,8},{1,13},{5,1},{9,5},{13,9},{2,14},{6,2},{... | collective-permute-start | bytes 6291464 | tf_op jit(solution)/shard_map/ppermute | solution.py:26
  2.4 1.6 %copy-start = (bf16[1,1024,1024]{2,1,0:T(8,128)(2,1)S(1)}, bf16[1,1024,1024]{2,1,0:T(8,128)(2,1)}, u32[]{:S(2)}) copy-start(bf16[1,1024,1024]{2,1,0:T(8,128)(2,1)} %param.1) | copy-start | bytes 6291460
  5.2 14.7 %collective-permute-start.1 = (bf16[2064,128]{1,0:T(8,128)(2,1)S(1)}, bf16[2064,128]{1,0:T(8,128)(2,1)S(1)}, u32[]{:S(2)}, u32[]{:S(2)}) collective-permute-start(bf16[2064,128]{1,0:T(8,128)(2,1)S(1)} %shard_map.17.refs_2_), channel_id=1, source_target_pairs={{0,1},{3,2},{4,5},{7,6},{8,9},{11,10},{12,13},{15,14},{16,17},{19,... | collective-permute-start | bytes 1585160 | tf_op jit(solution)/shard_map/ppermute | solution.py:404
  8.9 22.9 %collective-permute-start.3 = (bf16[2096,128]{1,0:T(8,128)(2,1)S(1)}, bf16[2096,128]{1,0:T(8,128)(2,1)S(1)}, u32[]{:S(2)}, u32[]{:S(2)}) collective-permute-start(bf16[2096,128]{1,0:T(8,128)(2,1)S(1)} %shard_map.18.refs_3_), channel_id=1, source_target_pairs={{0,1},{3,2},{4,5},{7,6},{8,9},{11,10},{12,13},{15,14},{16,17},{19,... | collective-permute-start | bytes 1609736 | tf_op jit(solution)/shard_map/ppermute | solution.py:404
  19.9 31.9 %collective-permute-start.8 = (bf16[2064,128]{1,0:T(8,128)(2,1)S(1)}, bf16[2064,128]{1,0:T(8,128)(2,1)S(1)}, u32[]{:S(2)}, u32[]{:S(2)}) collective-permute-start(bf16[2064,128]{1,0:T(8,128)(2,1)S(1)} %shard_map.19.refs_2_), channel_id=1, source_target_pairs={{1,2},{2,1},{5,6},{6,5},{9,10},{10,9},{13,14},{14,13},{17,18},{18,... | collective-permute-start | bytes 1585160 | tf_op jit(solution)/shard_map/ppermute | solution.py:404
  27.5 4.4 %copy-start.1 = (bf16[1,1024,1024]{2,1,0:T(8,128)(2,1)S(1)}, bf16[1,1024,1024]{2,1,0:T(8,128)(2,1)}, u32[]{:S(2)}) copy-start(bf16[1,1024,1024]{2,1,0:T(8,128)(2,1)} %param.1) | copy-start | bytes 6291460
  27.5 15.7 %collective-permute-start.6 = (bf16[2064,128]{1,0:T(8,128)(2,1)S(1)}, bf16[2064,128]{1,0:T(8,128)(2,1)S(1)}, u32[]{:S(2)}, u32[]{:S(2)}) collective-permute-start(bf16[2064,128]{1,0:T(8,128)(2,1)S(1)} %shard_map.20.refs_1_), channel_id=1, source_target_pairs={{0,1},{3,2},{4,5},{7,6},{8,9},{11,10},{12,13},{15,14},{16,17},{19,... | collective-permute-start | bytes 1585160 | tf_op jit(solution)/shard_map/ppermute | solution.py:404
  30.0 8.6 %collective-permute-start.2 = (bf16[1024,256]{1,0:T(8,128)(2,1)S(1)}, bf16[1024,256]{1,0:T(8,128)(2,1)S(1)}, u32[]{:S(2)}, u32[]{:S(2)}) collective-permute-start(bf16[1024,256]{1,0:T(8,128)(2,1)S(1)} %shard_map.21.refs_3_), channel_id=1, source_target_pairs={{0,12},{4,0},{8,4},{12,8},{1,13},{5,1},{9,5},{13,9},{2,14},{6,2},{... | collective-permute-start | bytes 1572872 | tf_op jit(solution)/shard_map/ppermute | solution.py:26
  31.9 12.0 %collective-permute-start.5 = (bf16[1552,128]{1,0:T(8,128)(2,1)S(1)}, bf16[1552,128]{1,0:T(8,128)(2,1)S(1)}, u32[]{:S(2)}, u32[]{:S(2)}) collective-permute-start(bf16[1552,128]{1,0:T(8,128)(2,1)S(1)} %shard_map.22.refs_2_), channel_id=1, source_target_pairs={{1,2},{2,1},{5,6},{6,5},{9,10},{10,9},{13,14},{14,13},{17,18},{18,... | collective-permute-start | bytes 1191944 | tf_op jit(solution)/shard_map/ppermute | solution.py:404
  39.8 13.7 %collective-permute-start.11 = (bf16[2064,128]{1,0:T(8,128)(2,1)S(1)}, bf16[2064,128]{1,0:T(8,128)(2,1)S(1)}, u32[]{:S(2)}, u32[]{:S(2)}) collective-permute-start(bf16[2064,128]{1,0:T(8,128)(2,1)S(1)} %shard_map.23.refs_1_), channel_id=1, source_target_pairs={{0,1},{3,2},{4,5},{7,6},{8,9},{11,10},{12,13},{15,14},{16,17},{19,... | collective-permute-start | bytes 1585160 | tf_op jit(solution)/shard_map/ppermute | solution.py:404
  41.2 19.9 %collective-permute-start.4 = (bf16[1024,768]{1,0:T(8,128)(2,1)S(1)}, bf16[1024,768]{1,0:T(8,128)(2,1)S(1)}, u32[]{:S(2)}, u32[]{:S(2)}) collective-permute-start(bf16[1024,768]{1,0:T(8,128)(2,1)S(1)} %shard_map.24.refs_3_), channel_id=1, source_target_pairs={{0,12},{4,0},{8,4},{12,8},{1,13},{5,1},{9,5},{13,9},{2,14},{6,2},{... | collective-permute-start | bytes 4718600 | tf_op jit(solution)/shard_map/ppermute | solution.py:26
  43.2 20.2 %collective-permute-start.10 = (bf16[2064,128]{1,0:T(8,128)(2,1)S(1)}, bf16[2064,128]{1,0:T(8,128)(2,1)S(1)}, u32[]{:S(2)}, u32[]{:S(2)}) collective-permute-start(bf16[2064,128]{1,0:T(8,128)(2,1)S(1)} %shard_map.25.refs_3_), channel_id=1, source_target_pairs={{1,2},{2,1},{5,6},{6,5},{9,10},{10,9},{13,14},{14,13},{17,18},{18,... | collective-permute-start | bytes 1585160 | tf_op jit(solution)/shard_map/ppermute | solution.py:404
  45.1 25.5 %collective-permute-start.7 = (bf16[2064,128]{1,0:T(8,128)(2,1)S(1)}, bf16[2064,128]{1,0:T(8,128)(2,1)S(1)}, u32[]{:S(2)}, u32[]{:S(2)}) collective-permute-start(bf16[2064,128]{1,0:T(8,128)(2,1)S(1)} %shard_map.26.refs_3_), channel_id=1, source_target_pairs={{0,1},{3,2},{4,5},{7,6},{8,9},{11,10},{12,13},{15,14},{16,17},{19,... | collective-permute-start | bytes 1585160 | tf_op jit(solution)/shard_map/ppermute | solution.py:404
  52.1 15.5 %collective-permute-start.9 = (bf16[2064,128]{1,0:T(8,128)(2,1)S(1)}, bf16[2064,128]{1,0:T(8,128)(2,1)S(1)}, u32[]{:S(2)}, u32[]{:S(2)}) collective-permute-start(bf16[2064,128]{1,0:T(8,128)(2,1)S(1)} %shard_map.27.refs_3_), channel_id=1, source_target_pairs={{1,0},{2,3},{5,4},{6,7},{9,8},{10,11},{13,12},{14,15},{17,16},{18,... | collective-permute-start | bytes 1585160 | tf_op jit(solution)/shard_map/ppermute | solution.py:404
  53.5 17.8 %collective-permute-start.15 = (bf16[2064,128]{1,0:T(8,128)(2,1)S(1)}, bf16[2064,128]{1,0:T(8,128)(2,1)S(1)}, u32[]{:S(2)}, u32[]{:S(2)}) collective-permute-start(bf16[2064,128]{1,0:T(8,128)(2,1)S(1)} %shard_map.28.refs_2_), channel_id=1, source_target_pairs={{1,2},{2,1},{5,6},{6,5},{9,10},{10,9},{13,14},{14,13},{17,18},{18,... | collective-permute-start | bytes 1585160 | tf_op jit(solution)/shard_map/ppermute | solution.py:404
  62.1 11.3 %collective-permute-start.14 = (bf16[1552,128]{1,0:T(8,128)(2,1)S(1)}, bf16[1552,128]{1,0:T(8,128)(2,1)S(1)}, u32[]{:S(2)}, u32[]{:S(2)}) collective-permute-start(bf16[1552,128]{1,0:T(8,128)(2,1)S(1)} %shard_map.29.refs_3_), channel_id=1, source_target_pairs={{0,1},{3,2},{4,5},{7,6},{8,9},{11,10},{12,13},{15,14},{16,17},{19,... | collective-permute-start | bytes 1191944 | tf_op jit(solution)/shard_map/ppermute | solution.py:404
  63.5 16.6 %collective-permute-start.13 = (bf16[2064,128]{1,0:T(8,128)(2,1)S(1)}, bf16[2064,128]{1,0:T(8,128)(2,1)S(1)}, u32[]{:S(2)}, u32[]{:S(2)}) collective-permute-start(bf16[2064,128]{1,0:T(8,128)(2,1)S(1)} %shard_map.30.refs_4_), channel_id=1, source_target_pairs={{1,0},{2,3},{5,4},{6,7},{9,8},{10,11},{13,12},{14,15},{17,16},{18,... | collective-permute-start | bytes 1585160 | tf_op jit(solution)/shard_map/ppermute | solution.py:404
  69.2 21.3 %collective-permute-start.16 = (bf16[3088,128]{1,0:T(8,128)(2,1)S(1)}, bf16[3088,128]{1,0:T(8,128)(2,1)S(1)}, u32[]{:S(2)}, u32[]{:S(2)}) collective-permute-start(bf16[3088,128]{1,0:T(8,128)(2,1)S(1)} %shard_map.31.refs_3_), channel_id=1, source_target_pairs={{0,1},{3,2},{4,5},{7,6},{8,9},{11,10},{12,13},{15,14},{16,17},{19,... | collective-permute-start | bytes 2371592 | tf_op jit(solution)/shard_map/ppermute | solution.py:404
  70.6 5.8 %collective-permute-start.12 = (bf16[2064,128]{1,0:T(8,128)(2,1)S(1)}, bf16[2064,128]{1,0:T(8,128)(2,1)S(1)}, u32[]{:S(2)}, u32[]{:S(2)}) collective-permute-start(bf16[2064,128]{1,0:T(8,128)(2,1)S(1)} %shard_map.32.refs_3_), channel_id=1, source_target_pairs={{1,2},{2,1},{5,6},{6,5},{9,10},{10,9},{13,14},{14,13},{17,18},{18,... | collective-permute-start | bytes 1585160 | tf_op jit(solution)/shard_map/ppermute | solution.py:404
  71.3 19.1 %collective-permute-start.17 = (bf16[2064,128]{1,0:T(8,128)(2,1)S(1)}, bf16[2064,128]{1,0:T(8,128)(2,1)S(1)}, u32[]{:S(2)}, u32[]{:S(2)}) collective-permute-start(bf16[2064,128]{1,0:T(8,128)(2,1)S(1)} %shard_map.33.refs_3_), channel_id=1, source_target_pairs={{1,8},{2,11},{5,12},{6,15},{9,0},{10,3},{13,4},{14,7},{17,24},{18,... | collective-permute-start | bytes 1585160 | tf_op jit(solution)/shard_map/ppermute | solution.py:404
  73.3 18.7 %collective-permute-start.18 = (bf16[1552,128]{1,0:T(8,128)(2,1)S(1)}, bf16[1552,128]{1,0:T(8,128)(2,1)S(1)}, u32[]{:S(2)}, u32[]{:S(2)}) collective-permute-start(bf16[1552,128]{1,0:T(8,128)(2,1)S(1)} %shard_map.34.refs_6_), channel_id=1, source_target_pairs={{1,10},{2,9},{5,14},{6,13},{9,2},{10,1},{13,6},{14,5},{17,26},{18,... | collective-permute-start | bytes 1191944 | tf_op jit(solution)/shard_map/ppermute | solution.py:404

commit v6 on v5

--- a/solution.py
+++ b/solution.py
@@ -65,6 +65,14 @@
 def product(inverse, left_ref, right_ref, upper, row, column, rows):
     left = block_of(left_ref, upper, row, rows)
     return tile_rows(inverse, left, block_of(right_ref, upper, column, rows))
+
+
+def row_products(inverse, left_ref, right_ref, upper, row, columns, rows):
+    left = block_of(left_ref, upper, row, rows).T
+    return [
+        jnp.dot(left, block_of(right_ref, upper, column, rows), preferred_element_type=jnp.float32) * inverse
+        for column in columns
+    ]
 
 
 def row_factor(rows):
@@ -175,10 +183,7 @@
     def _():
         write_message(
             message_ref,
-            [
-                product(inverse, left_ref, right_ref, upper, row, column, rows)
-                for column in range(count)
-            ],
+            row_products(inverse, left_ref, right_ref, upper, row, range(count), rows),
         )
 
 
@@ -234,9 +239,10 @@
         write_message(
             message_ref,
             [
-                product(inverse, left_ref, right_ref, upper, row, column, rows)
-                + read_block(in_ref, column, rows)
-                for column in range(count)
+                block + read_block(in_ref, column, rows)
+                for column, block in enumerate(
+                    row_products(inverse, left_ref, right_ref, upper, row, range(count), rows)
+                )
             ],
         )
 

time: 94.7 us -> 94.7 us (level)
  no operation moved by 1% of the time
where the time goes in v6:
time: 94.7 us; the launch traced here: 93.1 us
  waiting for transfers between devices  44.4 us (47%)
  starting transfers between devices  30.9 us (33%)
  Pallas kernels  15.9 us (17%)
  local copies, waits for them, and re-layouts  1.63 us (2%)
    ppermute x16, waiting for transfers between devices, hop(): return lax.ppermute(message, ('layer', 'tok'), pairs)  25.9 us
    ppermute x16, starting transfers between devices, hop(): return lax.ppermute(message, ('layer', 'tok'), pairs)  24.7 us
    ppermute x3, waiting for transfers between devices, shifted(): return lax.ppermute(value, axis, pairs)  18.6 us
    pallas_call x22, Pallas kernels, call(): pl.pallas_call(functools.partial(ordered, body, len(operands), len(held))...  15.9 us
    ppermute x3, starting transfers between devices, shifted(): return lax.ppermute(value, axis, pairs)  6.2 us
  transfers between devices with their start and end apart: 19, of which 9 were waited for; matrix products, arithmetic and copies ran while one was open for 0% of the time, Pallas kernels for 16%

profile of v6, /device:TPU:0, one launch (start us, length us, event | category | flops | bytes accessed | tf_op | source)
XLA Modules:
  0.0 93.1 jit_solution(3261018343447548379)
XLA Ops:
  0.0 2.4 %collective-permute-start = (bf16[1024,1024]{1,0:T(8,128)(2,1)}, bf16[1024,1024]{1,0:T(8,128)(2,1)S(1)}, u32[]{:S(2)}, u32[]{:S(2)}) collective-permute-start(bf16[1024,1024]{1,0:T(8,128)(2,1)} %bitcast.1), channel_id=1, source_target_pairs={{0,12},{4,0},{8,4},{12,8},{1,13},{5,1},{9,5},{13,9},{2,14},{6,2},{... | collective-permute-start | bytes 6291464 | tf_op jit(solution)/shard_map/ppermute | solution.py:26
  2.4 1.6 %copy-done = bf16[1,1024,1024]{2,1,0:T(8,128)(2,1)S(1)} copy-done((bf16[1,1024,1024]{2,1,0:T(8,128)(2,1)S(1)}, bf16[1,1024,1024]{2,1,0:T(8,128)(2,1)}, u32[]{:S(2)}) %copy-start) | copy-done | bytes 2097176
  4.0 1.2 %shard_map.17.refs_2_ = bf16[2064,128]{1,0:T(8,128)(2,1)S(1)} custom-call(bf16[1024,1024]{1,0:T(8,128)(2,1)S(1)} %bitcast.2, bf16[1024,1024]{1,0:T(8,128)(2,1)S(1)} %bitcast.3, bf16[1024,1024]{1,0:T(8,128)(2,1)S(1)} %bitcast.4), custom_call_target="tpu_custom_call" | custom-call | flops 6000000000 | bytes 6000000 | tf_op jit(solution)/shard_map/pallas_call | solution.py:380
  5.2 2.3 %collective-permute-start.1 = (bf16[2064,128]{1,0:T(8,128)(2,1)S(1)}, bf16[2064,128]{1,0:T(8,128)(2,1)S(1)}, u32[]{:S(2)}, u32[]{:S(2)}) collective-permute-start(bf16[2064,128]{1,0:T(8,128)(2,1)S(1)} %shard_map.17.refs_2_), channel_id=1, source_target_pairs={{0,1},{3,2},{4,5},{7,6},{8,9},{11,10},{12,13},{15,14},{16,17},{19,... | collective-permute-start | bytes 1585160 | tf_op jit(solution)/shard_map/ppermute | solution.py:410
  7.5 1.4 %shard_map.18.refs_3_ = bf16[2096,128]{1,0:T(8,128)(2,1)S(1)} custom-call(bf16[1024,1024]{1,0:T(8,128)(2,1)S(1)} %bitcast.5, bf16[1024,1024]{1,0:T(8,128)(2,1)S(1)} %bitcast.6, bf16[2064,128]{1,0:T(8,128)(2,1)S(1)} %shard_map.17.refs_2_), custom_call_target="tpu_custom_call" | custom-call | flops 6000000000 | bytes 6000000 | tf_op jit(solution)/shard_map/pallas_call | solution.py:380
  8.9 1.3 %collective-permute-start.3 = (bf16[2096,128]{1,0:T(8,128)(2,1)S(1)}, bf16[2096,128]{1,0:T(8,128)(2,1)S(1)}, u32[]{:S(2)}, u32[]{:S(2)}) collective-permute-start(bf16[2096,128]{1,0:T(8,128)(2,1)S(1)} %shard_map.18.refs_3_), channel_id=1, source_target_pairs={{0,1},{3,2},{4,5},{7,6},{8,9},{11,10},{12,13},{15,14},{16,17},{19,... | collective-permute-start | bytes 1609736 | tf_op jit(solution)/shard_map/ppermute | solution.py:410
  10.3 9.7 %collective-permute-done.1.refs_2_.refs_4_ = bf16[2064,128]{1,0:T(8,128)(2,1)S(1)} collective-permute-done((bf16[2064,128]{1,0:T(8,128)(2,1)S(1)}, bf16[2064,128]{1,0:T(8,128)(2,1)S(1)}, u32[]{:S(2)}, u32[]{:S(2)}) %collective-permute-start.1) | collective-permute-done | bytes 528416 | tf_op jit(solution)/shard_map/ppermute | solution.py:410
  20.6 5.6 %collective-permute-done.refs_1_.refs_0_ = bf16[1024,1024]{1,0:T(8,128)(2,1)S(1)} collective-permute-done((bf16[1024,1024]{1,0:T(8,128)(2,1)}, bf16[1024,1024]{1,0:T(8,128)(2,1)S(1)}, u32[]{:S(2)}, u32[]{:S(2)}) %collective-permute-start) | collective-permute-done | bytes 2097184 | tf_op jit(solution)/shard_map/ppermute | solution.py:26
  26.2 1.2 %shard_map.20.refs_1_ = bf16[2064,128]{1,0:T(8,128)(2,1)S(1)} custom-call(bf16[1024,1024]{1,0:T(8,128)(2,1)S(1)} %bitcast.9, bf16[1024,1024]{1,0:T(8,128)(2,1)S(1)} %collective-permute-done.refs_1_.refs_0_, bf16[2064,128]{1,0:T(8,128)(2,1)S(1)} %shard_map.19.refs_2_), custom_call_target="tpu_custom_call" | custom-call | flops 6000000000 | bytes 6000000 | tf_op jit(solution)/shard_map/pallas_call | solution.py:380
  27.5 2.4 %collective-permute-start.6 = (bf16[2064,128]{1,0:T(8,128)(2,1)S(1)}, bf16[2064,128]{1,0:T(8,128)(2,1)S(1)}, u32[]{:S(2)}, u32[]{:S(2)}) collective-permute-start(bf16[2064,128]{1,0:T(8,128)(2,1)S(1)} %shard_map.20.refs_1_), channel_id=1, source_target_pairs={{0,1},{3,2},{4,5},{7,6},{8,9},{11,10},{12,13},{15,14},{16,17},{19,... | collective-permute-start | bytes 1585160 | tf_op jit(solution)/shard_map/ppermute | solution.py:410
  30.0 1.9 %collective-permute-start.2 = (bf16[1024,256]{1,0:T(8,128)(2,1)S(1)}, bf16[1024,256]{1,0:T(8,128)(2,1)S(1)}, u32[]{:S(2)}, u32[]{:S(2)}) collective-permute-start(bf16[1024,256]{1,0:T(8,128)(2,1)S(1)} %shard_map.21.refs_3_), channel_id=1, source_target_pairs={{0,12},{4,0},{8,4},{12,8},{1,13},{5,1},{9,5},{13,9},{2,14},{6,2},{... | collective-permute-start | bytes 1572872 | tf_op jit(solution)/shard_map/ppermute | solution.py:26
  32.5 6.0 %collective-permute-done.2.refs_0_.refs_3_ = bf16[1024,256]{1,0:T(8,128)(2,1)S(1)} collective-permute-done((bf16[1024,256]{1,0:T(8,128)(2,1)S(1)}, bf16[1024,256]{1,0:T(8,128)(2,1)S(1)}, u32[]{:S(2)}, u32[]{:S(2)}) %collective-permute-start.2) | collective-permute-done | bytes 524320 | tf_op jit(solution)/shard_map/ppermute | solution.py:26
  38.5 1.2 %shard_map.23.refs_1_ = bf16[2064,128]{1,0:T(8,128)(2,1)S(1)} custom-call(bf16[1024,256]{1,0:T(8,128)(2,1)S(1)} %collective-permute-done.2.refs_0_.refs_3_, bf16[1024,1024]{1,0:T(8,128)(2,1)S(1)} %bitcast.12, bf16[1552,128]{1,0:T(8,128)(2,1)S(1)} %shard_map.22.refs_2_), custom_call_target="tpu_custom_call" | custom-call | flops 6000000000 | bytes 6000000 | tf_op jit(solution)/shard_map/pallas_call | solution.py:380
  39.8 1.3 %collective-permute-start.11 = (bf16[2064,128]{1,0:T(8,128)(2,1)S(1)}, bf16[2064,128]{1,0:T(8,128)(2,1)S(1)}, u32[]{:S(2)}, u32[]{:S(2)}) collective-permute-start(bf16[2064,128]{1,0:T(8,128)(2,1)S(1)} %shard_map.23.refs_1_), channel_id=1, source_target_pairs={{0,1},{3,2},{4,5},{7,6},{8,9},{11,10},{12,13},{15,14},{16,17},{19,... | collective-permute-start | bytes 1585160 | tf_op jit(solution)/shard_map/ppermute | solution.py:410
  41.2 2.0 %collective-permute-start.4 = (bf16[1024,768]{1,0:T(8,128)(2,1)S(1)}, bf16[1024,768]{1,0:T(8,128)(2,1)S(1)}, u32[]{:S(2)}, u32[]{:S(2)}) collective-permute-start(bf16[1024,768]{1,0:T(8,128)(2,1)S(1)} %shard_map.24.refs_3_), channel_id=1, source_target_pairs={{0,12},{4,0},{8,4},{12,8},{1,13},{5,1},{9,5},{13,9},{2,14},{6,2},{... | collective-permute-start | bytes 4718600 | tf_op jit(solution)/shard_map/ppermute | solution.py:26
  43.9 1.2 %shard_map.26.refs_3_ = bf16[2064,128]{1,0:T(8,128)(2,1)S(1)} custom-call(bf16[1024,1024]{1,0:T(8,128)(2,1)S(1)} %bitcast.14, bf16[1024,1024]{1,0:T(8,128)(2,1)S(1)} %collective-permute-done.refs_1_.refs_0_, bf16[1552,128]{1,0:T(8,128)(2,1)S(1)} %collective-permute-done.5.refs_2_.refs_1_, bf16[2064,128]{1,0:T(8,128)(2,1)S(1)} %shard_map.25.refs_3_), custom_call_target="tpu_custom_call" | custom-call | flops 6000000000 | bytes 6000000 | tf_op jit(solution)/shard_map/pallas_call | solution.py:380
  45.1 6.7 %collective-permute-start.7 = (bf16[2064,128]{1,0:T(8,128)(2,1)S(1)}, bf16[2064,128]{1,0:T(8,128)(2,1)S(1)}, u32[]{:S(2)}, u32[]{:S(2)}) collective-permute-start(bf16[2064,128]{1,0:T(8,128)(2,1)S(1)} %shard_map.26.refs_3_), channel_id=1, source_target_pairs={{0,1},{3,2},{4,5},{7,6},{8,9},{11,10},{12,13},{15,14},{16,17},{19,... | collective-permute-start | bytes 1585160 | tf_op jit(solution)/shard_map/ppermute | solution.py:410
  52.1 1.3 %collective-permute-start.9 = (bf16[2064,128]{1,0:T(8,128)(2,1)S(1)}, bf16[2064,128]{1,0:T(8,128)(2,1)S(1)}, u32[]{:S(2)}, u32[]{:S(2)}) collective-permute-start(bf16[2064,128]{1,0:T(8,128)(2,1)S(1)} %shard_map.27.refs_3_), channel_id=1, source_target_pairs={{1,0},{2,3},{5,4},{6,7},{9,8},{10,11},{13,12},{14,15},{17,16},{18,... | collective-permute-start | bytes 1585160 | tf_op jit(solution)/shard_map/ppermute | solution.py:410
  54.2 6.9 %collective-permute-done.4.refs_0_.refs_2_ = bf16[1024,768]{1,0:T(8,128)(2,1)S(1)} collective-permute-done((bf16[1024,768]{1,0:T(8,128)(2,1)S(1)}, bf16[1024,768]{1,0:T(8,128)(2,1)S(1)}, u32[]{:S(2)}, u32[]{:S(2)}) %collective-permute-start.4) | collective-permute-done | bytes 1572896 | tf_op jit(solution)/shard_map/ppermute | solution.py:26
  61.1 1.0 %shard_map.29.refs_3_ = bf16[1552,128]{1,0:T(8,128)(2,1)S(1)} custom-call(bf16[1024,768]{1,0:T(8,128)(2,1)S(1)} %collective-permute-done.4.refs_0_.refs_2_, bf16[1024,1024]{1,0:T(8,128)(2,1)S(1)} %bitcast.18, bf16[2064,128]{1,0:T(8,128)(2,1)S(1)} %shard_map.28.refs_2_), custom_call_target="tpu_custom_call" | custom-call | flops 6000000000 | bytes 6000000 | tf_op jit(solution)/shard_map/pallas_call | solution.py:380
  62.1 1.3 %collective-permute-start.14 = (bf16[1552,128]{1,0:T(8,128)(2,1)S(1)}, bf16[1552,128]{1,0:T(8,128)(2,1)S(1)}, u32[]{:S(2)}, u32[]{:S(2)}) collective-permute-start(bf16[1552,128]{1,0:T(8,128)(2,1)S(1)} %shard_map.29.refs_3_), channel_id=1, source_target_pairs={{0,1},{3,2},{4,5},{7,6},{8,9},{11,10},{12,13},{15,14},{16,17},{19,... | collective-permute-start | bytes 1191944 | tf_op jit(solution)/shard_map/ppermute | solution.py:410
  63.5 1.3 %collective-permute-start.13 = (bf16[2064,128]{1,0:T(8,128)(2,1)S(1)}, bf16[2064,128]{1,0:T(8,128)(2,1)S(1)}, u32[]{:S(2)}, u32[]{:S(2)}) collective-permute-start(bf16[2064,128]{1,0:T(8,128)(2,1)S(1)} %shard_map.30.refs_4_), channel_id=1, source_target_pairs={{1,0},{2,3},{5,4},{6,7},{9,8},{10,11},{13,12},{14,15},{17,16},{18,... | collective-permute-start | bytes 1585160 | tf_op jit(solution)/shard_map/ppermute | solution.py:410
  64.8 2.8 %collective-permute-done.9.refs_3_ = bf16[2064,128]{1,0:T(8,128)(2,1)S(1)} collective-permute-done((bf16[2064,128]{1,0:T(8,128)(2,1)S(1)}, bf16[2064,128]{1,0:T(8,128)(2,1)S(1)}, u32[]{:S(2)}, u32[]{:S(2)}) %collective-permute-start.9) | collective-permute-done | bytes 528416 | tf_op jit(solution)/shard_map/ppermute | solution.py:410
  67.5 1.7 %shard_map.31.refs_3_ = bf16[3088,128]{1,0:T(8,128)(2,1)S(1)} custom-call(bf16[1024,1024]{1,0:T(8,128)(2,1)S(1)} %bitcast.20, bf16[1024,1024]{1,0:T(8,128)(2,1)S(1)} %collective-permute-done.refs_1_.refs_0_, bf16[1024,768]{1,0:T(8,128)(2,1)S(1)} %collective-permute-done.4.refs_0_.refs_2_, bf16[2064,128]{1,0:T(8,128)(2,1)S(1)} %collective-permute-done.9.refs_3_, ...), custom_call_target="tpu_custom_call" | custom-call | flops 6000000000 | bytes 6000000 | tf_op jit(solution)/shard_map/pallas_call | solution.py:380
  69.2 1.3 %collective-permute-start.16 = (bf16[3088,128]{1,0:T(8,128)(2,1)S(1)}, bf16[3088,128]{1,0:T(8,128)(2,1)S(1)}, u32[]{:S(2)}, u32[]{:S(2)}) collective-permute-start(bf16[3088,128]{1,0:T(8,128)(2,1)S(1)} %shard_map.31.refs_3_), channel_id=1, source_target_pairs={{0,1},{3,2},{4,5},{7,6},{8,9},{11,10},{12,13},{15,14},{16,17},{19,... | collective-permute-start | bytes 2371592 | tf_op jit(solution)/shard_map/ppermute | solution.py:410
  71.3 1.3 %collective-permute-start.17 = (bf16[2064,128]{1,0:T(8,128)(2,1)S(1)}, bf16[2064,128]{1,0:T(8,128)(2,1)S(1)}, u32[]{:S(2)}, u32[]{:S(2)}) collective-permute-start(bf16[2064,128]{1,0:T(8,128)(2,1)S(1)} %shard_map.33.refs_3_), channel_id=1, source_target_pairs={{1,8},{2,11},{5,12},{6,15},{9,0},{10,3},{13,4},{14,7},{17,24},{18,... | collective-permute-start | bytes 1585160 | tf_op jit(solution)/shard_map/ppermute | solution.py:410
  74.0 2.4 %shard_map.35 = (bf16[16,128]{1,0:T(8,128)(2,1)S(1)}, f32[1,3,256,1024]{3,2,1,0:T(8,128)}) custom-call(bf16[1024,1024]{1,0:T(8,128)(2,1)S(1)} %bitcast.24, bf16[1552,128]{1,0:T(8,128)(2,1)S(1)} %collective-permute-done.5.refs_2_.refs_1_, bf16[2096,128]{1,0:T(8,128)(2,1)S(1)} %collective-permute-done.3.refs_2_, ...), custom_call_target="tpu_custom_call" | custom-call | flops 6000000000 | bytes 6000000 | tf_op jit(solution)/shard_map/pallas_call | solution.py:380
  76.4 3.7 %collective-permute-done.13.refs_5_ = bf16[2064,128]{1,0:T(8,128)(2,1)S(1)} collective-permute-done((bf16[2064,128]{1,0:T(8,128)(2,1)S(1)}, bf16[2064,128]{1,0:T(8,128)(2,1)S(1)}, u32[]{:S(2)}, u32[]{:S(2)}) %collective-permute-start.13) | collective-permute-done | bytes 528416 | tf_op jit(solution)/shard_map/ppermute | solution.py:410
  80.1 1.5 %shard_map.36 = (f32[256,1024]{1,0:T(8,128)S(1)}, f32[256,1024]{1,0:T(8,128)S(1)}) custom-call(bf16[1024,1024]{1,0:T(8,128)(2,1)S(1)} %bitcast.25, bf16[1024,1024]{1,0:T(8,128)(2,1)S(1)} %collective-permute-done.refs_1_.refs_0_, bf16[1024,768]{1,0:T(8,128)(2,1)S(1)} %collective-permute-done.4.refs_0_.refs_2_, ...), custom_call_target="tpu_custom_call" | custom-call | flops 6000000000 | bytes 6000000 | tf_op jit(solution)/shard_map/pallas_call | solution.py:380
  81.5 8.9 %collective-permute-done.17.refs_3_ = bf16[2064,128]{1,0:T(8,128)(2,1)S(1)} collective-permute-done((bf16[2064,128]{1,0:T(8,128)(2,1)S(1)}, bf16[2064,128]{1,0:T(8,128)(2,1)S(1)}, u32[]{:S(2)}, u32[]{:S(2)}) %collective-permute-start.17) | collective-permute-done | bytes 528416 | tf_op jit(solution)/shard_map/ppermute | solution.py:410
  90.5 1.5 %shard_map.37 = (f32[256,1024]{1,0:T(8,128)S(1)}, f32[1,3,256,1024]{3,2,1,0:T(8,128)}) custom-call(f32[256,1024]{1,0:T(8,128)S(1)} %get-tuple-element.13.refs_0_.refs_5_, f32[256,1024]{1,0:T(8,128)S(1)} %get-tuple-element.14.refs_1_, bf16[3088,128]{1,0:T(8,128)(2,1)S(1)} %collective-permute-done.16.refs_2_, ...), custom_call_target="tpu_custom_call", output_to_operand_aliasing={{1}: (4, {})} | custom-call | flops 6000000000 | bytes 6000000 | tf_op jit(solution)/shard_map/pallas_call | solution.py:380
  92.0 1.1 %shard_map.38 = (bf16[16,128]{1,0:T(8,128)(2,1)}, f32[1,3,256,1024]{3,2,1,0:T(8,128)}) custom-call(f32[256,1024]{1,0:T(8,128)S(1)} %get-tuple-element.16.refs_0_.refs_3_, bf16[1552,128]{1,0:T(8,128)(2,1)S(1)} %collective-permute-done.18.refs_1_, f32[1,3,256,1024]{3,2,1,0:T(8,128)} %get-tuple-element.17.refs_2_, ...), custom_call_target="tpu_custom_call", output_to_operand_aliasing={{1}: (2, {})} | custom-call | flops 6000000000 | bytes 6000000 | tf_op jit(solution)/shard_map/pallas_call | solution.py:380
  (32 shorter events, 5.4 us)
Async XLA Ops:
  0.0 26.2 %collective-permute-start = (bf16[1024,1024]{1,0:T(8,128)(2,1)}, bf16[1024,1024]{1,0:T(8,128)(2,1)S(1)}, u32[]{:S(2)}, u32[]{:S(2)}) collective-permute-start(bf16[1024,1024]{1,0:T(8,128)(2,1)} %bitcast.1), channel_id=1, source_target_pairs={{0,12},{4,0},{8,4},{12,8},{1,13},{5,1},{9,5},{13,9},{2,14},{6,2},{... | collective-permute-start | bytes 6291464 | tf_op jit(solution)/shard_map/ppermute | solution.py:26
  2.4 1.6 %copy-start = (bf16[1,1024,1024]{2,1,0:T(8,128)(2,1)S(1)}, bf16[1,1024,1024]{2,1,0:T(8,128)(2,1)}, u32[]{:S(2)}) copy-start(bf16[1,1024,1024]{2,1,0:T(8,128)(2,1)} %param.1) | copy-start | bytes 6291460
  5.2 14.7 %collective-permute-start.1 = (bf16[2064,128]{1,0:T(8,128)(2,1)S(1)}, bf16[2064,128]{1,0:T(8,128)(2,1)S(1)}, u32[]{:S(2)}, u32[]{:S(2)}) collective-permute-start(bf16[2064,128]{1,0:T(8,128)(2,1)S(1)} %shard_map.17.refs_2_), channel_id=1, source_target_pairs={{0,1},{3,2},{4,5},{7,6},{8,9},{11,10},{12,13},{15,14},{16,17},{19,... | collective-permute-start | bytes 1585160 | tf_op jit(solution)/shard_map/ppermute | solution.py:410
  8.9 22.9 %collective-permute-start.3 = (bf16[2096,128]{1,0:T(8,128)(2,1)S(1)}, bf16[2096,128]{1,0:T(8,128)(2,1)S(1)}, u32[]{:S(2)}, u32[]{:S(2)}) collective-permute-start(bf16[2096,128]{1,0:T(8,128)(2,1)S(1)} %shard_map.18.refs_3_), channel_id=1, source_target_pairs={{0,1},{3,2},{4,5},{7,6},{8,9},{11,10},{12,13},{15,14},{16,17},{19,... | collective-permute-start | bytes 1609736 | tf_op jit(solution)/shard_map/ppermute | solution.py:410
  19.9 31.9 %collective-permute-start.8 = (bf16[2064,128]{1,0:T(8,128)(2,1)S(1)}, bf16[2064,128]{1,0:T(8,128)(2,1)S(1)}, u32[]{:S(2)}, u32[]{:S(2)}) collective-permute-start(bf16[2064,128]{1,0:T(8,128)(2,1)S(1)} %shard_map.19.refs_2_), channel_id=1, source_target_pairs={{1,2},{2,1},{5,6},{6,5},{9,10},{10,9},{13,14},{14,13},{17,18},{18,... | collective-permute-start | bytes 1585160 | tf_op jit(solution)/shard_map/ppermute | solution.py:410
  27.5 4.4 %copy-start.1 = (bf16[1,1024,1024]{2,1,0:T(8,128)(2,1)S(1)}, bf16[1,1024,1024]{2,1,0:T(8,128)(2,1)}, u32[]{:S(2)}) copy-start(bf16[1,1024,1024]{2,1,0:T(8,128)(2,1)} %param.1) | copy-start | bytes 6291460
  27.5 15.7 %collective-permute-start.6 = (bf16[2064,128]{1,0:T(8,128)(2,1)S(1)}, bf16[2064,128]{1,0:T(8,128)(2,1)S(1)}, u32[]{:S(2)}, u32[]{:S(2)}) collective-permute-start(bf16[2064,128]{1,0:T(8,128)(2,1)S(1)} %shard_map.20.refs_1_), channel_id=1, source_target_pairs={{0,1},{3,2},{4,5},{7,6},{8,9},{11,10},{12,13},{15,14},{16,17},{19,... | collective-permute-start | bytes 1585160 | tf_op jit(solution)/shard_map/ppermute | solution.py:410
  30.0 8.6 %collective-permute-start.2 = (bf16[1024,256]{1,0:T(8,128)(2,1)S(1)}, bf16[1024,256]{1,0:T(8,128)(2,1)S(1)}, u32[]{:S(2)}, u32[]{:S(2)}) collective-permute-start(bf16[1024,256]{1,0:T(8,128)(2,1)S(1)} %shard_map.21.refs_3_), channel_id=1, source_target_pairs={{0,12},{4,0},{8,4},{12,8},{1,13},{5,1},{9,5},{13,9},{2,14},{6,2},{... | collective-permute-start | bytes 1572872 | tf_op jit(solution)/shard_map/ppermute | solution.py:26
  31.9 12.0 %collective-permute-start.5 = (bf16[1552,128]{1,0:T(8,128)(2,1)S(1)}, bf16[1552,128]{1,0:T(8,128)(2,1)S(1)}, u32[]{:S(2)}, u32[]{:S(2)}) collective-permute-start(bf16[1552,128]{1,0:T(8,128)(2,1)S(1)} %shard_map.22.refs_2_), channel_id=1, source_target_pairs={{1,2},{2,1},{5,6},{6,5},{9,10},{10,9},{13,14},{14,13},{17,18},{18,... | collective-permute-start | bytes 1191944 | tf_op jit(solution)/shard_map/ppermute | solution.py:410
  39.8 13.7 %collective-permute-start.11 = (bf16[2064,128]{1,0:T(8,128)(2,1)S(1)}, bf16[2064,128]{1,0:T(8,128)(2,1)S(1)}, u32[]{:S(2)}, u32[]{:S(2)}) collective-permute-start(bf16[2064,128]{1,0:T(8,128)(2,1)S(1)} %shard_map.23.refs_1_), channel_id=1, source_target_pairs={{0,1},{3,2},{4,5},{7,6},{8,9},{11,10},{12,13},{15,14},{16,17},{19,... | collective-permute-start | bytes 1585160 | tf_op jit(solution)/shard_map/ppermute | solution.py:410
  41.2 19.9 %collective-permute-start.4 = (bf16[1024,768]{1,0:T(8,128)(2,1)S(1)}, bf16[1024,768]{1,0:T(8,128)(2,1)S(1)}, u32[]{:S(2)}, u32[]{:S(2)}) collective-permute-start(bf16[1024,768]{1,0:T(8,128)(2,1)S(1)} %shard_map.24.refs_3_), channel_id=1, source_target_pairs={{0,12},{4,0},{8,4},{12,8},{1,13},{5,1},{9,5},{13,9},{2,14},{6,2},{... | collective-permute-start | bytes 4718600 | tf_op jit(solution)/shard_map/ppermute | solution.py:26
  43.2 20.2 %collective-permute-start.10 = (bf16[2064,128]{1,0:T(8,128)(2,1)S(1)}, bf16[2064,128]{1,0:T(8,128)(2,1)S(1)}, u32[]{:S(2)}, u32[]{:S(2)}) collective-permute-start(bf16[2064,128]{1,0:T(8,128)(2,1)S(1)} %shard_map.25.refs_3_), channel_id=1, source_target_pairs={{1,2},{2,1},{5,6},{6,5},{9,10},{10,9},{13,14},{14,13},{17,18},{18,... | collective-permute-start | bytes 1585160 | tf_op jit(solution)/shard_map/ppermute | solution.py:410
  45.1 25.5 %collective-permute-start.7 = (bf16[2064,128]{1,0:T(8,128)(2,1)S(1)}, bf16[2064,128]{1,0:T(8,128)(2,1)S(1)}, u32[]{:S(2)}, u32[]{:S(2)}) collective-permute-start(bf16[2064,128]{1,0:T(8,128)(2,1)S(1)} %shard_map.26.refs_3_), channel_id=1, source_target_pairs={{0,1},{3,2},{4,5},{7,6},{8,9},{11,10},{12,13},{15,14},{16,17},{19,... | collective-permute-start | bytes 1585160 | tf_op jit(solution)/shard_map/ppermute | solution.py:410
  52.1 15.5 %collective-permute-start.9 = (bf16[2064,128]{1,0:T(8,128)(2,1)S(1)}, bf16[2064,128]{1,0:T(8,128)(2,1)S(1)}, u32[]{:S(2)}, u32[]{:S(2)}) collective-permute-start(bf16[2064,128]{1,0:T(8,128)(2,1)S(1)} %shard_map.27.refs_3_), channel_id=1, source_target_pairs={{1,0},{2,3},{5,4},{6,7},{9,8},{10,11},{13,12},{14,15},{17,16},{18,... | collective-permute-start | bytes 1585160 | tf_op jit(solution)/shard_map/ppermute | solution.py:410
  53.5 17.8 %collective-permute-start.15 = (bf16[2064,128]{1,0:T(8,128)(2,1)S(1)}, bf16[2064,128]{1,0:T(8,128)(2,1)S(1)}, u32[]{:S(2)}, u32[]{:S(2)}) collective-permute-start(bf16[2064,128]{1,0:T(8,128)(2,1)S(1)} %shard_map.28.refs_2_), channel_id=1, source_target_pairs={{1,2},{2,1},{5,6},{6,5},{9,10},{10,9},{13,14},{14,13},{17,18},{18,... | collective-permute-start | bytes 1585160 | tf_op jit(solution)/shard_map/ppermute | solution.py:410
  62.1 11.3 %collective-permute-start.14 = (bf16[1552,128]{1,0:T(8,128)(2,1)S(1)}, bf16[1552,128]{1,0:T(8,128)(2,1)S(1)}, u32[]{:S(2)}, u32[]{:S(2)}) collective-permute-start(bf16[1552,128]{1,0:T(8,128)(2,1)S(1)} %shard_map.29.refs_3_), channel_id=1, source_target_pairs={{0,1},{3,2},{4,5},{7,6},{8,9},{11,10},{12,13},{15,14},{16,17},{19,... | collective-permute-start | bytes 1191944 | tf_op jit(solution)/shard_map/ppermute | solution.py:410
  63.5 16.6 %collective-permute-start.13 = (bf16[2064,128]{1,0:T(8,128)(2,1)S(1)}, bf16[2064,128]{1,0:T(8,128)(2,1)S(1)}, u32[]{:S(2)}, u32[]{:S(2)}) collective-permute-start(bf16[2064,128]{1,0:T(8,128)(2,1)S(1)} %shard_map.30.refs_4_), channel_id=1, source_target_pairs={{1,0},{2,3},{5,4},{6,7},{9,8},{10,11},{13,12},{14,15},{17,16},{18,... | collective-permute-start | bytes 1585160 | tf_op jit(solution)/shard_map/ppermute | solution.py:410
  69.2 21.3 %collective-permute-start.16 = (bf16[3088,128]{1,0:T(8,128)(2,1)S(1)}, bf16[3088,128]{1,0:T(8,128)(2,1)S(1)}, u32[]{:S(2)}, u32[]{:S(2)}) collective-permute-start(bf16[3088,128]{1,0:T(8,128)(2,1)S(1)} %shard_map.31.refs_3_), channel_id=1, source_target_pairs={{0,1},{3,2},{4,5},{7,6},{8,9},{11,10},{12,13},{15,14},{16,17},{19,... | collective-permute-start | bytes 2371592 | tf_op jit(solution)/shard_map/ppermute | solution.py:410
  70.6 5.8 %collective-permute-start.12 = (bf16[2064,128]{1,0:T(8,128)(2,1)S(1)}, bf16[2064,128]{1,0:T(8,128)(2,1)S(1)}, u32[]{:S(2)}, u32[]{:S(2)}) collective-permute-start(bf16[2064,128]{1,0:T(8,128)(2,1)S(1)} %shard_map.32.refs_3_), channel_id=1, source_target_pairs={{1,2},{2,1},{5,6},{6,5},{9,10},{10,9},{13,14},{14,13},{17,18},{18,... | collective-permute-start | bytes 1585160 | tf_op jit(solution)/shard_map/ppermute | solution.py:410
  71.3 19.1 %collective-permute-start.17 = (bf16[2064,128]{1,0:T(8,128)(2,1)S(1)}, bf16[2064,128]{1,0:T(8,128)(2,1)S(1)}, u32[]{:S(2)}, u32[]{:S(2)}) collective-permute-start(bf16[2064,128]{1,0:T(8,128)(2,1)S(1)} %shard_map.33.refs_3_), channel_id=1, source_target_pairs={{1,8},{2,11},{5,12},{6,15},{9,0},{10,3},{13,4},{14,7},{17,24},{18,... | collective-permute-start | bytes 1585160 | tf_op jit(solution)/shard_map/ppermute | solution.py:410
  73.3 18.7 %collective-permute-start.18 = (bf16[1552,128]{1,0:T(8,128)(2,1)S(1)}, bf16[1552,128]{1,0:T(8,128)(2,1)S(1)}, u32[]{:S(2)}, u32[]{:S(2)}) collective-permute-start(bf16[1552,128]{1,0:T(8,128)(2,1)S(1)} %shard_map.34.refs_6_), channel_id=1, source_target_pairs={{1,10},{2,9},{5,14},{6,13},{9,2},{10,1},{13,6},{14,5},{17,26},{18,... | collective-permute-start | bytes 1191944 | tf_op jit(solution)/shard_map/ppermute | solution.py:410
